TPU v7x, 32 devices: a whole 2x2x4 slice. The times are simulated.
32 devices in a mesh: seq: 1, res: 32 (over z, y, x, core).
Axes of the slice: x: 2, y: 2, z: 4, core: 2. Of those that a mesh axis runs over, the one named last changes fastest.
Arguments:
- extra_activations: bfloat16 [32, 65536], P('seq', 'res'), may hold values from -6 to 6
- twofold_representation: bfloat16 [1024, 1024, 128], P('res', 'seq'), may hold values from -6 to 6
- present_indicator: int32 [32, 1024], P('seq', 'res'), may hold values 0 or 1
- amino_presence: int32 [1024], P('res'), may hold values 0 or 1
- twofold_offset_matrix: bfloat16 [128, 8], replicated, may hold values from -1.5859375 to 1.5859375
- horizontal_matrix: bfloat16 [64, 256], replicated, may hold values from -8 to 8, as said below
- horizontal_exit_matrix: bfloat16 [64, 64], replicated, may hold values from -1.5 to 1.5
- vertical_matrix: bfloat16 [64, 144], replicated, may hold values from -8 to 8, as said below
- vertical_exit_matrix: bfloat16 [64, 64], replicated, may hold values from -0.75 to 0.75
Outputs:
- msa_out: bfloat16 [32, 65536], P('seq', 'res')
Inputs may be any that keep to these rules, and one draw needn't show every extreme that they name: `horizontal_matrix`: a projection matrix. `vertical_matrix`: a projection matrix.
All inputs are finite; a program needn't handle non-finite values. No bound on the sum of `present_indicator` or of `amino_presence` on one device may be relied on, other than what follows from the above.
Results may differ from a plain program's by a relative error of at most 0.02.
The roundings to bfloat16 on the way count: a program that leaves them out, or rounds other values in their place, can miss the bound.
Values may be sent and summed in bfloat16 or wider, within the bound.
No kernel may reach another device: no remote copies, remote signals or barrier semaphores. Data moves between devices by JAX's collectives and lax.ppermute only.
A program may use at most 64 MiB of HBM per device.

v0:
```python
import jax
import jax.numpy as jnp
from jax import lax
from jax.sharding import PartitionSpec as P


def layer_normalize(values_in):
    centre = values_in - jnp.mean(values_in, axis=-1, keepdims=True)
    spread = jnp.mean(centre * centre, axis=-1, keepdims=True)
    return centre * lax.rsqrt(spread + 1e-05)


def complete_column(homolog_line, column_gate, attended_output, vertical_exit_matrix):
    sequence_count, column_count, feature_size = homolog_line.shape
    head_number, head_channel_width = (attended_output.shape[1], attended_output.shape[2])
    hidden_size = head_number * head_channel_width
    gated = (
        jax.nn.sigmoid(column_gate).reshape(
            sequence_count, column_count, head_number, head_channel_width
        )
        * attended_output[None]
    )
    gated = gated.reshape(sequence_count * column_count, hidden_size).astype(jnp.bfloat16)
    horizontal_update = jnp.dot(
        gated, vertical_exit_matrix, preferred_element_type=jnp.float32
    ).reshape(sequence_count, column_count, feature_size)
    return (homolog_line.astype(jnp.float32) + horizontal_update).astype(jnp.bfloat16)


def column_pieces(homolog_line, vertical_matrix, head_number, head_channel_width):
    sequence_count, column_count, feature_size = homolog_line.shape
    hidden_size = head_number * head_channel_width
    column_normalized = layer_normalize(homolog_line.astype(jnp.float32)).astype(jnp.bfloat16)
    mapped_linear = jnp.dot(
        column_normalized.reshape(-1, feature_size),
        vertical_matrix,
        preferred_element_type=jnp.float32,
    )
    mapped_linear = mapped_linear.reshape(sequence_count, column_count, -1)
    return (
        mapped_linear[..., :hidden_size],
        mapped_linear[..., hidden_size : 2 * hidden_size],
        mapped_linear[..., 2 * hidden_size : 2 * hidden_size + head_channel_width],
        mapped_linear[..., 2 * hidden_size + head_channel_width :],
    )


def column_logits(kept_entries, mean_query, column_key, head_number, head_channel_width):
    column_count = mean_query.shape[0]
    logits = jnp.einsum(
        "ihc,sic->sih",
        mean_query.reshape(column_count, head_number, head_channel_width),
        column_key,
    )
    return logits + 1000000000.0 * (kept_entries - 1.0)[..., None]


def column_complete(
    homolog_line,
    kept_entries,
    vertical_matrix,
    vertical_exit_matrix,
    head_number,
    head_channel_width,
):
    column_query, column_gate, column_key, column_value = column_pieces(
        homolog_line, vertical_matrix, head_number, head_channel_width
    )
    query_total = jnp.sum(kept_entries[..., None] * column_query, axis=0)
    kept_count = jnp.sum(kept_entries, axis=0)
    mean_query = query_total / jnp.maximum(kept_count, 1.0)[:, None] * head_channel_width ** (-0.5)
    logits = column_logits(kept_entries, mean_query, column_key, head_number, head_channel_width)
    exped = jnp.exp(logits - jnp.max(logits, axis=0, keepdims=True))
    attended_output = (
        jnp.einsum("sih,sic->ihc", exped, column_value) / jnp.sum(exped, axis=0)[..., None]
    )
    return complete_column(homolog_line, column_gate, attended_output, vertical_exit_matrix)


def on_device(
    extra_activations,
    twofold_representation,
    present_indicator,
    amino_presence,
    twofold_offset_matrix,
    horizontal_matrix,
    horizontal_exit_matrix,
    vertical_matrix,
    vertical_exit_matrix,
):
    homolog_lines, amino_lines = present_indicator.shape
    feature_size = horizontal_matrix.shape[0]
    hidden_size = horizontal_exit_matrix.shape[0]
    head_number = twofold_offset_matrix.shape[1]
    head_channel_width = hidden_size // head_number
    local_lines = extra_activations.reshape(homolog_lines, amino_lines, feature_size)
    kept_entries = (present_indicator * amino_presence[None, :]).astype(jnp.float32)
    standardised = layer_normalize(local_lines.astype(jnp.float32)).astype(jnp.bfloat16)
    mapped_linear = jnp.dot(
        standardised.reshape(-1, feature_size),
        horizontal_matrix,
        preferred_element_type=jnp.float32,
    )
    mapped_linear = mapped_linear.reshape(homolog_lines, amino_lines, 4 * hidden_size)
    queries = (mapped_linear[..., :hidden_size] * head_channel_width ** (-0.5)).astype(jnp.bfloat16)
    query_heads = queries.reshape(homolog_lines, amino_lines, head_number, head_channel_width)
    gating = mapped_linear[..., 3 * hidden_size :]
    pair_normed = layer_normalize(twofold_representation.astype(jnp.float32)).astype(jnp.bfloat16)
    bias_local = jnp.einsum(
        "ikc,ch->hik", pair_normed, twofold_offset_matrix, preferred_element_type=jnp.float32
    )
    bias_panel = lax.all_gather(bias_local.astype(jnp.bfloat16), "seq", axis=2, tiled=True)
    mask_wire = kept_entries.astype(jnp.bfloat16)

    def attend_block(running, key_block, value_block, mask_block, key_start):
        block_size = key_block.shape[1]
        key_heads = key_block.reshape(homolog_lines, block_size, head_number, head_channel_width)
        value_heads = value_block.reshape(
            homolog_lines, block_size, head_number, head_channel_width
        )
        logits = jnp.einsum(
            "sihc,sjhc->hsij", query_heads, key_heads, preferred_element_type=jnp.float32
        )
        bias_block = lax.dynamic_slice_in_dim(bias_panel, key_start, block_size, 2).astype(
            jnp.float32
        )
        logits = (
            logits
            + bias_block[:, None]
            + (1000000000.0 * (mask_block.astype(jnp.float32) - 1.0))[None, :, None, :]
        )
        peak = jnp.maximum(running[0], jnp.max(logits, axis=-1))
        rescale = jnp.exp(running[0] - peak)
        exped = jnp.exp(logits - peak[..., None])
        total = running[1] * rescale + jnp.sum(exped, axis=-1)
        summed = jnp.einsum(
            "hsij,sjhc->hsic",
            exped.astype(jnp.bfloat16),
            value_heads,
            preferred_element_type=jnp.float32,
        )
        return (peak, total, running[2] * rescale[..., None] + summed)

    def attend_piece(running, key_piece, value_piece, mask_piece):
        key_count = key_piece.shape[1]
        block_size = 128

        def one_block(block_index, state):
            offset_rows = block_index * block_size
            return attend_block(
                state,
                lax.dynamic_slice_in_dim(key_piece, offset_rows, block_size, 1),
                lax.dynamic_slice_in_dim(value_piece, offset_rows, block_size, 1),
                lax.dynamic_slice_in_dim(mask_piece, offset_rows, block_size, 1),
                offset_rows,
            )

        return lax.fori_loop(0, key_count // block_size, one_block, running)

    initial = (
        jnp.full((head_number, homolog_lines, amino_lines), -jnp.inf, jnp.float32),
        jnp.zeros((head_number, homolog_lines, amino_lines), jnp.float32),
        jnp.zeros((head_number, homolog_lines, amino_lines, head_channel_width), jnp.float32),
    )
    key_local = mapped_linear[..., hidden_size : 2 * hidden_size].astype(jnp.bfloat16)
    value_local = mapped_linear[..., 2 * hidden_size : 3 * hidden_size].astype(jnp.bfloat16)
    key_piece = (
        lax.all_gather(key_local, "res", axis=1, tiled=True),
        lax.all_gather(value_local, "res", axis=1, tiled=True),
        lax.all_gather(mask_wire, "res", axis=1, tiled=True),
    )
    answer_tuple = attend_piece(initial, key_piece[0], key_piece[1], key_piece[2])
    attended_output = answer_tuple[2] / answer_tuple[1][..., None]
    attended_output = jnp.transpose(attended_output, (1, 2, 0, 3)).reshape(
        homolog_lines, amino_lines, hidden_size
    )
    row_gated = (jax.nn.sigmoid(gating) * attended_output).astype(jnp.bfloat16)
    horizontal_update = jnp.dot(
        row_gated.reshape(-1, hidden_size),
        horizontal_exit_matrix,
        preferred_element_type=jnp.float32,
    )
    homolog_line = (
        local_lines.astype(jnp.float32)
        + horizontal_update.reshape(homolog_lines, amino_lines, feature_size)
    ).astype(jnp.bfloat16)
    moved_rows, moved_mask = (
        lax.all_to_all(homolog_line, "seq", split_axis=1, concat_axis=0, tiled=True),
        lax.all_to_all(mask_wire, "seq", split_axis=1, concat_axis=0, tiled=True),
    )
    updated = column_complete(
        moved_rows,
        moved_mask.astype(jnp.float32),
        vertical_matrix,
        vertical_exit_matrix,
        head_number,
        head_channel_width,
    )
    ultimate_update = lax.all_to_all(updated, "seq", split_axis=0, concat_axis=1, tiled=True)
    return ultimate_update.reshape(homolog_lines, amino_lines * feature_size)


def solution(mesh):
    in_specs = (
        P("seq", "res"),
        P("res", "seq", None),
        P("seq", "res"),
        P("res"),
        P(),
        P(),
        P(),
        P(),
        P(),
    )
    out_specs = P("seq", "res")
    return jax.shard_map(
        on_device, mesh=mesh, in_specs=in_specs, out_specs=out_specs, check_vma=False
    )
```

profile of v0, /device:TPU:0, one launch (start us, length us, event | category | flops | bytes accessed | tf_op | source)
XLA Modules:
  0.0 289.6 jit_solution(6360556684521847174)
XLA Ops:
  13.4 44.6 %all_gather.11 = bf16[32,1024]{0,1:T(8,128)(2,1)S(1)} all-gather(bf16[32,32]{0,1:T(8,128)(2,1)S(1)} %get-tuple-element.306), channel_id=1, replica_groups=mesh['seq'=1,'res'=32] {'res'}, dimensions={1}, use_global_device_ids=true | all-gather | bytes 67584 | tf_op jit(solution)/shard_map/all_gather | solution.py:170
  58.2 5.6 %convert_reduce_fusion = f32[32,1024]{1,0:T(8,128)S(1)} fusion(bf16[32,1024,128]{2,1,0:T(8,128)(2,1)} %param.12), kind=kLoop, calls=%fused_computation.25 | loop fusion | flops 8355840 | bytes 8519680 | tf_op jit(solution)/shard_map/reduce_sum | solution.py:8
  63.9 11.0 %fusion.18 = f32[32,1024]{1,0:T(8,128)S(1)} fusion(bf16[32,1024,128]{2,1,0:T(8,128)(2,1)} %param.12, f32[32,1024]{1,0:T(8,128)S(1)} %broadcast_multiply_fusion), kind=kLoop, calls=%fused_computation.28 | loop fusion | flops 16744448 | bytes 8650752 | tf_op jit(solution)/shard_map/reduce_sum | solution.py:9
  75.0 12.1 %fusion.27 = bf16[8,32,1024]{2,0,1:T(8,128)(2,1)} fusion(bf16[32,1024,128]{2,1,0:T(8,128)(2,1)} %param.12, f32[32,1024]{1,0:T(8,128)S(1)} %add_rsqrt_fusion, f32[32,1024]{1,0:T(8,128)S(1)} %broadcast_multiply_fusion, bf16[128,8]{0,1:T(8,128)(2,1)S(1)} %copy-done.8), kind=kOutput, calls=%fused_computation.36 | convolution fusion | flops 84148224 | bytes 9177088 | tf_op jit(solution)/shard_map/ikc,ch->hik/dot_general | solution.py:109
  87.1 10.3 %all-gather.3.cloned.1.call-done = bf16[32,1024,64]{2,1,0:T(8,128)(2,1)} async-done(((bf16[32,32,64]{2,1,0:T(8,128)(2,1)}), bf16[32,1024,64]{2,1,0:T(8,128)(2,1)}) %all-gather.3.cloned.1.call-update) | async-done | bytes 4194320 | tf_op jit(solution)/shard_map/all_gather | solution.py:168
  97.4 8.6 %copy.35 = bf16[32,1024,64]{1,2,0:T(8,128)(2,1)} copy(bf16[32,1024,64]{2,1,0:T(8,128)(2,1)} %all-gather.3.cloned.1.call-done) | data formatting | bytes 8388608
  106.0 77.1 %all-gather.5.cloned.1.call-done = bf16[32,1024,64]{2,1,0:T(8,128)(2,1)} async-done(((bf16[32,32,64]{2,1,0:T(8,128)(2,1)}), bf16[32,1024,64]{2,1,0:T(8,128)(2,1)}) %all-gather.5.cloned.1.call-update) | async-done | bytes 4194320 | tf_op jit(solution)/shard_map/all_gather | solution.py:169
  183.0 8.5 %copy.39 = bf16[32,1024,64]{1,2,0:T(8,128)(2,1)} copy(bf16[32,1024,64]{2,1,0:T(8,128)(2,1)} %all-gather.5.cloned.1.call-done) | data formatting | bytes 8388608
  191.6 85.4 %while.20 = (s32[]{:T(128)}, f32[8,32,32]{2,1,0:T(8,128)S(1)}, f32[8,32,32]{2,1,0:T(8,128)S(1)}, f32[8,32,32,8]{2,3,1,0:T(8,128)S(1)}, bf16[32,1024,64]{1,2,0:T(...) while((s32[]{:T(128)}, f32[8,32,32]{2,1,0:T(8,128)S(1)}, ...), condition=%wide.region_7.0_spmd.clone, body=%wide.region_4.0_spmd.clone.sunk | while | flops 45371396 | bytes 34480348 | solution.py:158
  193.8 2.7 fusion.86
  196.5 4.3 %fusion.87 = f32[8,32,32]{2,1,0:T(8,128)S(1)} fusion(f32[8,32,128,32]{2,3,1,0:T(8,128)} %get-tuple-element.384, f32[8,32,32]{2,1,0:T(8,128)S(1)} %select_maximum_fusion.2, f32[32,128]{1,0:T(8,128)S(1)} %add_multiply_fusion.3, f32[8,32,128]{2,1,0:T(8,128)S(1)} %copy_convert_fusion.2), kind=kLoop, calls=%fused_computation.4.clone.1 | loop fusion | flops 4186112 | bytes 4407296 | tf_op jit(solution)/shard_map/while/body/eval_jaxpr/reduce_sum | solution.py:135
  200.9 1.3 fusion.89
  204.4 2.7 fusion.86
  207.2 4.3 %fusion.87 = f32[8,32,32]{2,1,0:T(8,128)S(1)} fusion(f32[8,32,128,32]{2,3,1,0:T(8,128)} %get-tuple-element.384, f32[8,32,32]{2,1,0:T(8,128)S(1)} %select_maximum_fusion.2, f32[32,128]{1,0:T(8,128)S(1)} %add_multiply_fusion.3, f32[8,32,128]{2,1,0:T(8,128)S(1)} %copy_convert_fusion.2), kind=kLoop, calls=%fused_computation.4.clone.1 | loop fusion | flops 4186112 | bytes 4407296 | tf_op jit(solution)/shard_map/while/body/eval_jaxpr/reduce_sum | solution.py:135
  211.6 1.3 fusion.89
  215.1 2.7 fusion.86
  217.9 4.3 %fusion.87 = f32[8,32,32]{2,1,0:T(8,128)S(1)} fusion(f32[8,32,128,32]{2,3,1,0:T(8,128)} %get-tuple-element.384, f32[8,32,32]{2,1,0:T(8,128)S(1)} %select_maximum_fusion.2, f32[32,128]{1,0:T(8,128)S(1)} %add_multiply_fusion.3, f32[8,32,128]{2,1,0:T(8,128)S(1)} %copy_convert_fusion.2), kind=kLoop, calls=%fused_computation.4.clone.1 | loop fusion | flops 4186112 | bytes 4407296 | tf_op jit(solution)/shard_map/while/body/eval_jaxpr/reduce_sum | solution.py:135
  225.8 2.7 fusion.86
  228.6 4.3 %fusion.87 = f32[8,32,32]{2,1,0:T(8,128)S(1)} fusion(f32[8,32,128,32]{2,3,1,0:T(8,128)} %get-tuple-element.384, f32[8,32,32]{2,1,0:T(8,128)S(1)} %select_maximum_fusion.2, f32[32,128]{1,0:T(8,128)S(1)} %add_multiply_fusion.3, f32[8,32,128]{2,1,0:T(8,128)S(1)} %copy_convert_fusion.2), kind=kLoop, calls=%fused_computation.4.clone.1 | loop fusion | flops 4186112 | bytes 4407296 | tf_op jit(solution)/shard_map/while/body/eval_jaxpr/reduce_sum | solution.py:135
  232.9 1.3 fusion.89
  236.5 2.7 fusion.86
  239.3 4.3 %fusion.87 = f32[8,32,32]{2,1,0:T(8,128)S(1)} fusion(f32[8,32,128,32]{2,3,1,0:T(8,128)} %get-tuple-element.384, f32[8,32,32]{2,1,0:T(8,128)S(1)} %select_maximum_fusion.2, f32[32,128]{1,0:T(8,128)S(1)} %add_multiply_fusion.3, f32[8,32,128]{2,1,0:T(8,128)S(1)} %copy_convert_fusion.2), kind=kLoop, calls=%fused_computation.4.clone.1 | loop fusion | flops 4186112 | bytes 4407296 | tf_op jit(solution)/shard_map/while/body/eval_jaxpr/reduce_sum | solution.py:135
  243.6 1.3 fusion.89
  247.2 2.7 fusion.86
  249.9 4.3 %fusion.87 = f32[8,32,32]{2,1,0:T(8,128)S(1)} fusion(f32[8,32,128,32]{2,3,1,0:T(8,128)} %get-tuple-element.384, f32[8,32,32]{2,1,0:T(8,128)S(1)} %select_maximum_fusion.2, f32[32,128]{1,0:T(8,128)S(1)} %add_multiply_fusion.3, f32[8,32,128]{2,1,0:T(8,128)S(1)} %copy_convert_fusion.2), kind=kLoop, calls=%fused_computation.4.clone.1 | loop fusion | flops 4186112 | bytes 4407296 | tf_op jit(solution)/shard_map/while/body/eval_jaxpr/reduce_sum | solution.py:135
  257.8 2.7 fusion.86
  260.6 4.3 %fusion.87 = f32[8,32,32]{2,1,0:T(8,128)S(1)} fusion(f32[8,32,128,32]{2,3,1,0:T(8,128)} %get-tuple-element.384, f32[8,32,32]{2,1,0:T(8,128)S(1)} %select_maximum_fusion.2, f32[32,128]{1,0:T(8,128)S(1)} %add_multiply_fusion.3, f32[8,32,128]{2,1,0:T(8,128)S(1)} %copy_convert_fusion.2), kind=kLoop, calls=%fused_computation.4.clone.1 | loop fusion | flops 4186112 | bytes 4407296 | tf_op jit(solution)/shard_map/while/body/eval_jaxpr/reduce_sum | solution.py:135
  265.0 1.3 fusion.89
  268.5 2.7 fusion.86
  271.3 4.3 %fusion.87 = f32[8,32,32]{2,1,0:T(8,128)S(1)} fusion(f32[8,32,128,32]{2,3,1,0:T(8,128)} %get-tuple-element.384, f32[8,32,32]{2,1,0:T(8,128)S(1)} %select_maximum_fusion.2, f32[32,128]{1,0:T(8,128)S(1)} %add_multiply_fusion.3, f32[8,32,128]{2,1,0:T(8,128)S(1)} %copy_convert_fusion.2), kind=kLoop, calls=%fused_computation.4.clone.1 | loop fusion | flops 4186112 | bytes 4407296 | tf_op jit(solution)/shard_map/while/body/eval_jaxpr/reduce_sum | solution.py:135
  275.7 1.3 fusion.89
  277.5 1.5 fusion.72
  (133 shorter events, 32.1 us)
Async XLA Ops:
  6.5 1.8 copy-start
  6.5 6.6 %copy-start.4 = (s32[32,32]{1,0:T(8,128)S(1)}, s32[32,32]{1,0:T(8,128)}, u32[]{:S(2)}) copy-start(s32[32,32]{1,0:T(8,128)} %param.13) | copy-start | bytes 12292
  6.5 6.7 %copy-start.5 = (s32[32]{0:T(128)S(1)}, s32[32]{0:T(128)}, u32[]{:S(2)}) copy-start(s32[32]{0:T(128)} %param.14) | copy-start | bytes 388
  6.5 90.9 %all-gather.3.cloned.1.call-start = ((), (), s32[]{:S(2)}) async-start(), calls=%async_computation | async-start | bytes 8650752 | tf_op jit(solution)/shard_map/all_gather | solution.py:168
  9.0 2.9 %copy-start.2 = (f32[32,32,256]{2,1,0:T(8,128)}, f32[32,32,256]{2,1,0:T(8,128)S(1)}, u32[]{:S(2)}) copy-start(f32[32,32,256]{2,1,0:T(8,128)S(1)} %get-tuple-element.316) | copy-start | bytes 3145732
  10.1 172.9 %all-gather.5.cloned.1.call-start = ((), (), s32[]{:S(2)}) async-start(), calls=%async_computation.1 | async-start | bytes 8650752 | tf_op jit(solution)/shard_map/all_gather | solution.py:169
  63.9 11.1 %copy-start.8 = (bf16[128,8]{0,1:T(8,128)(2,1)S(1)}, bf16[128,8]{0,1:T(8,128)(2,1)}, u32[]{:S(2)}) copy-start(bf16[128,8]{0,1:T(8,128)(2,1)} %param.15) | copy-start | bytes 6148
  191.6 85.9 %copy-start.6 = (bf16[64,64]{1,0:T(8,128)(2,1)S(1)}, bf16[64,64]{1,0:T(8,128)(2,1)}, u32[]{:S(2)}) copy-start(bf16[64,64]{1,0:T(8,128)(2,1)} %param.17) | copy-start | bytes 24580
  196.5 4.4 %copy-start.1 = (f32[8,32,128,32]{2,3,1,0:T(8,128)S(1)}, f32[8,32,128,32]{2,3,1,0:T(8,128)}, u32[]{:S(2)}) copy-start(f32[8,32,128,32]{2,3,1,0:T(8,128)} %get-tuple-element.384) | copy-start | bytes 12582916 | tf_op jit(solution)/shard_map/while
  207.2 4.4 %copy-start.1 = (f32[8,32,128,32]{2,3,1,0:T(8,128)S(1)}, f32[8,32,128,32]{2,3,1,0:T(8,128)}, u32[]{:S(2)}) copy-start(f32[8,32,128,32]{2,3,1,0:T(8,128)} %get-tuple-element.384) | copy-start | bytes 12582916 | tf_op jit(solution)/shard_map/while
  217.9 4.4 %copy-start.1 = (f32[8,32,128,32]{2,3,1,0:T(8,128)S(1)}, f32[8,32,128,32]{2,3,1,0:T(8,128)}, u32[]{:S(2)}) copy-start(f32[8,32,128,32]{2,3,1,0:T(8,128)} %get-tuple-element.384) | copy-start | bytes 12582916 | tf_op jit(solution)/shard_map/while
  228.5 4.4 %copy-start.1 = (f32[8,32,128,32]{2,3,1,0:T(8,128)S(1)}, f32[8,32,128,32]{2,3,1,0:T(8,128)}, u32[]{:S(2)}) copy-start(f32[8,32,128,32]{2,3,1,0:T(8,128)} %get-tuple-element.384) | copy-start | bytes 12582916 | tf_op jit(solution)/shard_map/while
  239.2 4.4 %copy-start.1 = (f32[8,32,128,32]{2,3,1,0:T(8,128)S(1)}, f32[8,32,128,32]{2,3,1,0:T(8,128)}, u32[]{:S(2)}) copy-start(f32[8,32,128,32]{2,3,1,0:T(8,128)} %get-tuple-element.384) | copy-start | bytes 12582916 | tf_op jit(solution)/shard_map/while
  249.9 4.4 %copy-start.1 = (f32[8,32,128,32]{2,3,1,0:T(8,128)S(1)}, f32[8,32,128,32]{2,3,1,0:T(8,128)}, u32[]{:S(2)}) copy-start(f32[8,32,128,32]{2,3,1,0:T(8,128)} %get-tuple-element.384) | copy-start | bytes 12582916 | tf_op jit(solution)/shard_map/while
  260.6 4.4 %copy-start.1 = (f32[8,32,128,32]{2,3,1,0:T(8,128)S(1)}, f32[8,32,128,32]{2,3,1,0:T(8,128)}, u32[]{:S(2)}) copy-start(f32[8,32,128,32]{2,3,1,0:T(8,128)} %get-tuple-element.384) | copy-start | bytes 12582916 | tf_op jit(solution)/shard_map/while
  271.3 4.4 %copy-start.1 = (f32[8,32,128,32]{2,3,1,0:T(8,128)S(1)}, f32[8,32,128,32]{2,3,1,0:T(8,128)}, u32[]{:S(2)}) copy-start(f32[8,32,128,32]{2,3,1,0:T(8,128)} %get-tuple-element.384) | copy-start | bytes 12582916 | tf_op jit(solution)/shard_map/while
  277.0 2.4 copy-start.3
  277.5 3.9 %copy-start.7 = (bf16[64,64]{1,0:T(8,128)(2,1)S(1)}, bf16[64,64]{1,0:T(8,128)(2,1)}, u32[]{:S(2)}) copy-start(bf16[64,64]{1,0:T(8,128)(2,1)} %param.19) | copy-start | bytes 24580
Sparse Core Ops, SparseCore 0:
  10.2 87.1 all-gather.2
  100.3 82.6 all-gather.4
where the time goes:
time: 291 us; the launch traced here: 290 us
  waiting for transfers between devices  88.1 us (30%)
  other arithmetic  53.7 us (18%)
  matrix products  48.2 us (17%)
  blocking collectives  44.6 us (15%)
  local copies, waits for them, and re-layouts  40.8 us (14%)
  between operations  13.7 us (5%)
    all_gather x1, waiting for transfers between devices, on_device(): lax.all_gather(value_local, 'res', axis=1, tiled=True)  77.1 us
    all_gather x1, blocking collectives, on_device(): lax.all_gather(mask_wire, 'res', axis=1, tiled=True)  44.6 us
    reduce_sum x8, other arithmetic, attend_block(): total = running[1] * rescale + jnp.sum(exped, axis=-1)  34.1 us
    dot_general x8, matrix products, attend_block(): jnp.einsum('sihc,sjhc->hsij', query_heads, key_heads, preferred_element_t...  21.9 us
    unnamed x21, local copies, waits for them, and re-layouts  18.5 us
    dot_general x1, matrix products, on_device(): jnp.einsum('ikc,ch->hik', pair_normed, twofold_offset_matrix, preferred_e...  12.1 us
    reduce_sum x3, other arithmetic, layer_normalize(): spread = jnp.mean(centre * centre, axis=-1, keepdims=True)  11.8 us
    dot_general x8, matrix products, attend_block(): jnp.einsum('hsij,sjhc->hsic', exped.astype(jnp.bfloat16), value_heads, pr...  10.5 us
  transfers between devices with their start and end apart: 2, of which 2 were waited for; matrix products, arithmetic and copies ran while one was open for 14% of the time, Pallas kernels for 0%

commit v1 on v0

v1 whole, which is shorter than its diff:
```python
import functools
import math

import jax
import jax.numpy as jnp
from jax import lax
from jax.experimental import pallas as pl
from jax.experimental.pallas import tpu as pltpu
from jax.sharding import PartitionSpec as P

F32 = jnp.float32
BF16 = jnp.bfloat16
LOG2E = math.log2(math.e)
EPS = 1e-05
VMEM_LIMIT = 56 * 1024 * 1024

NT = (((1,), (1,)), ((), ()))


def mm(a, b):
    return jnp.dot(a, b, preferred_element_type=F32)


def mm_nt(a, b):
    return lax.dot_general(a, b, NT, preferred_element_type=F32)


def iota(shape, axis):
    return lax.broadcasted_iota(jnp.int32, shape, axis)


def one_hot(condition):
    return jnp.where(condition, 1.0, 0.0).astype(BF16)


def block_matrix(size, block, on_diagonal, elsewhere):
    row, col = iota((size, size), 0), iota((size, size), 1)
    inside = jnp.where(row == col, on_diagonal, elsewhere)
    return jnp.where(row // block == col // block, inside, 0.0).astype(BF16)


def halves(value):
    high = value.astype(BF16)
    return high, (value - high.astype(F32)).astype(BF16)


def mm_split(value, matrix):
    high, low = halves(value)
    return mm(high, matrix) + mm(low, matrix)


def paired_norm(x, width):
    lanes = x.shape[1]
    centre = mm(x, block_matrix(lanes, width, 1.0 - 1.0 / width, -1.0 / width))
    spread = mm_split(centre * centre, block_matrix(lanes, width, 1.0 / width, 1.0 / width))
    return (centre * lax.rsqrt(spread + EPS)).astype(BF16)


def row_shuffle(rows, inner, outer):
    total = rows.shape[0]
    row, col = iota((total, total), 0), iota((total, total), 1)
    return mm(one_hot(col == (row % inner) * outer + row // inner), rows).astype(BF16)


def prep_kernel(groups, m_ref, present_ref, amino_ref, *outs):
    chunk_refs, line_ref = outs[:groups], outs[groups]
    lines, width = m_ref.shape
    pairs = width // 128
    stacked = jnp.concatenate([m_ref[:, t * 128 : (t + 1) * 128] for t in range(pairs)], axis=0)
    normed = paired_norm(stacked, 64)
    both = row_shuffle(jnp.concatenate([normed, stacked], axis=1), pairs, lines)
    line_ref[...] = both[:, 128:]
    kept = (present_ref[...] * amino_ref[...]).astype(F32).astype(BF16)
    size = lines // groups
    residues = 2 * pairs
    for g in range(groups):
        chunk_refs[g][: size * pairs, :] = both[g * size * pairs : (g + 1) * size * pairs, :128]
        row, col = iota((128, lines), 0), iota((128, lines), 1)
        spread = mm(one_hot((row % size == col - g * size) & (row < 2 * size)), kept).astype(BF16)
        row, col = iota((pairs, residues), 0), iota((pairs, residues), 1)
        even = mm_nt(one_hot(col == 2 * row), spread)
        odd = mm_nt(one_hot(col == 2 * row + 1), spread)
        chunk_refs[g][size * pairs :, :] = jnp.where(
            iota((pairs, 128), 1) < size, even, odd
        ).astype(BF16)


def bias_kernel(x_ref, w_ref, out_ref, acc_ref):
    step = pl.program_id(0)
    heads = w_ref.shape[0]
    per_step, keys, channels = x_ref.shape
    centring = block_matrix(channels, channels, 1.0 - 1.0 / channels, -1.0 / channels)
    mean_row = jnp.full((heads, channels), 1.0 / channels, BF16)
    for n in range(per_step):
        centre = mm(x_ref[n], centring).astype(BF16)
        projected = mm_nt(w_ref[...], centre)
        spread = mm_nt(mean_row, centre * centre)
        start = pl.multiple_of((step * per_step + n) * heads, heads)
        acc_ref[pl.ds(start, heads), :] = projected * lax.rsqrt(spread + EPS)

    @pl.when(step == pl.num_programs(0) - 1)
    def _():
        out_ref[...] = acc_ref[...].astype(BF16)


def order_kernel(residues, index_of, me_ref, bias_ref, out_ref):
    keys = bias_ref.shape[1]
    lane = iota((1, keys), 1)
    half = keys // 2
    parity, rest = lane // half, lane % half
    place, pair = rest // (residues // 2), rest % (residues // 2)
    target = (index_of(place) ^ me_ref[0]) * residues + 2 * pair + parity
    piece = 256
    total = jnp.zeros(bias_ref.shape, F32)
    for start in range(0, keys, piece):
        chosen = one_hot(iota((piece, keys), 0) + start == target)
        total = total + mm(bias_ref[:, start : start + piece], chosen)
    out_ref[...] = total * LOG2E


def attend_kernel(heads, pieces, size, pairs, own_ref, wq_ref, wk_ref, wv_ref, bias_ref, *refs):
    piece_refs, out_ref, mask_ref, query_ref = refs[: len(pieces)], refs[-3], refs[-2], refs[-1]
    depth = 128 // (2 * heads)
    rows = pairs * 2 * heads
    order = sorted(
        (place, n, k) for n, places in enumerate(pieces) for k, place in enumerate(places)
    )
    keys = len(order) * pairs
    present = jnp.concatenate(
        [piece_refs[n][k, size * pairs :, :] for _, n, k in order], axis=0
    )
    identity = one_hot(iota((2 * size, 128), 0) == iota((2 * size, 128), 1))
    mask_ref[...] = (1e9 * LOG2E) * (mm_nt(identity, present) - 1.0)
    query = mm(own_ref[: size * pairs, :], wq_ref[...]) * (depth**-0.5)
    query_ref[...] = query.astype(BF16).astype(F32)
    lane, row = iota((2 * heads, 128), 1), iota((2 * heads, 128), 0)
    own_head = jnp.where(lane // depth == row, 1.0, 0.0)[None]
    low_lanes = iota((rows, 128), 1) < 64

    def one_line(s, carry):
        q = query_ref[pl.ds(pl.multiple_of(s * pairs, pairs), pairs), :]
        spread = (q[:, None, :] * own_head).reshape(rows, 128).astype(BF16)
        folded = (mm(spread, wk_ref[...]) * LOG2E).astype(BF16)
        start = pl.multiple_of(s * pairs, pairs)
        keyed = jnp.concatenate(
            [piece_refs[n][k, pl.ds(start, pairs), :] for _, n, k in order], axis=0
        )
        logits = [
            mm_nt(folded[:, 128 * p : 128 * (p + 1)], keyed)
            + bias_ref[:, p * keys : (p + 1) * keys]
            + mask_ref[pl.ds(p * size + s, 1), :]
            for p in range(2)
        ]
        peak = jnp.max(jnp.maximum(logits[0], logits[1]), axis=-1, keepdims=True)
        exped = [jnp.exp2(part - peak) for part in logits]
        total = jnp.sum(exped[0] + exped[1], axis=-1, keepdims=True)
        summed = [mm(part.astype(BF16), keyed) for part in exped]
        mean = (jnp.where(low_lanes, summed[0], summed[1]) / total).astype(BF16)
        valued = mm(mean, wv_ref[...]).reshape(pairs, 2 * heads, 128)
        out_ref[pl.ds(start, pairs), :] = jnp.sum(valued * own_head, axis=1)
        return carry

    lax.fori_loop(0, size, one_line, 0)


def final_kernel(
    lines, with_column, normed_refs, line_ref, attended_refs, present_ref, amino_ref, weights, out_ref
):
    wg, wo, wc, wout = weights
    total = line_ref.shape[0]
    pairs = total // lines
    normed = jnp.concatenate([r[: total // len(normed_refs), :] for r in normed_refs], axis=0)
    attended = jnp.concatenate([r[...] for r in attended_refs], axis=0)
    gated = (jax.nn.sigmoid(mm(normed, wg[...])) * attended).astype(BF16)
    row = (line_ref[...].astype(F32) + mm(gated, wo[...])).astype(BF16)
    if not with_column:
        out_ref[...] = row
        return
    kept_small = (present_ref[...] * amino_ref[...]).astype(F32).astype(BF16)
    spread = mm(one_hot(iota((total, lines), 0) // pairs == iota((total, lines), 1)), kept_small)
    own = iota((total, 2 * pairs), 1) // 2 == iota((total, 2 * pairs), 0) % pairs
    sides = one_hot(iota((2 * pairs, 128), 0) % 2 == iota((2 * pairs, 128), 1) // 64)
    kept = mm(jnp.where(own, spread, 0.0).astype(BF16), sides)

    projected = mm(paired_norm(row, 64), wc[...])
    query, gate, key, value = [projected[:, 128 * n : 128 * (n + 1)] for n in range(4)]

    def grid(a):
        return a.reshape(lines, pairs, 128)

    count = jnp.maximum(jnp.sum(grid(kept), axis=0), 1.0)
    mean_query = jnp.sum(grid(kept * query), axis=0) / count * (8**-0.5)
    same_head = block_matrix(128, 8, 1.0, 1.0)
    product = (mean_query[None] * grid(key)).reshape(total, 128)
    logits = grid(mm_split(product, same_head) + 1e9 * (kept - 1.0))
    exped = jnp.exp(logits - jnp.max(logits, axis=0, keepdims=True))
    mixed = jnp.sum(exped * grid(value), axis=0) / jnp.sum(exped, axis=0)
    gated = (jax.nn.sigmoid(grid(gate)) * mixed[None]).reshape(total, 128).astype(BF16)
    result = (row.astype(F32) + mm(gated, wout[...])).astype(BF16)
    shuffled = row_shuffle(result, lines, pairs)
    for t in range(pairs):
        out_ref[:, t * 128 : (t + 1) * 128] = shuffled[t * lines : (t + 1) * lines, :]


def call(kernel, out_shape, *args, **options):
    flops = options.pop("flops", 0)
    limit = pltpu.CompilerParams(vmem_limit_bytes=VMEM_LIMIT)
    moved = sum(a.size * a.dtype.itemsize for a in args)
    cost = pl.CostEstimate(flops=flops, bytes_accessed=moved, transcendentals=0)
    return pl.pallas_call(
        kernel, out_shape=out_shape, compiler_params=limit, cost_estimate=cost, **options
    )(*args)


def shape(*dims, dtype=BF16):
    return jax.ShapeDtypeStruct(dims, dtype)


def twice(matrix):
    return jnp.kron(jnp.eye(2, dtype=matrix.dtype), matrix)


def exchange(x, flip, devices):
    return lax.ppermute(x, "res", [(d, d ^ flip) for d in range(devices)])


def layer_normalize(values_in):
    centre = values_in - jnp.mean(values_in, axis=-1, keepdims=True)
    spread = jnp.mean(centre * centre, axis=-1, keepdims=True)
    return centre * lax.rsqrt(spread + EPS)


def column_complete(line, kept, vertical_matrix, vertical_exit_matrix, heads, depth):
    lines, columns, features = line.shape
    hidden = heads * depth
    normed = layer_normalize(line.astype(F32)).astype(BF16)
    projected = mm(normed.reshape(-1, features), vertical_matrix).reshape(lines, columns, -1)
    query, gate = projected[..., :hidden], projected[..., hidden : 2 * hidden]
    key = projected[..., 2 * hidden : 2 * hidden + depth]
    value = projected[..., 2 * hidden + depth :]
    count = jnp.maximum(jnp.sum(kept, axis=0), 1.0)[:, None]
    mean_query = jnp.sum(kept[..., None] * query, axis=0) / count * depth**-0.5
    logits = jnp.einsum("ihc,sic->sih", mean_query.reshape(columns, heads, depth), key)
    logits = logits + 1e9 * (kept - 1.0)[..., None]
    exped = jnp.exp(logits - jnp.max(logits, axis=0, keepdims=True))
    mixed = jnp.einsum("sih,sic->ihc", exped, value) / jnp.sum(exped, axis=0)[..., None]
    gate = jax.nn.sigmoid(gate).reshape(lines, columns, heads, depth)
    gated = (gate * mixed[None]).reshape(-1, hidden).astype(BF16)
    update = mm(gated, vertical_exit_matrix).reshape(lines, columns, features)
    return (line.astype(F32) + update).astype(BF16)


def on_device(
    seq_size,
    res_size,
    extra_activations,
    pair,
    present,
    amino,
    offset_matrix,
    horizontal_matrix,
    horizontal_exit_matrix,
    vertical_matrix,
    vertical_exit_matrix,
):
    lines, residues = present.shape
    pairs = residues // 2
    hidden = horizontal_exit_matrix.shape[0]
    heads = offset_matrix.shape[1]
    depth = hidden // heads
    groups = 4
    size = lines // groups
    chunk_rows = size * pairs + pairs
    keys = res_size * residues
    rows = residues * heads
    amino_row = amino.reshape(1, residues)

    prepared = call(
        functools.partial(prep_kernel, groups),
        [shape(chunk_rows, 128)] * groups + [shape(lines * pairs, 128)],
        extra_activations,
        present,
        amino_row,
    )
    chunks, line = prepared[:groups], prepared[groups]

    gathered = []
    core, near, far, high = 1, 2, 4, 8
    for g, chunk in enumerate(chunks):
        first, second = (near, far) if g % 2 == 0 else (far, near)
        column = jnp.stack([chunk] + [exchange(chunk, high * k, res_size) for k in range(1, 4)])
        plane = jnp.concatenate([column, exchange(column, first, res_size)])
        other = exchange(plane, second, res_size)
        whole = jnp.concatenate([plane, other])
        mirrored = exchange(whole, core, res_size)
        gathered.append((whole, mirrored))

    per_step = 4
    bias = call(
        bias_kernel,
        shape(rows, pair.shape[1]),
        pair,
        offset_matrix.T,
        grid=(residues // per_step,),
        in_specs=[
            pl.BlockSpec((per_step,) + pair.shape[1:], lambda n: (n, 0, 0)),
            pl.BlockSpec((heads, pair.shape[2]), lambda n: (0, 0)),
        ],
        out_specs=pl.BlockSpec((rows, pair.shape[1]), lambda n: (0, 0)),
        scratch_shapes=[pltpu.VMEM((rows, pair.shape[1]), F32)],
        flops=4 * pair.size * 128,
    )
    if seq_size > 1:
        bias = lax.all_gather(bias, "seq", axis=1, tiled=True)

    def index_of(place):
        return (place % 4) * 8 + (place // 8 % 2) * 4 + (place // 4 % 2) * 2 + place // 16

    me = lax.axis_index("res").astype(jnp.int32).reshape(1)
    vmem = pl.BlockSpec(memory_space=pltpu.VMEM)
    bias = call(
        functools.partial(order_kernel, residues, index_of),
        shape(rows, keys, dtype=F32),
        me,
        bias,
        in_specs=[pl.BlockSpec(memory_space=pltpu.SMEM), vmem],
        flops=2 * rows * keys * keys,
    )

    w_query, w_key, w_value, w_gate = [
        horizontal_matrix[:, n * hidden : (n + 1) * hidden] for n in range(4)
    ]
    folded = jnp.concatenate([w_key.T, w_key.T], axis=0)
    empty = jnp.zeros_like(folded)
    wk = jnp.concatenate([folded, empty, empty, folded], axis=1)
    wv = jnp.tile(w_value, (2, 2))
    wq = twice(w_query)

    attended = []
    for g, (whole, mirrored) in enumerate(gathered):
        half = whole.shape[0]
        if g % 2 == 0:
            places = list(range(half))
        else:
            places = [(n // 4 % 2) * 8 + (n // 8) * 4 + n % 4 for n in range(half)]
        pieces = (tuple(places), tuple(p + half for p in places))
        attended.append(
            call(
                functools.partial(attend_kernel, heads, pieces, size, pairs),
                shape(size * pairs, 128, dtype=F32),
                chunks[g],
                wq,
                wk,
                wv,
                bias,
                whole,
                mirrored,
                scratch_shapes=[
                    pltpu.VMEM((2 * size, keys // 2), F32),
                    pltpu.VMEM((size * pairs, 128), F32),
                ],
                flops=size * rows * keys * 2 * 256 * 2,
            )
        )

    w_column = [
        vertical_matrix[:, :hidden],
        vertical_matrix[:, hidden : 2 * hidden],
        jnp.tile(vertical_matrix[:, 2 * hidden : 2 * hidden + depth], (1, heads)),
        jnp.tile(vertical_matrix[:, 2 * hidden + depth :], (1, heads)),
    ]
    weights = (
        twice(w_gate),
        twice(horizontal_exit_matrix),
        jnp.concatenate([twice(w) for w in w_column], axis=1),
        twice(vertical_exit_matrix),
    )
    with_column = seq_size == 1

    def finish(*refs):
        final_kernel(
            lines,
            with_column,
            refs[:groups],
            refs[groups],
            refs[groups + 1 : 2 * groups + 1],
            refs[2 * groups + 1],
            refs[2 * groups + 2],
            refs[2 * groups + 3 : 2 * groups + 7],
            refs[-1],
        )

    out_shape = shape(*extra_activations.shape) if with_column else shape(lines * pairs, 128)
    result = call(finish, out_shape, *chunks, line, *attended, present, amino_row, *weights)
    if with_column:
        return result
    row = result.reshape(lines, residues, hidden)
    kept = (present * amino_row).astype(BF16)
    moved = lax.all_to_all(row, "seq", split_axis=1, concat_axis=0, tiled=True)
    moved_kept = lax.all_to_all(kept, "seq", split_axis=1, concat_axis=0, tiled=True)
    updated = column_complete(
        moved, moved_kept.astype(F32), vertical_matrix, vertical_exit_matrix, heads, depth
    )
    back = lax.all_to_all(updated, "seq", split_axis=0, concat_axis=1, tiled=True)
    return back.reshape(extra_activations.shape)


def solution(mesh):
    in_specs = (
        P("seq", "res"),
        P("res", "seq", None),
        P("seq", "res"),
        P("res"),
        P(),
        P(),
        P(),
        P(),
        P(),
    )
    sizes = mesh.shape
    return jax.shard_map(
        functools.partial(on_device, sizes["seq"], sizes["res"]),
        mesh=mesh,
        in_specs=in_specs,
        out_specs=P("seq", "res"),
        check_vma=False,
    )
```

time: 291 us -> 119 us (0.41)
  waiting for transfers between devices: 88.1 us -> 6.63 us
  Pallas kernels: 0 us -> 60.6 us
  other arithmetic: 53.7 us -> 2.7 us
  matrix products: 48.2 us -> 0 us
  blocking collectives: 44.6 us -> 0 us
  starting transfers between devices: 0.04 us -> 30.4 us
  local copies, waits for them, and re-layouts: 40.8 us -> 17.7 us
  between operations: 13.7 us -> 0.25 us
    all_gather x2 -> x0, waiting for transfers between devices: 87.4 us -> none  [the longest x1 77.1 us: on_device(): lax.all_gather(value_local, 'res', axis=1, tiled=True)]
    pallas_call x0 -> x8, Pallas kernels: none -> 60.6 us  [call(): pl.pallas_call(kernel, out_shape=out_shape, compiler_params=limit, cost_e...]
    reduce_sum x16 -> x0, other arithmetic: 52.2 us -> none  [the longest x8 34.1 us: attend_block(): total = running[1] * rescale + jnp.sum(exped, axis=-1)]
    dot_general x23 -> x0, matrix products: 48.2 us -> none  [the longest x8 21.9 us: attend_block(): jnp.einsum('sihc,sjhc->hsij', query_heads, key_heads, preferred_element_t...]
    all_gather x1 -> x0, blocking collectives: 44.6 us -> none  [on_device(): lax.all_gather(mask_wire, 'res', axis=1, tiled=True)]
    ppermute x0 -> x24, starting transfers between devices: none -> 30.4 us  [exchange(): return lax.ppermute(x, 'res', [(d, d ^ flip) for d in range(devices)])]
    reshape x10 -> x0, local copies, waits for them, and re-layouts: 11.6 us -> none  [the longest x8 10.3 us: attend_block(): value_block.reshape(homolog_lines, block_size, head_number, head_channel_...]
    unnamed x21 -> x31, local copies, waits for them, and re-layouts: 18.5 us -> 8.45 us
  transfers between devices with their start and end apart: 2 -> 24, of which waited for: 2 -> 4; matrix products, arithmetic and copies ran while one was open for 14% -> 16% of each run, Pallas kernels for 0% -> 38%
where the time goes in v1:
time: 119 us; the launch traced here: 118 us
  Pallas kernels  60.6 us (51%)
  starting transfers between devices  30.4 us (26%)
  local copies, waits for them, and re-layouts  17.7 us (15%)
  waiting for transfers between devices  6.63 us (6%)
  other arithmetic  2.7 us (2%)
    pallas_call x8, Pallas kernels, call(): pl.pallas_call(kernel, out_shape=out_shape, compiler_params=limit, cost_e...  60.6 us
    ppermute x24, starting transfers between devices, exchange(): return lax.ppermute(x, 'res', [(d, d ^ flip) for d in range(devices)])  30.4 us
    unnamed x31, local copies, waits for them, and re-layouts  8.45 us
    ppermute x24, waiting for transfers between devices, exchange(): return lax.ppermute(x, 'res', [(d, d ^ flip) for d in range(devices)])  6.63 us
    mul x8, local copies, waits for them, and re-layouts, twice(): return jnp.kron(jnp.eye(2, dtype=matrix.dtype), matrix)  3.19 us
  transfers between devices with their start and end apart: 24, of which 4 were waited for; matrix products, arithmetic and copies ran while one was open for 16% of the time, Pallas kernels for 38%

profile of v1, /device:TPU:0, one launch (start us, length us, event | category | flops | bytes accessed | tf_op | source)
XLA Modules:
  0.0 118.3 jit_solution(15324921507958858073)
XLA Ops:
  0.0 2.8 %shard_map.91 = (bf16[144,128]{1,0:T(8,128)(2,1)}, bf16[144,128]{1,0:T(8,128)(2,1)}, bf16[144,128]{1,0:T(8,128)(2,1)}, bf16[144,128]{1,0:T(8,128)(2,1)}, bf16[512,128]{1,0:T(8,128)(2,1)}) custom-call(bf16[32,2048]{1,0:T(8,128)(2,1)} %m_ref.1, s32[32,32]{1,0:T(8,128)} %refs_9_.1, s32[1,32]{1,0:T(1,128)} %bitcast.74), custom_call_target="tpu_custom_call" | custom-call | bytes 135296 | tf_op jit(solution)/shard_map/pallas_call | solution.py:210
  2.8 3.1 %collective-permute-start = (bf16[144,128]{1,0:T(8,128)(2,1)}, bf16[144,128]{1,0:T(8,128)(2,1)S(1)}, u32[]{:S(2)}, u32[]{:S(2)}) collective-permute-start(bf16[144,128]{1,0:T(8,128)(2,1)} %get-tuple-element.10.own_ref.refs_0_), channel_id=1, source_target_pairs={{0,8},{1,9},{2,10},{3,11},{4,12},{5,13},{6,14},{7,15},{8,0},{9,1},... | collective-permute-start | bytes 110600 | tf_op jit(solution)/shard_map/ppermute | solution.py:224
  5.9 2.6 %collective-permute-start.1 = (bf16[144,128]{1,0:T(8,128)(2,1)}, bf16[144,128]{1,0:T(8,128)(2,1)S(1)}, u32[]{:S(2)}, u32[]{:S(2)}) collective-permute-start(bf16[144,128]{1,0:T(8,128)(2,1)} %get-tuple-element.10.own_ref.refs_0_), channel_id=1, source_target_pairs={{0,16},{1,17},{2,18},{3,19},{4,20},{5,21},{6,22},{7,23},{8,24},{9,... | collective-permute-start | bytes 110600 | tf_op jit(solution)/shard_map/ppermute | solution.py:224
  8.5 0.9 collective-permute-start.6
  9.4 3.5 %collective-permute-start.7 = (bf16[144,128]{1,0:T(8,128)(2,1)}, bf16[144,128]{1,0:T(8,128)(2,1)S(1)}, u32[]{:S(2)}, u32[]{:S(2)}) collective-permute-start(bf16[144,128]{1,0:T(8,128)(2,1)} %get-tuple-element.11.own_ref.refs_1_), channel_id=1, source_target_pairs={{0,16},{1,17},{2,18},{3,19},{4,20},{5,21},{6,22},{7,23},{8,24},{9,... | collective-permute-start | bytes 110600 | tf_op jit(solution)/shard_map/ppermute | solution.py:224
  12.9 1.4 %constant_dynamic-update-slice_fusion.4 = (bf16[8,144,128]{2,1,0:T(8,128)(2,1)S(1)}, bf16[16,144,128]{2,1,0:T(8,128)(2,1)}, bf16[16,144,128]{2,1,0:T(8,128)(2,1)S(1)}, bf16[8,144,128]{2,1,0:T(8,128)(2,1)S(1)}) fusion(bf16[144,128]{1,0:T(8,128)(2,1)} %get-tuple-element.10.own_ref.refs_0_, bf16[144,128]{1,0:T(8,128)(2,1)} %get-tuple-element.11.own_ref.refs_1_), kind=kLoop, calls=%fused_computation.9 | loop fusion | bytes 221184
  14.3 0.9 fusion.1
  15.2 0.9 fusion
  17.4 1.4 %constant_dynamic-update-slice_fusion.26 = (bf16[8,144,128]{2,1,0:T(8,128)(2,1)S(1)}, bf16[16,144,128]{2,1,0:T(8,128)(2,1)}, bf16[16,144,128]{2,1,0:T(8,128)(2,1)S(1)}, bf16[8,144,128]{2,1,0:T(8,128)(2,1)S(1)}) fusion(bf16[144,128]{1,0:T(8,128)(2,1)} %get-tuple-element.12.own_ref.refs_2_, bf16[144,128]{1,0:T(8,128)(2,1)} %get-tuple-element.13.own_ref.refs_3_), kind=kLoop, calls=%fused_computation.31 | loop fusion | bytes 221184
  18.8 1.2 %broadcast_multiply_fusion = (bf16[2,64,2,64]{3,2,1,0:T(2,128)(2,1)S(1)}, bf16[2,64,2,64]{3,2,1,0:T(2,128)(2,1)S(1)}, bf16[2,64,2,64]{3,2,1,0:T(2,128)(2,1)S(1)}...) fusion(bf16[64,64]{1,0:T(8,128)(2,1)} %param.17, ...), kind=kLoop, calls=%fused_computation.50 | loop fusion | flops 131072 | bytes 327688 | tf_op jit(solution)/shard_map/jit(kron)/mul | solution.py:220
  20.0 13.1 %shard_map.92.bias_ref = bf16[256,1024]{1,0:T(8,128)(2,1)} custom-call(bf16[32,1024,128]{2,1,0:T(8,128)(2,1)} %x_ref.1, bf16[8,128]{1,0:T(8,128)(2,1)} %bitcast.73), custom_call_target="tpu_custom_call" | custom-call | flops 2147483648 | bytes 8390656 | tf_op jit(solution)/shard_map/pallas_call | solution.py:210
  34.3 3.8 %collective-permute-start.13 = (bf16[144,128]{1,0:T(8,128)(2,1)S(1)}, bf16[144,128]{1,0:T(8,128)(2,1)S(1)}, u32[]{:S(2)}, u32[]{:S(2)}) collective-permute-start(bf16[144,128]{1,0:T(8,128)(2,1)S(1)} %copy-done.2), channel_id=1, source_target_pairs={{0,16},{1,17},{2,18},{3,19},{4,20},{5,21},{6,22},{7,23},{8,24},{9,... | collective-permute-start | bytes 110600 | tf_op jit(solution)/shard_map/ppermute | solution.py:224
  39.4 3.1 %collective-permute-start.19 = (bf16[144,128]{1,0:T(8,128)(2,1)S(1)}, bf16[144,128]{1,0:T(8,128)(2,1)S(1)}, u32[]{:S(2)}, u32[]{:S(2)}) collective-permute-start(bf16[144,128]{1,0:T(8,128)(2,1)S(1)} %copy-done.3), channel_id=1, source_target_pairs={{0,16},{1,17},{2,18},{3,19},{4,20},{5,21},{6,22},{7,23},{8,24},{9,... | collective-permute-start | bytes 110600 | tf_op jit(solution)/shard_map/ppermute | solution.py:224
  42.7 1.6 %collective-permute-start.3 = (bf16[4,144,128]{2,1,0:T(8,128)(2,1)S(1)}, bf16[4,144,128]{2,1,0:T(8,128)(2,1)S(1)}, u32[]{:S(2)}, u32[]{:S(2)}) collective-permute-start(bf16[4,144,128]{2,1,0:T(8,128)(2,1)S(1)} %pad_maximum_fusion), channel_id=1, source_target_pairs={{0,2},{1,3},{2,0},{3,1},{4,6},{5,7},{6,4},{7,5},{8,10},{9,11},{10,... | collective-permute-start | bytes 442376 | tf_op jit(solution)/shard_map/ppermute | solution.py:224
  44.4 1.5 %collective-permute-start.9 = (bf16[4,144,128]{2,1,0:T(8,128)(2,1)S(1)}, bf16[4,144,128]{2,1,0:T(8,128)(2,1)S(1)}, u32[]{:S(2)}, u32[]{:S(2)}) collective-permute-start(bf16[4,144,128]{2,1,0:T(8,128)(2,1)S(1)} %pad_maximum_fusion.1), channel_id=1, source_target_pairs={{0,4},{1,5},{2,6},{3,7},{4,0},{5,1},{6,2},{7,3},{8,12},{9,13},{10,... | collective-permute-start | bytes 442376 | tf_op jit(solution)/shard_map/ppermute | solution.py:224
  45.9 1.2 %collective-permute-start.15 = (bf16[4,144,128]{2,1,0:T(8,128)(2,1)S(1)}, bf16[4,144,128]{2,1,0:T(8,128)(2,1)S(1)}, u32[]{:S(2)}, u32[]{:S(2)}) collective-permute-start(bf16[4,144,128]{2,1,0:T(8,128)(2,1)S(1)} %pad_maximum_fusion.2), channel_id=1, source_target_pairs={{0,2},{1,3},{2,0},{3,1},{4,6},{5,7},{6,4},{7,5},{8,10},{9,11},{10,... | collective-permute-start | bytes 442376 | tf_op jit(solution)/shard_map/ppermute | solution.py:224
  47.1 1.3 %collective-permute-done.20 = bf16[144,128]{1,0:T(8,128)(2,1)S(1)} collective-permute-done((bf16[144,128]{1,0:T(8,128)(2,1)S(1)}, bf16[144,128]{1,0:T(8,128)(2,1)S(1)}, u32[]{:S(2)}, u32[]{:S(2)}) %collective-permute-start.20) | collective-permute-done | bytes 36896 | tf_op jit(solution)/shard_map/ppermute | solution.py:224
  48.4 1.6 %collective-permute-start.21 = (bf16[4,144,128]{2,1,0:T(8,128)(2,1)S(1)}, bf16[4,144,128]{2,1,0:T(8,128)(2,1)S(1)}, u32[]{:S(2)}, u32[]{:S(2)}) collective-permute-start(bf16[4,144,128]{2,1,0:T(8,128)(2,1)S(1)} %pad_maximum_fusion.3), channel_id=1, source_target_pairs={{0,4},{1,5},{2,6},{3,7},{4,0},{5,1},{6,2},{7,3},{8,12},{9,13},{10,... | collective-permute-start | bytes 442376 | tf_op jit(solution)/shard_map/ppermute | solution.py:224
  55.1 1.6 %collective-permute-start.10 = (bf16[8,144,128]{2,1,0:T(8,128)(2,1)S(1)}, bf16[8,144,128]{2,1,0:T(8,128)(2,1)S(1)}, u32[]{:S(2)}, u32[]{:S(2)}) collective-permute-start(bf16[8,144,128]{2,1,0:T(8,128)(2,1)S(1)} %get-tuple-element.19), channel_id=1, source_target_pairs={{0,2},{1,3},{2,0},{3,1},{4,6},{5,7},{6,4},{7,5},{8,10},{9,11},{10,... | collective-permute-start | bytes 884744 | tf_op jit(solution)/shard_map/ppermute | solution.py:224
  57.4 1.5 %collective-permute-start.16 = (bf16[8,144,128]{2,1,0:T(8,128)(2,1)S(1)}, bf16[8,144,128]{2,1,0:T(8,128)(2,1)S(1)}, u32[]{:S(2)}, u32[]{:S(2)}) collective-permute-start(bf16[8,144,128]{2,1,0:T(8,128)(2,1)S(1)} %get-tuple-element.17), channel_id=1, source_target_pairs={{0,4},{1,5},{2,6},{3,7},{4,0},{5,1},{6,2},{7,3},{8,12},{9,13},{10,... | collective-permute-start | bytes 884744 | tf_op jit(solution)/shard_map/ppermute | solution.py:224
  58.9 4.2 %collective-permute-done.4 = bf16[8,144,128]{2,1,0:T(8,128)(2,1)S(1)} collective-permute-done((bf16[8,144,128]{2,1,0:T(8,128)(2,1)S(1)}, bf16[8,144,128]{2,1,0:T(8,128)(2,1)S(1)}, u32[]{:S(2)}, u32[]{:S(2)}) %collective-permute-start.4) | collective-permute-done | bytes 294944 | tf_op jit(solution)/shard_map/ppermute | solution.py:224
  63.1 0.7 constant_dynamic-update-slice_fusion.5.refs_0_
  63.9 1.6 %collective-permute-start.22 = (bf16[8,144,128]{2,1,0:T(8,128)(2,1)S(1)}, bf16[8,144,128]{2,1,0:T(8,128)(2,1)S(1)}, u32[]{:S(2)}, u32[]{:S(2)}) collective-permute-start(bf16[8,144,128]{2,1,0:T(8,128)(2,1)S(1)} %get-tuple-element.15), channel_id=1, source_target_pairs={{0,2},{1,3},{2,0},{3,1},{4,6},{5,7},{6,4},{7,5},{8,10},{9,11},{10,... | collective-permute-start | bytes 884744 | tf_op jit(solution)/shard_map/ppermute | solution.py:224
  66.3 0.7 constant_dynamic-update-slice_fusion.27.refs_0_
  71.2 2.8 %shard_map.93.bias_ref = f32[256,1024]{1,0:T(8,128)} custom-call(s32[1]{0:T(128)} %bitcast.2.me_ref, bf16[256,1024]{1,0:T(8,128)(2,1)} %shard_map.92.bias_ref), custom_call_target="tpu_custom_call" | custom-call | flops 536870912 | bytes 524292 | tf_op jit(solution)/shard_map/pallas_call | solution.py:210
  74.7 0.9 copy-done.6
  75.5 9.6 %shard_map.94.refs_5_ = f32[128,128]{1,0:T(8,128)} custom-call(bf16[144,128]{1,0:T(8,128)(2,1)} %get-tuple-element.10.own_ref.refs_0_, bf16[128,128]{1,0:T(8,128)(2,1)} %mul.146.wq_ref, bf16[128,256]{1,0:T(8,128)(2,1)} %maximum_maximum_fusion.wk_ref, bf16[128,128]{1,0:T(8,128)(2,1)} %tile.13.wv_ref, f32[256,1024]{1,0:T(8,128)} %shard_map.93.bias_ref, ...), custom_call_target="tpu_custom_call" | custom-call | flops 2147483648 | bytes 2396160 | tf_op jit(solution)/shard_map/pallas_call | solution.py:210
  85.1 9.6 %shard_map.95.refs_6_ = f32[128,128]{1,0:T(8,128)} custom-call(bf16[144,128]{1,0:T(8,128)(2,1)} %get-tuple-element.11.own_ref.refs_1_, bf16[128,128]{1,0:T(8,128)(2,1)} %mul.146.wq_ref, bf16[128,256]{1,0:T(8,128)(2,1)} %maximum_maximum_fusion.wk_ref, bf16[128,128]{1,0:T(8,128)(2,1)} %tile.13.wv_ref, f32[256,1024]{1,0:T(8,128)} %shard_map.93.bias_ref, ...), custom_call_target="tpu_custom_call" | custom-call | flops 2147483648 | bytes 2396160 | tf_op jit(solution)/shard_map/pallas_call | solution.py:210
  94.7 9.6 %shard_map.96.refs_7_ = f32[128,128]{1,0:T(8,128)} custom-call(bf16[144,128]{1,0:T(8,128)(2,1)} %get-tuple-element.12.own_ref.refs_2_, bf16[128,128]{1,0:T(8,128)(2,1)} %mul.146.wq_ref, bf16[128,256]{1,0:T(8,128)(2,1)} %maximum_maximum_fusion.wk_ref, bf16[128,128]{1,0:T(8,128)(2,1)} %tile.13.wv_ref, f32[256,1024]{1,0:T(8,128)} %shard_map.93.bias_ref, ...), custom_call_target="tpu_custom_call" | custom-call | flops 2147483648 | bytes 2396160 | tf_op jit(solution)/shard_map/pallas_call | solution.py:210
  104.3 0.8 copy-done.7
  105.1 9.6 %shard_map.97.refs_8_ = f32[128,128]{1,0:T(8,128)} custom-call(bf16[144,128]{1,0:T(8,128)(2,1)} %get-tuple-element.13.own_ref.refs_3_, bf16[128,128]{1,0:T(8,128)(2,1)} %mul.146.wq_ref, bf16[128,256]{1,0:T(8,128)(2,1)} %maximum_maximum_fusion.wk_ref, bf16[128,128]{1,0:T(8,128)(2,1)} %tile.13.wv_ref, f32[256,1024]{1,0:T(8,128)} %shard_map.93.bias_ref, ...), custom_call_target="tpu_custom_call" | custom-call | flops 2147483648 | bytes 2396160 | tf_op jit(solution)/shard_map/pallas_call | solution.py:210
  114.7 3.6 %shard_map.98 = bf16[32,2048]{1,0:T(8,128)(2,1)} custom-call(bf16[144,128]{1,0:T(8,128)(2,1)} %get-tuple-element.10.own_ref.refs_0_, bf16[144,128]{1,0:T(8,128)(2,1)} %get-tuple-element.11.own_ref.refs_1_, bf16[144,128]{1,0:T(8,128)(2,1)} %get-tuple-element.12.own_ref.refs_2_, bf16[144,128]{1,0:T(8,128)(2,1)} %get-tuple-element.13.own_ref.refs_3_, ...), custom_call_target="tpu_custom_call" | custom-call | bytes 774272 | tf_op jit(solution)/shard_map/pallas_call | solution.py:210
  (91 shorter events, 15.4 us)
Async XLA Ops:
  2.8 30.8 %copy-start.1 = (bf16[144,128]{1,0:T(8,128)(2,1)S(1)}, bf16[144,128]{1,0:T(8,128)(2,1)}, u32[]{:S(2)}) copy-start(bf16[144,128]{1,0:T(8,128)(2,1)} %get-tuple-element.11.own_ref.refs_1_) | copy-start | bytes 110596
  2.8 30.9 %copy-start.2 = (bf16[144,128]{1,0:T(8,128)(2,1)S(1)}, bf16[144,128]{1,0:T(8,128)(2,1)}, u32[]{:S(2)}) copy-start(bf16[144,128]{1,0:T(8,128)(2,1)} %get-tuple-element.12.own_ref.refs_2_) | copy-start | bytes 110596
  2.8 35.2 %copy-start = (bf16[144,128]{1,0:T(8,128)(2,1)S(1)}, bf16[144,128]{1,0:T(8,128)(2,1)}, u32[]{:S(2)}) copy-start(bf16[144,128]{1,0:T(8,128)(2,1)} %get-tuple-element.10.own_ref.refs_0_) | copy-start | bytes 110596
  2.8 35.4 %copy-start.3 = (bf16[144,128]{1,0:T(8,128)(2,1)S(1)}, bf16[144,128]{1,0:T(8,128)(2,1)}, u32[]{:S(2)}) copy-start(bf16[144,128]{1,0:T(8,128)(2,1)} %get-tuple-element.13.own_ref.refs_3_) | copy-start | bytes 110596
  2.8 30.7 %collective-permute-start = (bf16[144,128]{1,0:T(8,128)(2,1)}, bf16[144,128]{1,0:T(8,128)(2,1)S(1)}, u32[]{:S(2)}, u32[]{:S(2)}) collective-permute-start(bf16[144,128]{1,0:T(8,128)(2,1)} %get-tuple-element.10.own_ref.refs_0_), channel_id=1, source_target_pairs={{0,8},{1,9},{2,10},{3,11},{4,12},{5,13},{6,14},{7,15},{8,0},{9,1},... | collective-permute-start | bytes 110600 | tf_op jit(solution)/shard_map/ppermute | solution.py:224
  5.9 27.8 %collective-permute-start.1 = (bf16[144,128]{1,0:T(8,128)(2,1)}, bf16[144,128]{1,0:T(8,128)(2,1)S(1)}, u32[]{:S(2)}, u32[]{:S(2)}) collective-permute-start(bf16[144,128]{1,0:T(8,128)(2,1)} %get-tuple-element.10.own_ref.refs_0_), channel_id=1, source_target_pairs={{0,16},{1,17},{2,18},{3,19},{4,20},{5,21},{6,22},{7,23},{8,24},{9,... | collective-permute-start | bytes 110600 | tf_op jit(solution)/shard_map/ppermute | solution.py:224
  8.5 25.8 %collective-permute-start.2 = (bf16[144,128]{1,0:T(8,128)(2,1)}, bf16[144,128]{1,0:T(8,128)(2,1)S(1)}, u32[]{:S(2)}, u32[]{:S(2)}) collective-permute-start(bf16[144,128]{1,0:T(8,128)(2,1)} %get-tuple-element.10.own_ref.refs_0_), channel_id=1, source_target_pairs={{0,24},{1,25},{2,26},{3,27},{4,28},{5,29},{6,30},{7,31},{8,16},{9,... | collective-permute-start | bytes 110600 | tf_op jit(solution)/shard_map/ppermute | solution.py:224
  8.5 29.6 %collective-permute-start.6 = (bf16[144,128]{1,0:T(8,128)(2,1)}, bf16[144,128]{1,0:T(8,128)(2,1)S(1)}, u32[]{:S(2)}, u32[]{:S(2)}) collective-permute-start(bf16[144,128]{1,0:T(8,128)(2,1)} %get-tuple-element.11.own_ref.refs_1_), channel_id=1, source_target_pairs={{0,8},{1,9},{2,10},{3,11},{4,12},{5,13},{6,14},{7,15},{8,0},{9,1},... | collective-permute-start | bytes 110600 | tf_op jit(solution)/shard_map/ppermute | solution.py:224
  9.4 28.8 %collective-permute-start.7 = (bf16[144,128]{1,0:T(8,128)(2,1)}, bf16[144,128]{1,0:T(8,128)(2,1)S(1)}, u32[]{:S(2)}, u32[]{:S(2)}) collective-permute-start(bf16[144,128]{1,0:T(8,128)(2,1)} %get-tuple-element.11.own_ref.refs_1_), channel_id=1, source_target_pairs={{0,16},{1,17},{2,18},{3,19},{4,20},{5,21},{6,22},{7,23},{8,24},{9,... | collective-permute-start | bytes 110600 | tf_op jit(solution)/shard_map/ppermute | solution.py:224
  33.6 5.8 %collective-permute-start.8 = (bf16[144,128]{1,0:T(8,128)(2,1)S(1)}, bf16[144,128]{1,0:T(8,128)(2,1)S(1)}, u32[]{:S(2)}, u32[]{:S(2)}) collective-permute-start(bf16[144,128]{1,0:T(8,128)(2,1)S(1)} %copy-done.1), channel_id=1, source_target_pairs={{0,24},{1,25},{2,26},{3,27},{4,28},{5,29},{6,30},{7,31},{8,16},{9,... | collective-permute-start | bytes 110600 | tf_op jit(solution)/shard_map/ppermute | solution.py:224
  33.7 8.9 %collective-permute-start.12 = (bf16[144,128]{1,0:T(8,128)(2,1)S(1)}, bf16[144,128]{1,0:T(8,128)(2,1)S(1)}, u32[]{:S(2)}, u32[]{:S(2)}) collective-permute-start(bf16[144,128]{1,0:T(8,128)(2,1)S(1)} %copy-done.2), channel_id=1, source_target_pairs={{0,8},{1,9},{2,10},{3,11},{4,12},{5,13},{6,14},{7,15},{8,0},{9,1},... | collective-permute-start | bytes 110600 | tf_op jit(solution)/shard_map/ppermute | solution.py:224
  34.3 8.5 %collective-permute-start.13 = (bf16[144,128]{1,0:T(8,128)(2,1)S(1)}, bf16[144,128]{1,0:T(8,128)(2,1)S(1)}, u32[]{:S(2)}, u32[]{:S(2)}) collective-permute-start(bf16[144,128]{1,0:T(8,128)(2,1)S(1)} %copy-done.2), channel_id=1, source_target_pairs={{0,16},{1,17},{2,18},{3,19},{4,20},{5,21},{6,22},{7,23},{8,24},{9,... | collective-permute-start | bytes 110600 | tf_op jit(solution)/shard_map/ppermute | solution.py:224
  38.1 6.3 %collective-permute-start.14 = (bf16[144,128]{1,0:T(8,128)(2,1)S(1)}, bf16[144,128]{1,0:T(8,128)(2,1)S(1)}, u32[]{:S(2)}, u32[]{:S(2)}) collective-permute-start(bf16[144,128]{1,0:T(8,128)(2,1)S(1)} %copy-done.2), channel_id=1, source_target_pairs={{0,24},{1,25},{2,26},{3,27},{4,28},{5,29},{6,30},{7,31},{8,16},{9,... | collective-permute-start | bytes 110600 | tf_op jit(solution)/shard_map/ppermute | solution.py:224
  38.2 7.7 %collective-permute-start.18 = (bf16[144,128]{1,0:T(8,128)(2,1)S(1)}, bf16[144,128]{1,0:T(8,128)(2,1)S(1)}, u32[]{:S(2)}, u32[]{:S(2)}) collective-permute-start(bf16[144,128]{1,0:T(8,128)(2,1)S(1)} %copy-done.3), channel_id=1, source_target_pairs={{0,8},{1,9},{2,10},{3,11},{4,12},{5,13},{6,14},{7,15},{8,0},{9,1},... | collective-permute-start | bytes 110600 | tf_op jit(solution)/shard_map/ppermute | solution.py:224
  39.4 7.7 %collective-permute-start.19 = (bf16[144,128]{1,0:T(8,128)(2,1)S(1)}, bf16[144,128]{1,0:T(8,128)(2,1)S(1)}, u32[]{:S(2)}, u32[]{:S(2)}) collective-permute-start(bf16[144,128]{1,0:T(8,128)(2,1)S(1)} %copy-done.3), channel_id=1, source_target_pairs={{0,16},{1,17},{2,18},{3,19},{4,20},{5,21},{6,22},{7,23},{8,24},{9,... | collective-permute-start | bytes 110600 | tf_op jit(solution)/shard_map/ppermute | solution.py:224
  42.6 5.8 %collective-permute-start.20 = (bf16[144,128]{1,0:T(8,128)(2,1)S(1)}, bf16[144,128]{1,0:T(8,128)(2,1)S(1)}, u32[]{:S(2)}, u32[]{:S(2)}) collective-permute-start(bf16[144,128]{1,0:T(8,128)(2,1)S(1)} %copy-done.3), channel_id=1, source_target_pairs={{0,24},{1,25},{2,26},{3,27},{4,28},{5,29},{6,30},{7,31},{8,16},{9,... | collective-permute-start | bytes 110600 | tf_op jit(solution)/shard_map/ppermute | solution.py:224
  42.7 11.1 %collective-permute-start.3 = (bf16[4,144,128]{2,1,0:T(8,128)(2,1)S(1)}, bf16[4,144,128]{2,1,0:T(8,128)(2,1)S(1)}, u32[]{:S(2)}, u32[]{:S(2)}) collective-permute-start(bf16[4,144,128]{2,1,0:T(8,128)(2,1)S(1)} %pad_maximum_fusion), channel_id=1, source_target_pairs={{0,2},{1,3},{2,0},{3,1},{4,6},{5,7},{6,4},{7,5},{8,10},{9,11},{10,... | collective-permute-start | bytes 442376 | tf_op jit(solution)/shard_map/ppermute | solution.py:224
  44.4 10.7 %collective-permute-start.9 = (bf16[4,144,128]{2,1,0:T(8,128)(2,1)S(1)}, bf16[4,144,128]{2,1,0:T(8,128)(2,1)S(1)}, u32[]{:S(2)}, u32[]{:S(2)}) collective-permute-start(bf16[4,144,128]{2,1,0:T(8,128)(2,1)S(1)} %pad_maximum_fusion.1), channel_id=1, source_target_pairs={{0,4},{1,5},{2,6},{3,7},{4,0},{5,1},{6,2},{7,3},{8,12},{9,13},{10,... | collective-permute-start | bytes 442376 | tf_op jit(solution)/shard_map/ppermute | solution.py:224
  45.9 10.8 %collective-permute-start.15 = (bf16[4,144,128]{2,1,0:T(8,128)(2,1)S(1)}, bf16[4,144,128]{2,1,0:T(8,128)(2,1)S(1)}, u32[]{:S(2)}, u32[]{:S(2)}) collective-permute-start(bf16[4,144,128]{2,1,0:T(8,128)(2,1)S(1)} %pad_maximum_fusion.2), channel_id=1, source_target_pairs={{0,2},{1,3},{2,0},{3,1},{4,6},{5,7},{6,4},{7,5},{8,10},{9,11},{10,... | collective-permute-start | bytes 442376 | tf_op jit(solution)/shard_map/ppermute | solution.py:224
  48.4 15.4 %collective-permute-start.21 = (bf16[4,144,128]{2,1,0:T(8,128)(2,1)S(1)}, bf16[4,144,128]{2,1,0:T(8,128)(2,1)S(1)}, u32[]{:S(2)}, u32[]{:S(2)}) collective-permute-start(bf16[4,144,128]{2,1,0:T(8,128)(2,1)S(1)} %pad_maximum_fusion.3), channel_id=1, source_target_pairs={{0,4},{1,5},{2,6},{3,7},{4,0},{5,1},{6,2},{7,3},{8,12},{9,13},{10,... | collective-permute-start | bytes 442376 | tf_op jit(solution)/shard_map/ppermute | solution.py:224
  54.5 8.6 %collective-permute-start.4 = (bf16[8,144,128]{2,1,0:T(8,128)(2,1)S(1)}, bf16[8,144,128]{2,1,0:T(8,128)(2,1)S(1)}, u32[]{:S(2)}, u32[]{:S(2)}) collective-permute-start(bf16[8,144,128]{2,1,0:T(8,128)(2,1)S(1)} %get-tuple-element.21), channel_id=1, source_target_pairs={{0,4},{1,5},{2,6},{3,7},{4,0},{5,1},{6,2},{7,3},{8,12},{9,13},{10,... | collective-permute-start | bytes 884744 | tf_op jit(solution)/shard_map/ppermute | solution.py:224
  55.1 10.4 %collective-permute-start.10 = (bf16[8,144,128]{2,1,0:T(8,128)(2,1)S(1)}, bf16[8,144,128]{2,1,0:T(8,128)(2,1)S(1)}, u32[]{:S(2)}, u32[]{:S(2)}) collective-permute-start(bf16[8,144,128]{2,1,0:T(8,128)(2,1)S(1)} %get-tuple-element.19), channel_id=1, source_target_pairs={{0,2},{1,3},{2,0},{3,1},{4,6},{5,7},{6,4},{7,5},{8,10},{9,11},{10,... | collective-permute-start | bytes 884744 | tf_op jit(solution)/shard_map/ppermute | solution.py:224
  57.4 8.9 %collective-permute-start.16 = (bf16[8,144,128]{2,1,0:T(8,128)(2,1)S(1)}, bf16[8,144,128]{2,1,0:T(8,128)(2,1)S(1)}, u32[]{:S(2)}, u32[]{:S(2)}) collective-permute-start(bf16[8,144,128]{2,1,0:T(8,128)(2,1)S(1)} %get-tuple-element.17), channel_id=1, source_target_pairs={{0,4},{1,5},{2,6},{3,7},{4,0},{5,1},{6,2},{7,3},{8,12},{9,13},{10,... | collective-permute-start | bytes 884744 | tf_op jit(solution)/shard_map/ppermute | solution.py:224
  63.9 10.8 %collective-permute-start.5 = (bf16[16,144,128]{2,1,0:T(8,128)(2,1)}, bf16[16,144,128]{2,1,0:T(8,128)(2,1)S(1)}, u32[]{:S(2)}, u32[]{:S(2)}) collective-permute-start(bf16[16,144,128]{2,1,0:T(8,128)(2,1)} %constant_dynamic-update-slice_fusion.5.refs_0_), channel_id=1, source_target_pairs={{0,1},{1,0},{2,3},{3,2},{4,5},{5,4},{6,7},{7,6},{8,9},{9,8},{10,11... | collective-permute-start | bytes 1769480 | tf_op jit(solution)/shard_map/ppermute | solution.py:224
  63.9 10.1 %collective-permute-start.22 = (bf16[8,144,128]{2,1,0:T(8,128)(2,1)S(1)}, bf16[8,144,128]{2,1,0:T(8,128)(2,1)S(1)}, u32[]{:S(2)}, u32[]{:S(2)}) collective-permute-start(bf16[8,144,128]{2,1,0:T(8,128)(2,1)S(1)} %get-tuple-element.15), channel_id=1, source_target_pairs={{0,2},{1,3},{2,0},{3,1},{4,6},{5,7},{6,4},{7,5},{8,10},{9,11},{10,... | collective-permute-start | bytes 884744 | tf_op jit(solution)/shard_map/ppermute | solution.py:224
  65.5 19.6 %copy-start.5 = (bf16[16,144,128]{2,1,0:T(8,128)(2,1)}, bf16[16,144,128]{2,1,0:T(8,128)(2,1)S(1)}, u32[]{:S(2)}) copy-start(bf16[16,144,128]{2,1,0:T(8,128)(2,1)S(1)} %constant_dynamic-update-slice_fusion.16.refs_0_) | copy-start | bytes 1769476
  65.5 19.6 %collective-permute-start.11 = (bf16[16,144,128]{2,1,0:T(8,128)(2,1)S(1)}, bf16[16,144,128]{2,1,0:T(8,128)(2,1)}, u32[]{:S(2)}, u32[]{:S(2)}) collective-permute-start(bf16[16,144,128]{2,1,0:T(8,128)(2,1)S(1)} %constant_dynamic-update-slice_fusion.16.refs_0_), channel_id=1, source_target_pairs={{0,1},{1,0},{2,3},{3,2},{4,5},{5,4},{6,7},{7,6},{8,9},{9,8},{10,11... | collective-permute-start | bytes 1769480 | tf_op jit(solution)/shard_map/ppermute | solution.py:224
  67.0 27.7 %collective-permute-start.17 = (bf16[16,144,128]{2,1,0:T(8,128)(2,1)}, bf16[16,144,128]{2,1,0:T(8,128)(2,1)}, u32[]{:S(2)}, u32[]{:S(2)}) collective-permute-start(bf16[16,144,128]{2,1,0:T(8,128)(2,1)} %constant_dynamic-update-slice_fusion.27.refs_0_), channel_id=1, source_target_pairs={{0,1},{1,0},{2,3},{3,2},{4,5},{5,4},{6,7},{7,6},{8,9},{9,8},{10,11... | collective-permute-start | bytes 1769480 | tf_op jit(solution)/shard_map/ppermute | solution.py:224
  74.1 30.2 %copy-start.4 = (bf16[16,144,128]{2,1,0:T(8,128)(2,1)}, bf16[16,144,128]{2,1,0:T(8,128)(2,1)S(1)}, u32[]{:S(2)}) copy-start(bf16[16,144,128]{2,1,0:T(8,128)(2,1)S(1)} %constant_dynamic-update-slice_fusion.38.refs_0_) | copy-start | bytes 1769476
  74.1 30.2 %collective-permute-start.23 = (bf16[16,144,128]{2,1,0:T(8,128)(2,1)S(1)}, bf16[16,144,128]{2,1,0:T(8,128)(2,1)S(1)}, u32[]{:S(2)}, u32[]{:S(2)}) collective-permute-start(bf16[16,144,128]{2,1,0:T(8,128)(2,1)S(1)} %constant_dynamic-update-slice_fusion.38.refs_0_), channel_id=1, source_target_pairs={{0,1},{1,0},{2,3},{3,2},{4,5},{5,4},{6,7},{7,6},{8,9},{9,8},{10,11... | collective-permute-start | bytes 1769480 | tf_op jit(solution)/shard_map/ppermute | solution.py:224
  74.7 0.9 copy-start.6
  104.3 0.8 copy-start.7

commit v2 on v1

--- a/solution.py
+++ b/solution.py
@@ -62,117 +62,157 @@
     return mm(one_hot(col == (row % inner) * outer + row // inner), rows).astype(BF16)
 
 
-def prep_kernel(groups, m_ref, present_ref, amino_ref, *outs):
-    chunk_refs, line_ref = outs[:groups], outs[groups]
+def prep_kernel(groups, me_ref, m_ref, present_ref, amino_ref, *refs):
+    keep_refs, send_ref, normed_ref, line_ref, spread_ref = refs[:groups], *refs[groups:]
     lines, width = m_ref.shape
     pairs = width // 128
     stacked = jnp.concatenate([m_ref[:, t * 128 : (t + 1) * 128] for t in range(pairs)], axis=0)
     normed = paired_norm(stacked, 64)
     both = row_shuffle(jnp.concatenate([normed, stacked], axis=1), pairs, lines)
+    normed_ref[...] = both[:, :128]
     line_ref[...] = both[:, 128:]
     kept = (present_ref[...] * amino_ref[...]).astype(F32).astype(BF16)
-    size = lines // groups
+    size = lines // (2 * groups)
     residues = 2 * pairs
-    for g in range(groups):
-        chunk_refs[g][: size * pairs, :] = both[g * size * pairs : (g + 1) * size * pairs, :128]
+    for n in range(2 * groups):
         row, col = iota((128, lines), 0), iota((128, lines), 1)
-        spread = mm(one_hot((row % size == col - g * size) & (row < 2 * size)), kept).astype(BF16)
+        spread = mm(one_hot((row % size == col - n * size) & (row < 2 * size)), kept).astype(BF16)
         row, col = iota((pairs, residues), 0), iota((pairs, residues), 1)
         even = mm_nt(one_hot(col == 2 * row), spread)
         odd = mm_nt(one_hot(col == 2 * row + 1), spread)
-        chunk_refs[g][size * pairs :, :] = jnp.where(
-            iota((pairs, 128), 1) < size, even, odd
-        ).astype(BF16)
+        spread_ref[n] = jnp.where(iota((pairs, 128), 1) < size, even, odd).astype(BF16)
+    core = me_ref[0] % 2
+    rows = size * pairs
+    for g in range(groups):
+        mine, theirs = core * groups + g, (1 - core) * groups + g
+        start = g * (rows + pairs)
+        keep_refs[g][:rows, :] = normed_ref[pl.ds(pl.multiple_of(mine * rows, rows), rows), :]
+        keep_refs[g][rows:, :] = spread_ref[mine]
+        send_ref[start : start + rows, :] = normed_ref[
+            pl.ds(pl.multiple_of(theirs * rows, rows), rows), :
+        ]
+        send_ref[start + rows : start + rows + pairs, :] = spread_ref[theirs]
 
 
 def bias_kernel(x_ref, w_ref, out_ref, acc_ref):
     step = pl.program_id(0)
     heads = w_ref.shape[0]
     per_step, keys, channels = x_ref.shape
-    centring = block_matrix(channels, channels, 1.0 - 1.0 / channels, -1.0 / channels)
-    mean_row = jnp.full((heads, channels), 1.0 / channels, BF16)
-    for n in range(per_step):
-        centre = mm(x_ref[n], centring).astype(BF16)
-        projected = mm_nt(w_ref[...], centre)
-        spread = mm_nt(mean_row, centre * centre)
-        start = pl.multiple_of((step * per_step + n) * heads, heads)
-        acc_ref[pl.ds(start, heads), :] = projected * lax.rsqrt(spread + EPS)
+    centring = block_matrix(2 * channels, channels, 1.0 - 1.0 / channels, -1.0 / channels)
+    averaging = block_matrix(2 * channels, channels, 1.0 / channels, 1.0 / channels)
+    for n in range(0, per_step, 2):
+        centre = mm(jnp.concatenate([x_ref[n], x_ref[n + 1]], axis=1), centring)
+        spread = mm_split(centre * centre, averaging)
+        normed = (centre * lax.rsqrt(spread + EPS)).astype(BF16)
+        for k in range(2):
+            start = pl.multiple_of((step * per_step + n + k) * heads, heads)
+            part = normed[:, k * channels : (k + 1) * channels]
+            acc_ref[pl.ds(start, heads), :] = mm_nt(w_ref[...], part)
 
     @pl.when(step == pl.num_programs(0) - 1)
     def _():
         out_ref[...] = acc_ref[...].astype(BF16)
 
 
-def order_kernel(residues, index_of, me_ref, bias_ref, out_ref):
-    keys = bias_ref.shape[1]
+def order_kernel(residues, device_of, me_ref, own_ref, peer_ref, out_ref):
+    rows, keys = own_ref.shape
     lane = iota((1, keys), 1)
     half = keys // 2
     parity, rest = lane // half, lane % half
     place, pair = rest // (residues // 2), rest % (residues // 2)
-    target = (index_of(place) ^ me_ref[0]) * residues + 2 * pair + parity
+    target = device_of(place, me_ref[0] % 2) * residues + 2 * pair + parity
     piece = 256
-    total = jnp.zeros(bias_ref.shape, F32)
+    total = jnp.zeros((2 * rows, keys), F32)
     for start in range(0, keys, piece):
         chosen = one_hot(iota((piece, keys), 0) + start == target)
-        total = total + mm(bias_ref[:, start : start + piece], chosen)
+        both = jnp.concatenate(
+            [own_ref[:, start : start + piece], peer_ref[:, start : start + piece]], axis=0
+        )
+        total = total + mm(both, chosen)
     out_ref[...] = total * LOG2E
 
 
-def attend_kernel(heads, pieces, size, pairs, own_ref, wq_ref, wk_ref, wv_ref, bias_ref, *refs):
-    piece_refs, out_ref, mask_ref, query_ref = refs[: len(pieces)], refs[-3], refs[-2], refs[-1]
+def attend_kernel(
+    heads, size, pairs, own_ref, peer_ref, wq_ref, wk_ref, wv_ref, wg_ref, bias_ref, keyed_ref,
+    mine_ref, theirs_ref, mask_ref, query_ref, attended_ref,
+):
     depth = 128 // (2 * heads)
     rows = pairs * 2 * heads
-    order = sorted(
-        (place, n, k) for n, places in enumerate(pieces) for k, place in enumerate(places)
-    )
-    keys = len(order) * pairs
+    chips = keyed_ref.shape[0]
+    lead = size * pairs
+    stride = lead + pairs
+    places = [(chip, half * stride) for chip in range(chips) for half in range(2)]
+    keys = len(places) * pairs
     present = jnp.concatenate(
-        [piece_refs[n][k, size * pairs :, :] for _, n, k in order], axis=0
+        [keyed_ref[n, at + lead : at + stride, :] for n, at in places], axis=0
     )
     identity = one_hot(iota((2 * size, 128), 0) == iota((2 * size, 128), 1))
     mask_ref[...] = (1e9 * LOG2E) * (mm_nt(identity, present) - 1.0)
-    query = mm(own_ref[: size * pairs, :], wq_ref[...]) * (depth**-0.5)
-    query_ref[...] = query.astype(BF16).astype(F32)
+    for n, ref in enumerate((own_ref, peer_ref)):
+        query = mm(ref[:lead, :], wq_ref[...]) * (depth**-0.5)
+        query_ref[n] = query.astype(BF16).astype(F32)
     lane, row = iota((2 * heads, 128), 1), iota((2 * heads, 128), 0)
     own_head = jnp.where(lane // depth == row, 1.0, 0.0)[None]
-    low_lanes = iota((rows, 128), 1) < 64
+    low_lanes = iota((keys, 128), 1) < 64
+    ones = jnp.ones((keys, 128), BF16)
 
     def one_line(s, carry):
-        q = query_ref[pl.ds(pl.multiple_of(s * pairs, pairs), pairs), :]
-        spread = (q[:, None, :] * own_head).reshape(rows, 128).astype(BF16)
-        folded = (mm(spread, wk_ref[...]) * LOG2E).astype(BF16)
         start = pl.multiple_of(s * pairs, pairs)
         keyed = jnp.concatenate(
-            [piece_refs[n][k, pl.ds(start, pairs), :] for _, n, k in order], axis=0
+            [keyed_ref[n, pl.ds(at + start, pairs), :] for n, at in places], axis=0
         )
-        logits = [
-            mm_nt(folded[:, 128 * p : 128 * (p + 1)], keyed)
-            + bias_ref[:, p * keys : (p + 1) * keys]
-            + mask_ref[pl.ds(p * size + s, 1), :]
-            for p in range(2)
+        zero = jnp.zeros_like(keyed)
+        valued = [
+            jnp.concatenate([jnp.where(low_lanes, keyed, zero), ones], axis=1),
+            jnp.concatenate([jnp.where(low_lanes, zero, keyed), ones], axis=1),
         ]
-        peak = jnp.max(jnp.maximum(logits[0], logits[1]), axis=-1, keepdims=True)
-        exped = [jnp.exp2(part - peak) for part in logits]
-        total = jnp.sum(exped[0] + exped[1], axis=-1, keepdims=True)
-        summed = [mm(part.astype(BF16), keyed) for part in exped]
-        mean = (jnp.where(low_lanes, summed[0], summed[1]) / total).astype(BF16)
-        valued = mm(mean, wv_ref[...]).reshape(pairs, 2 * heads, 128)
-        out_ref[pl.ds(start, pairs), :] = jnp.sum(valued * own_head, axis=1)
+        masks = [mask_ref[pl.ds(p * size + s, 1), :] for p in range(2)]
+
+        def logits_of(n):
+            q = query_ref[n, pl.ds(start, pairs), :]
+            spread = (q[:, None, :] * own_head).reshape(rows, 128).astype(BF16)
+            folded = (mm(spread, wk_ref[...]) * LOG2E).astype(BF16)
+            return [
+                mm_nt(folded[:, 128 * p : 128 * (p + 1)], keyed)
+                + bias_ref[n * rows : (n + 1) * rows, p * keys : (p + 1) * keys]
+                + masks[p]
+                for p in range(2)
+            ]
+
+        def finish(n, logits):
+            peak = jnp.max(jnp.maximum(logits[0], logits[1]), axis=-1, keepdims=True)
+            exped = [jnp.exp2(part - peak).astype(BF16) for part in logits]
+            summed = mm(exped[0], valued[0]) + mm(exped[1], valued[1])
+            mean = (summed[:, :128] / summed[:, 128:]).astype(BF16)
+            mixed = mm(mean, wv_ref[...]).reshape(pairs, 2 * heads, 128)
+            attended_ref[n, pl.ds(start, pairs), :] = jnp.sum(mixed * own_head, axis=1)
+
+        first = logits_of(0)
+        second = logits_of(1)
+        finish(0, first)
+        finish(1, second)
         return carry
 
-    lax.fori_loop(0, size, one_line, 0)
+    lax.fori_loop(0, size, one_line, 0, unroll=2)
+    for n, (ref, out_ref) in enumerate(((own_ref, mine_ref), (peer_ref, theirs_ref))):
+        gate = jax.nn.sigmoid(mm(ref[:lead, :], wg_ref[...]))
+        out_ref[...] = (gate * attended_ref[n]).astype(BF16)
 
 
 def final_kernel(
-    lines, with_column, normed_refs, line_ref, attended_refs, present_ref, amino_ref, weights, out_ref
+    lines, groups, with_column, me_ref, line_ref, present_ref, amino_ref, wo, wc, wout, *refs
 ):
-    wg, wo, wc, wout = weights
+    mine_refs, theirs_refs = refs[:groups], refs[groups : 2 * groups]
+    out_ref, gated_ref = refs[-2:]
     total = line_ref.shape[0]
     pairs = total // lines
-    normed = jnp.concatenate([r[: total // len(normed_refs), :] for r in normed_refs], axis=0)
-    attended = jnp.concatenate([r[...] for r in attended_refs], axis=0)
-    gated = (jax.nn.sigmoid(mm(normed, wg[...])) * attended).astype(BF16)
-    row = (line_ref[...].astype(F32) + mm(gated, wo[...])).astype(BF16)
+    core = me_ref[0] % 2
+    share = total // (2 * groups)
+    for g in range(groups):
+        for owner, ref in ((core, mine_refs[g]), (1 - core, theirs_refs[g])):
+            at = pl.multiple_of((owner * groups + g) * share, share)
+            gated_ref[pl.ds(at, share), :] = ref[...]
+    row = (line_ref[...].astype(F32) + mm(gated_ref[...], wo[...])).astype(BF16)
     if not with_column:
         out_ref[...] = row
         return
@@ -222,6 +262,17 @@
 
 def exchange(x, flip, devices):
     return lax.ppermute(x, "res", [(d, d ^ flip) for d in range(devices)])
+
+
+def ring_path(chips):
+    if chips != 16:
+        return list(range(chips))
+    columns = [0, 1, 3, 2]
+    path = []
+    for n, column in enumerate(columns):
+        heights = range(4) if n % 2 == 0 else range(3, -1, -1)
+        path += [4 * z + column for z in heights]
+    return path
 
 
 def layer_normalize(values_in):
@@ -268,32 +319,42 @@
     hidden = horizontal_exit_matrix.shape[0]
     heads = offset_matrix.shape[1]
     depth = hidden // heads
-    groups = 4
-    size = lines // groups
-    chunk_rows = size * pairs + pairs
+    groups = 2
+    size = lines // (2 * groups)
+    lead = size * pairs
     keys = res_size * residues
     rows = residues * heads
+    chips = res_size // 2
     amino_row = amino.reshape(1, residues)
+    me = lax.axis_index("res").astype(jnp.int32).reshape(1)
+    smem = pl.BlockSpec(memory_space=pltpu.SMEM)
+    vmem = pl.BlockSpec(memory_space=pltpu.VMEM)
 
     prepared = call(
         functools.partial(prep_kernel, groups),
-        [shape(chunk_rows, 128)] * groups + [shape(lines * pairs, 128)],
+        [shape(lead + pairs, 128)] * groups
+        + [shape(groups * (lead + pairs), 128)]
+        + [shape(lines * pairs, 128)] * 2,
+        me,
         extra_activations,
         present,
         amino_row,
-    )
-    chunks, line = prepared[:groups], prepared[groups]
-
-    gathered = []
-    core, near, far, high = 1, 2, 4, 8
-    for g, chunk in enumerate(chunks):
-        first, second = (near, far) if g % 2 == 0 else (far, near)
-        column = jnp.stack([chunk] + [exchange(chunk, high * k, res_size) for k in range(1, 4)])
-        plane = jnp.concatenate([column, exchange(column, first, res_size)])
-        other = exchange(plane, second, res_size)
-        whole = jnp.concatenate([plane, other])
-        mirrored = exchange(whole, core, res_size)
-        gathered.append((whole, mirrored))
+        in_specs=[smem, vmem, vmem, vmem],
+        scratch_shapes=[pltpu.VMEM((2 * groups, pairs, 128), BF16)],
+    )
+    keeps, send, line = prepared[:groups], prepared[groups], prepared[groups + 2]
+
+    received = exchange(send, 1, res_size).reshape(groups, lead + pairs, 128)
+    path = ring_path(chips)
+    rings = [[2 * c for c in path], [2 * c + 1 for c in reversed(path)]]
+    gathered = [
+        lax.all_gather(
+            jnp.concatenate([keeps[g], received[g]], axis=0),
+            "res",
+            axis_index_groups=rings,
+        )
+        for g in range(groups)
+    ]
 
     per_step = 4
     bias = call(
@@ -313,18 +374,22 @@
     if seq_size > 1:
         bias = lax.all_gather(bias, "seq", axis=1, tiled=True)
 
-    def index_of(place):
-        return (place % 4) * 8 + (place // 8 % 2) * 4 + (place // 4 % 2) * 2 + place // 16
-
-    me = lax.axis_index("res").astype(jnp.int32).reshape(1)
-    vmem = pl.BlockSpec(memory_space=pltpu.VMEM)
+    def device_of(place, core):
+        at = place // 2
+        at = jnp.where(core == 0, at, chips - 1 - at)
+        chip = jnp.zeros_like(at)
+        for n, c in enumerate(path):
+            chip = jnp.where(at == n, c, chip)
+        return 2 * chip + (place % 2 + core) % 2
+
     bias = call(
-        functools.partial(order_kernel, residues, index_of),
-        shape(rows, keys, dtype=F32),
+        functools.partial(order_kernel, residues, device_of),
+        shape(2 * rows, keys, dtype=F32),
         me,
         bias,
-        in_specs=[pl.BlockSpec(memory_space=pltpu.SMEM), vmem],
-        flops=2 * rows * keys * keys,
+        exchange(bias, 1, res_size),
+        in_specs=[smem, vmem, vmem],
+        flops=4 * rows * keys * keys,
     )
 
     w_query, w_key, w_value, w_gate = [
@@ -334,34 +399,30 @@
     empty = jnp.zeros_like(folded)
     wk = jnp.concatenate([folded, empty, empty, folded], axis=1)
     wv = jnp.tile(w_value, (2, 2))
-    wq = twice(w_query)
-
-    attended = []
-    for g, (whole, mirrored) in enumerate(gathered):
-        half = whole.shape[0]
-        if g % 2 == 0:
-            places = list(range(half))
-        else:
-            places = [(n // 4 % 2) * 8 + (n // 8) * 4 + n % 4 for n in range(half)]
-        pieces = (tuple(places), tuple(p + half for p in places))
-        attended.append(
-            call(
-                functools.partial(attend_kernel, heads, pieces, size, pairs),
-                shape(size * pairs, 128, dtype=F32),
-                chunks[g],
-                wq,
-                wk,
-                wv,
-                bias,
-                whole,
-                mirrored,
-                scratch_shapes=[
-                    pltpu.VMEM((2 * size, keys // 2), F32),
-                    pltpu.VMEM((size * pairs, 128), F32),
-                ],
-                flops=size * rows * keys * 2 * 256 * 2,
-            )
+    wq, wg = twice(w_query), twice(w_gate)
+
+    attended = [
+        call(
+            functools.partial(attend_kernel, heads, size, pairs),
+            [shape(lead, 128)] * 2,
+            keeps[g],
+            received[g],
+            wq,
+            wk,
+            wv,
+            wg,
+            bias,
+            gathered[g],
+            scratch_shapes=[
+                pltpu.VMEM((2 * size, keys // 2), F32),
+                pltpu.VMEM((2, lead, 128), F32),
+                pltpu.VMEM((2, lead, 128), F32),
+            ],
+            flops=2 * size * rows * keys * 2 * 256 * 2,
         )
+        for g in range(groups)
+    ]
+    returned = [exchange(theirs, 1, res_size) for _, theirs in attended]
 
     w_column = [
         vertical_matrix[:, :hidden],
@@ -369,29 +430,24 @@
         jnp.tile(vertical_matrix[:, 2 * hidden : 2 * hidden + depth], (1, heads)),
         jnp.tile(vertical_matrix[:, 2 * hidden + depth :], (1, heads)),
     ]
-    weights = (
-        twice(w_gate),
+    with_column = seq_size == 1
+    final_args = [
+        me,
+        line,
+        present,
+        amino_row,
         twice(horizontal_exit_matrix),
         jnp.concatenate([twice(w) for w in w_column], axis=1),
         twice(vertical_exit_matrix),
-    )
-    with_column = seq_size == 1
-
-    def finish(*refs):
-        final_kernel(
-            lines,
-            with_column,
-            refs[:groups],
-            refs[groups],
-            refs[groups + 1 : 2 * groups + 1],
-            refs[2 * groups + 1],
-            refs[2 * groups + 2],
-            refs[2 * groups + 3 : 2 * groups + 7],
-            refs[-1],
-        )
-
-    out_shape = shape(*extra_activations.shape) if with_column else shape(lines * pairs, 128)
-    result = call(finish, out_shape, *chunks, line, *attended, present, amino_row, *weights)
+    ]
+    final_args += [mine for mine, _ in attended] + returned
+    result = call(
+        functools.partial(final_kernel, lines, groups, with_column),
+        shape(*extra_activations.shape) if with_column else shape(lines * pairs, 128),
+        *final_args,
+        in_specs=[smem] + [vmem] * (len(final_args) - 1),
+        scratch_shapes=[pltpu.VMEM((lines * pairs, 128), BF16)],
+    )
     if with_column:
         return result
     row = result.reshape(lines, residues, hidden)

time: 119 us -> 152 us (1.28)
  waiting for transfers between devices: 6.63 us -> 67.3 us
  starting transfers between devices: 30.4 us -> 1.38 us
  between operations: 0.25 us -> 13.5 us
  local copies, waits for them, and re-layouts: 17.7 us -> 6.16 us
  Pallas kernels: 60.6 us -> 58.1 us
  other arithmetic: 2.7 us -> 4.73 us
    all_gather x0 -> x2, waiting for transfers between devices: none -> 66.1 us  [on_device(): lax.all_gather(jnp.concatenate([keeps[g], received[g]], axis=0), 'res', a...]
    ppermute x24 -> x4, starting transfers between devices: 30.4 us -> 1.33 us  [exchange(): return lax.ppermute(x, 'res', [(d, d ^ flip) for d in range(devices)])]
    unnamed x31 -> x21, local copies, waits for them, and re-layouts: 8.45 us -> 1.58 us
    ppermute x24 -> x4, waiting for transfers between devices: 6.63 us -> 1.13 us  [exchange(): return lax.ppermute(x, 'res', [(d, d ^ flip) for d in range(devices)])]
    concatenate x8 -> x0, local copies, waits for them, and re-layouts: 3.08 us -> none  [the longest x4 1.56 us: on_device(): whole = jnp.concatenate([plane, other])]
    concatenate x0 -> x2, other arithmetic: none -> 2.85 us  [on_device(): jnp.concatenate([keeps[g], received[g]], axis=0)]
    pallas_call x8 -> x6, Pallas kernels: 60.6 us -> 58.1 us  [call(): pl.pallas_call(kernel, out_shape=out_shape, compiler_params=limit, cost_e...]
  transfers between devices with their start and end apart: 24 -> 6, of which waited for: 4 -> 3; matrix products, arithmetic and copies ran while one was open for 16% -> 5% of each run, Pallas kernels for 38% -> 25%
where the time goes in v2:
time: 152 us; the launch traced here: 151 us
  waiting for transfers between devices  67.3 us (44%)
  Pallas kernels  58.1 us (38%)
  between operations  13.5 us (9%)
  local copies, waits for them, and re-layouts  6.16 us (4%)
  other arithmetic  4.73 us (3%)
    all_gather x2, waiting for transfers between devices, on_device(): lax.all_gather(jnp.concatenate([keeps[g], received[g]], axis=0), 'res', a...  66.1 us
    pallas_call x6, Pallas kernels, call(): pl.pallas_call(kernel, out_shape=out_shape, compiler_params=limit, cost_e...  58.1 us
    mul x8, local copies, waits for them, and re-layouts, twice(): return jnp.kron(jnp.eye(2, dtype=matrix.dtype), matrix)  3.22 us
  transfers between devices with their start and end apart: 6, of which 3 were waited for; matrix products, arithmetic and copies ran while one was open for 5% of the time, Pallas kernels for 25%

profile of v2, /device:TPU:0, one launch (start us, length us, event | category | flops | bytes accessed | tf_op | source)
XLA Modules:
  0.0 151.2 jit_solution(15386742364169788727)
XLA Ops:
  6.5 2.8 %shard_map.91 = (bf16[144,128]{1,0:T(8,128)(2,1)}, bf16[144,128]{1,0:T(8,128)(2,1)}, bf16[288,128]{1,0:T(8,128)(2,1)}, bf16[512,128]{1,0:T(8,128)(2,1)}, bf16[512,128]{1,0:T(8,128)(2,1)}) custom-call(s32[1]{0:T(128)} %bitcast.me_ref, bf16[32,2048]{1,0:T(8,128)(2,1)} %m_ref.1, s32[32,32]{1,0:T(8,128)} %present_ref.3, s32[1,32]{1,0:T(1,128)} %bitcast.12), custom_call_target="tpu_custom_call" | custom-call | bytes 135300 | tf_op jit(solution)/shard_map/pallas_call | solution.py:250
  9.3 0.5 collective-permute-start
  9.8 1.1 collective-permute-done
  10.9 1.4 pad_maximum_fusion.1
  12.4 1.4 pad_maximum_fusion.2
  13.9 18.5 %shard_map.92.own_ref = bf16[256,1024]{1,0:T(8,128)(2,1)} custom-call(bf16[32,1024,128]{2,1,0:T(8,128)(2,1)} %x_ref.1, bf16[8,128]{1,0:T(8,128)(2,1)} %bitcast.11), custom_call_target="tpu_custom_call" | custom-call | flops 2147483648 | bytes 8390656 | tf_op jit(solution)/shard_map/pallas_call | solution.py:250
  32.5 0.4 collective-permute-start.1
  33.0 0.1 copy.12
  33.2 0.1 copy.14
  33.3 0.1 fusion.1
  33.4 0.5 broadcast_multiply_fusion
  33.9 0.1 mul.158
  34.0 0.1 mul.155
  34.1 0.1 mul.152
  34.2 0.1 mul.149
  34.3 0.7 mul.164.wq_ref
  35.0 0.1 copy.16
  35.2 0.7 tile.32.wv_ref
  35.9 0.7 mul.167.wg_ref
  36.7 0.7 maximum_maximum_fusion.wk_ref
  37.4 0.8 copy-done.8
  38.2 3.9 %shard_map.93.bias_ref = f32[512,1024]{1,0:T(8,128)} custom-call(s32[1]{0:T(128)} %bitcast.me_ref, bf16[256,1024]{1,0:T(8,128)(2,1)} %shard_map.92.own_ref, bf16[256,1024]{1,0:T(8,128)(2,1)} %copy-done.8), custom_call_target="tpu_custom_call" | custom-call | flops 1073741824 | bytes 1048580 | tf_op jit(solution)/shard_map/pallas_call | solution.py:250
  42.1 27.1 %all-gather.5.cloned.1.call-done = bf16[4608,128]{1,0:T(8,128)(2,1)} async-done(((bf16[288,128]{1,0:T(8,128)(2,1)}), bf16[4608,128]{1,0:T(8,128)(2,1)}) %all-gather.5.cloned.1.call-update) | async-done | bytes 1179664 | tf_op jit(solution)/shard_map/all_gather | solution.py:351
  69.1 14.8 %shard_map.94 = (bf16[128,128]{1,0:T(8,128)(2,1)}, bf16[128,128]{1,0:T(8,128)(2,1)}) custom-call(bf16[144,128]{1,0:T(8,128)(2,1)} %get-tuple-element.14.own_ref, bf16[144,128]{1,0:T(8,128)(2,1)} %copy-done.1, bf16[128,128]{1,0:T(8,128)(2,1)} %mul.164.wq_ref, bf16[128,256]{1,0:T(8,128)(2,1)} %maximum_maximum_fusion.wk_ref, bf16[128,128]{1,0:T(8,128)(2,1)} %tile.32.wv_ref, ...), custom_call_target="tpu_custom_call" | custom-call | flops 4294967296 | bytes 3514368 | tf_op jit(solution)/shard_map/pallas_call | solution.py:250
  83.9 39.0 %all-gather.7.cloned.1.call-done = bf16[4608,128]{1,0:T(8,128)(2,1)} async-done(((bf16[288,128]{1,0:T(8,128)(2,1)}), bf16[4608,128]{1,0:T(8,128)(2,1)}) %all-gather.7.cloned.1.call-update) | async-done | bytes 1179664 | tf_op jit(solution)/shard_map/all_gather | solution.py:351
  122.9 14.8 %shard_map.95 = (bf16[128,128]{1,0:T(8,128)(2,1)}, bf16[128,128]{1,0:T(8,128)(2,1)}) custom-call(bf16[144,128]{1,0:T(8,128)(2,1)} %get-tuple-element.17.own_ref, bf16[144,128]{1,0:T(8,128)(2,1)} %copy-done, bf16[128,128]{1,0:T(8,128)(2,1)} %mul.164.wq_ref, bf16[128,256]{1,0:T(8,128)(2,1)} %maximum_maximum_fusion.wk_ref, bf16[128,128]{1,0:T(8,128)(2,1)} %tile.32.wv_ref, ...), custom_call_target="tpu_custom_call" | custom-call | flops 4294967296 | bytes 3514368 | tf_op jit(solution)/shard_map/pallas_call | solution.py:250
  137.7 0.5 collective-permute-start.3
  138.2 0.7 pad_maximum_fusion.wc
  138.9 0.7 mul.146.wo
  139.6 0.7 mul.161.wout
  140.3 0.6 copy-done.4
  141.0 3.4 %shard_map.96 = bf16[32,2048]{1,0:T(8,128)(2,1)} custom-call(s32[1]{0:T(128)} %bitcast.me_ref, bf16[512,128]{1,0:T(8,128)(2,1)} %get-tuple-element.13.line_ref, s32[32,32]{1,0:T(8,128)} %present_ref.3, s32[1,32]{1,0:T(1,128)} %bitcast.13, bf16[128,128]{1,0:T(8,128)(2,1)} %mul.146.wo, bf16[128,512]{1,0:T(8,128)(2,1)} %pad_maximum_fusion.wc, ...), custom_call_target="tpu_custom_call" | custom-call | bytes 462980 | tf_op jit(solution)/shard_map/pallas_call | solution.py:250
  (36 shorter events, 0.5 us)
Async XLA Ops:
  6.5 62.6 %all-gather.5.cloned.1.call-start = ((), (), s32[]{:S(2)}) async-start(), calls=%async_computation | async-start | bytes 1253376 | tf_op jit(solution)/shard_map/all_gather | solution.py:351
  9.3 1.6 %collective-permute-start = (bf16[288,128]{1,0:T(8,128)(2,1)}, bf16[288,128]{1,0:T(8,128)(2,1)S(1)}, u32[]{:S(2)}, u32[]{:S(2)}) collective-permute-start(bf16[288,128]{1,0:T(8,128)(2,1)} %get-tuple-element.15), channel_id=1, source_target_pairs={{0,1},{1,0},{2,3},{3,2},{4,5},{5,4},{6,7},{7,6},{8,9},{9,8},{10,11... | collective-permute-start | bytes 221192 | tf_op jit(solution)/shard_map/ppermute | solution.py:264
  10.9 21.5 %copy-start = (bf16[144,128]{1,0:T(8,128)(2,1)}, bf16[144,128]{1,0:T(8,128)(2,1)S(1)}, u32[]{:S(2)}) copy-start(bf16[144,128]{1,0:T(8,128)(2,1)S(1)} %get-tuple-element.21.peer_ref) | copy-start | bytes 110596
  10.9 21.5 %copy-start.1 = (bf16[144,128]{1,0:T(8,128)(2,1)}, bf16[144,128]{1,0:T(8,128)(2,1)S(1)}, u32[]{:S(2)}) copy-start(bf16[144,128]{1,0:T(8,128)(2,1)S(1)} %get-tuple-element.22.peer_ref) | copy-start | bytes 110596
  12.4 110.6 %all-gather.7.cloned.1.call-start = ((), (), s32[]{:S(2)}) async-start(), calls=%async_computation.1 | async-start | bytes 1253376 | tf_op jit(solution)/shard_map/all_gather | solution.py:351
  13.9 19.0 %copy-start.3 = (bf16[64,144]{1,0:T(8,128)(2,1)S(1)}, bf16[64,144]{1,0:T(8,128)(2,1)}, u32[]{:S(2)}) copy-start(bf16[64,144]{1,0:T(8,128)(2,1)} %param.16) | copy-start | bytes 55300
  13.9 19.4 %copy-start.2 = (bf16[64,256]{1,0:T(8,128)(2,1)S(1)}, bf16[64,256]{1,0:T(8,128)(2,1)}, u32[]{:S(2)}) copy-start(bf16[64,256]{1,0:T(8,128)(2,1)} %param.14) | copy-start | bytes 98308
  13.9 19.5 %copy-start.6 = (bf16[64,64]{1,0:T(8,128)(2,1)S(1)}, bf16[64,64]{1,0:T(8,128)(2,1)}, u32[]{:S(2)}) copy-start(bf16[64,64]{1,0:T(8,128)(2,1)} %param.17) | copy-start | bytes 24580
  13.9 19.5 %copy-start.7 = (bf16[64,64]{1,0:T(8,128)(2,1)S(1)}, bf16[64,64]{1,0:T(8,128)(2,1)}, u32[]{:S(2)}) copy-start(bf16[64,64]{1,0:T(8,128)(2,1)} %param.15) | copy-start | bytes 24580
  32.5 4.9 %collective-permute-start.1 = (bf16[256,1024]{1,0:T(8,128)(2,1)}, bf16[256,1024]{1,0:T(8,128)(2,1)S(1)}, u32[]{:S(2)}, u32[]{:S(2)}) collective-permute-start(bf16[256,1024]{1,0:T(8,128)(2,1)} %shard_map.92.own_ref), channel_id=1, source_target_pairs={{0,1},{1,0},{2,3},{3,2},{4,5},{5,4},{6,7},{7,6},{8,9},{9,8},{10,11... | collective-permute-start | bytes 1572872 | tf_op jit(solution)/shard_map/ppermute | solution.py:264
  37.4 0.8 copy-start.8
  122.9 14.8 %copy-start.9 = (bf16[128,128]{1,0:T(8,128)(2,1)S(1)}, bf16[128,128]{1,0:T(8,128)(2,1)}, u32[]{:S(2)}) copy-start(bf16[128,128]{1,0:T(8,128)(2,1)} %get-tuple-element.19) | copy-start | bytes 98308
  137.7 2.6 %collective-permute-start.2 = (bf16[128,128]{1,0:T(8,128)(2,1)S(1)}, bf16[128,128]{1,0:T(8,128)(2,1)S(1)}, u32[]{:S(2)}, u32[]{:S(2)}) collective-permute-start(bf16[128,128]{1,0:T(8,128)(2,1)S(1)} %copy-done.9), channel_id=1, source_target_pairs={{0,1},{1,0},{2,3},{3,2},{4,5},{5,4},{6,7},{7,6},{8,9},{9,8},{10,11... | collective-permute-start | bytes 98312 | tf_op jit(solution)/shard_map/ppermute | solution.py:264
  137.7 2.6 %collective-permute-start.3 = (bf16[128,128]{1,0:T(8,128)(2,1)}, bf16[128,128]{1,0:T(8,128)(2,1)S(1)}, u32[]{:S(2)}, u32[]{:S(2)}) collective-permute-start(bf16[128,128]{1,0:T(8,128)(2,1)} %get-tuple-element.20), channel_id=1, source_target_pairs={{0,1},{1,0},{2,3},{3,2},{4,5},{5,4},{6,7},{7,6},{8,9},{9,8},{10,11... | collective-permute-start | bytes 98312 | tf_op jit(solution)/shard_map/ppermute | solution.py:264
  140.3 0.6 copy-start.4
  140.3 0.6 copy-start.5
Sparse Core Ops, SparseCore 0:
  12.5 56.5 all-gather.4
  70.7 52.2 all-gather.6

commit v3 on v2

v3 whole, which is shorter than its diff:
```python
import functools
import math

import jax
import jax.numpy as jnp
from jax import lax
from jax.experimental import pallas as pl
from jax.experimental.pallas import tpu as pltpu
from jax.sharding import PartitionSpec as P

F32 = jnp.float32
BF16 = jnp.bfloat16
LOG2E = math.log2(math.e)
EPS = 1e-05
VMEM_LIMIT = 56 * 1024 * 1024

NT = (((1,), (1,)), ((), ()))


def mm(a, b):
    return jnp.dot(a, b, preferred_element_type=F32)


def mm_nt(a, b):
    return lax.dot_general(a, b, NT, preferred_element_type=F32)


def iota(shape, axis):
    return lax.broadcasted_iota(jnp.int32, shape, axis)


def one_hot(condition):
    return jnp.where(condition, 1.0, 0.0).astype(BF16)


def block_matrix(size, block, on_diagonal, elsewhere):
    row, col = iota((size, size), 0), iota((size, size), 1)
    inside = jnp.where(row == col, on_diagonal, elsewhere)
    return jnp.where(row // block == col // block, inside, 0.0).astype(BF16)


def halves(value):
    high = value.astype(BF16)
    return high, (value - high.astype(F32)).astype(BF16)


def mm_split(value, matrix):
    high, low = halves(value)
    return mm(high, matrix) + mm(low, matrix)


def paired_norm(x, width):
    lanes = x.shape[1]
    centre = mm(x, block_matrix(lanes, width, 1.0 - 1.0 / width, -1.0 / width))
    spread = mm_split(centre * centre, block_matrix(lanes, width, 1.0 / width, 1.0 / width))
    return (centre * lax.rsqrt(spread + EPS)).astype(BF16)


def row_shuffle(rows, inner, outer):
    total = rows.shape[0]
    row, col = iota((total, total), 0), iota((total, total), 1)
    return mm(one_hot(col == (row % inner) * outer + row // inner), rows).astype(BF16)


def prep_kernel(groups, me_ref, m_ref, present_ref, amino_ref, *refs):
    keep_ref, send_ref, line_ref, normed_ref, spread_ref = refs
    lines, width = m_ref.shape
    pairs = width // 128
    stacked = jnp.concatenate([m_ref[:, t * 128 : (t + 1) * 128] for t in range(pairs)], axis=0)
    normed = paired_norm(stacked, 64)
    both = row_shuffle(jnp.concatenate([normed, stacked], axis=1), pairs, lines)
    normed_ref[...] = both[:, :128]
    line_ref[...] = both[:, 128:]
    kept = (present_ref[...] * amino_ref[...]).astype(F32).astype(BF16)
    size = lines // (2 * groups)
    residues = 2 * pairs
    row, col = iota((pairs, residues), 0), iota((pairs, residues), 1)
    evens, odds = one_hot(col == 2 * row), one_hot(col == 2 * row + 1)
    row, col = iota((128, lines), 0) - 64, iota((128, lines), 1)
    for n in range(2 * groups):
        chosen = (row >= 0) & (row < 2 * size) & (row % size == col - n * size)
        spread = mm(one_hot(chosen), kept).astype(BF16)
        first = iota((pairs, 128), 1) < 64 + size
        spread_ref[n] = jnp.where(first, mm_nt(evens, spread), mm_nt(odds, spread)).astype(BF16)
    core = me_ref[0] % 2
    rows = size * pairs
    for ref, half in ((keep_ref, core), (send_ref, 1 - core)):
        for g in range(groups):
            index, start = half * groups + g, g * (rows + pairs)
            ref[start : start + rows, :] = normed_ref[
                pl.ds(pl.multiple_of(index * rows, rows), rows), :
            ]
            ref[start + rows : start + rows + pairs, :] = spread_ref[index]


def bias_kernel(x_ref, w_ref, out_ref, acc_ref):
    step = pl.program_id(0)
    heads = w_ref.shape[1]
    per_step, keys, channels = x_ref.shape
    per_tile = 128 // heads
    steps = per_tile // per_step
    centring = block_matrix(2 * channels, channels, 1.0 - 1.0 / channels, -1.0 / channels)
    averaging = block_matrix(2 * channels, channels, 1.0 / channels, 1.0 / channels)
    lane = iota((channels, 128), 1)
    wide = mm(w_ref[...], one_hot(iota((heads, 128), 1) % heads == iota((heads, 128), 0)))
    placed = []
    for n in range(per_step):
        mine = lane // heads == (step % steps) * per_step + n
        placed.append(jnp.where(mine, wide, 0.0).astype(BF16))
    placed = jnp.concatenate(placed, axis=0)
    tile = step // steps

    @pl.when(step % steps == 0)
    def _():
        acc_ref[tile] = jnp.zeros(acc_ref.shape[1:], F32)

    piece = 128
    for r in range(0, keys, piece):
        normed = []
        for n in range(0, per_step, 2):
            x = jnp.concatenate([x_ref[n, r : r + piece], x_ref[n + 1, r : r + piece]], axis=1)
            centre = mm(x, centring)
            spread = mm_split(centre * centre, averaging)
            normed.append((centre * lax.rsqrt(spread + EPS)).astype(BF16))
        acc_ref[tile, r : r + piece, :] += mm(jnp.concatenate(normed, axis=1), placed)

    @pl.when(step == pl.num_programs(0) - 1)
    def _():
        for n in range(acc_ref.shape[0]):
            out_ref[n * 128 : (n + 1) * 128, :] = acc_ref[n].T.astype(BF16)


def order_kernel(
    groups, size, pairs, heads, pieces, me_ref, own_ref, peer_ref, keep_ref, received_ref, w_ref,
    bias_ref, lhs_ref,
):
    rows, keys = own_ref.shape
    residues = 2 * pairs
    lane = iota((1, keys), 1)
    each = keys // pieces
    which, rest = lane // each, lane % each
    parity, rest = rest // (each // 2), rest % (each // 2)
    place, pair = rest // pairs, rest % pairs
    device = me_ref[0] ^ ((place % 2) + 2 * which + 2 * pieces * (place // 2))
    target = device * residues + 2 * pair + parity
    total = jnp.zeros((2 * rows, keys), F32)
    for start in range(0, keys, 256):
        chosen = one_hot(iota((256, keys), 0) + start == target)
        both = jnp.concatenate(
            [own_ref[:, start : start + 256], peer_ref[:, start : start + 256]], axis=0
        )
        total = total + mm(both, chosen)
    bias_ref[...] = total * LOG2E

    hidden = w_ref.shape[0]
    depth = hidden // heads
    row, col = iota((128, hidden), 0), iota((128, hidden), 1)
    twice_rows = one_hot(row % hidden == col)
    row, col = iota((4 * hidden, 128), 0), iota((4 * hidden, 128), 1)
    wq = mm(mm(twice_rows, w_ref[...]).astype(BF16), one_hot(row == col % hidden))
    row, col = iota((128, 128), 0), iota((128, 128), 1)
    wq = jnp.where(row // hidden == col // hidden, wq, 0.0).astype(BF16)
    row, col = iota((128, 4 * hidden), 0), iota((128, 4 * hidden), 1)
    wk = mm_nt(one_hot(col == hidden + row % hidden), w_ref[...]).astype(BF16)
    row, col = iota((hidden, 128), 0), iota((hidden, 128), 1)
    wk = mm(wk, one_hot(row == col)).astype(BF16)
    lane, row = iota((2 * heads, 128), 1), iota((2 * heads, 128), 0)
    own_head = jnp.where(lane // depth == row, 1.0, 0.0)[None]
    lead = size * pairs
    lane = iota((rows, 128), 1) - hidden
    for g in range(groups):
        for n, ref in enumerate((keep_ref, received_ref)):
            start = g * (lead + pairs)
            query = mm(ref[start : start + lead, :], wq) * (depth**-0.5)
            query = query.astype(BF16).astype(F32)
            for s in range(size):
                q = query[s * pairs : (s + 1) * pairs]
                spread = (q[:, None, :] * own_head).reshape(rows, 128).astype(BF16)
                folded = mm(spread, wk) * LOG2E
                picked = (lane == s) | (lane == size + s)
                lhs_ref[g * size + s, n * rows : (n + 1) * rows, :] = jnp.where(
                    picked, 1.0, folded
                ).astype(BF16)


def masks_of(ref, size, pairs):
    lead = size * pairs
    present = jnp.concatenate(
        [ref[k, c, lead : lead + pairs, :] for k in range(ref.shape[0]) for c in range(2)], axis=0
    ).astype(F32)
    lane = iota(present.shape, 1) - 64
    hidden = (1e9 * LOG2E) * (present - 1.0)
    return [
        jnp.where((lane >= p * size) & (lane < (p + 1) * size), hidden, 0.0).astype(BF16)
        for p in range(2)
    ]


def keys_of(ref, masks, s, pairs):
    start = pl.multiple_of(s * pairs, pairs)
    even = jnp.concatenate(
        [ref[k, c, pl.ds(start, pairs), :] for k in range(ref.shape[0]) for c in range(2)], axis=0
    )
    odd = pltpu.roll(even.astype(F32), 64, 1).astype(BF16)
    low = iota(even.shape, 1) < 64
    one = jnp.ones_like(even)
    keyed = [jnp.where(low, x, m) for x, m in zip((even, odd), masks)]
    valued = [jnp.where(low, x, one) for x in (even, odd)]
    return jnp.concatenate(keyed, axis=0), jnp.concatenate(valued, axis=0)


def partial_sums(lhs, bias_ref, piece, keyed, valued):
    width = keyed.shape[0]
    logits = mm_nt(lhs, keyed) + bias_ref[:, piece * width : (piece + 1) * width]
    return mm(jnp.exp2(logits).astype(BF16), valued)


def start_kernel(groups, size, pairs, places, lhs_ref, bias_ref, *refs):
    out_ref = refs[-1]
    piece_refs = [refs[n * groups : (n + 1) * groups] for n in range(len(places))]
    masks = [[masks_of(ref, size, pairs) for ref in piece] for piece in piece_refs]

    def one_line(s, carry):
        for g in range(groups):
            line = g * size + s
            total = None
            for n, place in enumerate(places):
                keyed, valued = keys_of(piece_refs[n][g], masks[n][g], s, pairs)
                part = partial_sums(lhs_ref[line], bias_ref, place, keyed, valued)
                total = part if total is None else total + part
            out_ref[line] = total
        return carry

    lax.fori_loop(0, size, one_line, 0, unroll=2)


def finish_kernel(
    heads, groups, size, pairs, place, lhs_ref, bias_ref, sums_ref, w_ref, keep_ref, received_ref,
    *refs,
):
    piece_refs, far_refs = refs[:groups], refs[groups : 4 * groups]
    mine_ref, theirs_ref, attended_ref, range_ref, copy_ref = refs[4 * groups :]
    hidden = w_ref.shape[0]
    depth = hidden // heads
    lead = size * pairs
    row, col = iota((4 * hidden, 128), 0), iota((4 * hidden, 128), 1)
    pick_value = one_hot(row == 2 * hidden + col % hidden)
    pick_gate = one_hot(row == 3 * hidden + col % hidden)
    row, col = iota((128, hidden), 0), iota((128, hidden), 1)
    wv = mm(mm(one_hot(row == col), w_ref[...]).astype(BF16), pick_value).astype(BF16)
    wg = mm(mm(one_hot(row % hidden == col), w_ref[...]).astype(BF16), pick_gate)
    row, col = iota((128, 128), 0), iota((128, 128), 1)
    wg = jnp.where(row // hidden == col // hidden, wg, 0.0).astype(BF16)
    lane, row = iota((2 * heads, 128), 1), iota((2 * heads, 128), 0)
    own_head = jnp.where(lane // depth == row, 1.0, 0.0)[None]
    masks = [masks_of(ref, size, pairs) for ref in piece_refs]
    low = iota((lhs_ref.shape[1], 128), 1) < 64

    def settle(line, total):
        mean = jnp.where(low, total / pltpu.roll(total, 64, 1), 0.0).astype(BF16)
        mixed = mm(mean, wv).reshape(2 * pairs, 2 * heads, 128)
        summed = jnp.sum(mixed * own_head, axis=1)
        start = pl.multiple_of(line * pairs, pairs)
        for n in range(2):
            attended_ref[n, pl.ds(start, pairs), :] = summed[n * pairs : (n + 1) * pairs]

    range_ref[...] = jnp.ones(range_ref.shape, F32)

    def one_line(s, carry):
        for g in range(groups):
            line = g * size + s
            keyed, valued = keys_of(piece_refs[g], masks[g], s, pairs)
            total = sums_ref[line] + partial_sums(lhs_ref[line], bias_ref, place, keyed, valued)
            settle(line, total)
            weight = jnp.where(low, 1.0, total).reshape(-1, 8, 128)
            range_ref[0] = jnp.minimum(range_ref[0], jnp.min(weight, axis=0))
            range_ref[1] = jnp.maximum(range_ref[1], jnp.max(weight, axis=0))
        return carry

    lax.fori_loop(0, size, one_line, 0, unroll=2)
    fine = (range_ref[0] > 2.0**-80) & (range_ref[1] < 2.0**100)

    @pl.when(jnp.min(jnp.where(fine, 1.0, 0.0)) < 0.5)
    def _():
        for n, ref in enumerate(far_refs):
            pltpu.sync_copy(ref, copy_ref.at[n])
        for g in range(groups):
            ordered = [copy_ref.at[n * groups + g] for n in range(3)] + [piece_refs[g]]
            all_masks = [masks_of(ref, size, pairs) for ref in ordered]

            def exact_line(s, carry):
                line = g * size + s
                both = [keys_of(r, m, s, pairs) for r, m in zip(ordered, all_masks)]
                logits = []
                for n, (keyed, _) in enumerate(both):
                    width = keyed.shape[0]
                    bias = bias_ref[:, n * width : (n + 1) * width]
                    logits.append(mm_nt(lhs_ref[line], keyed) + bias)
                peak = functools.reduce(jnp.maximum, logits)
                peak = jnp.max(peak, axis=-1, keepdims=True)
                parts = [
                    mm(jnp.exp2(part - peak).astype(BF16), valued)
                    for part, (_, valued) in zip(logits, both)
                ]
                settle(line, sum(parts[1:], parts[0]))
                return carry

            lax.fori_loop(0, size, exact_line, 0)

    for n, (ref, out_ref) in enumerate(((keep_ref, mine_ref), (received_ref, theirs_ref))):
        for g in range(groups):
            start = g * (lead + pairs)
            gate = jax.nn.sigmoid(mm(ref[start : start + lead, :], wg))
            at = slice(g * lead, (g + 1) * lead)
            out_ref[at, :] = (gate * attended_ref[n, at, :]).astype(BF16)


def final_kernel(
    lines, with_column, me_ref, line_ref, present_ref, amino_ref, wo, wc, wout, mine_ref,
    theirs_ref, out_ref, gated_ref,
):
    total = line_ref.shape[0]
    pairs = total // lines
    core = me_ref[0] % 2
    share = total // 2
    for owner, ref in ((core, mine_ref), (1 - core, theirs_ref)):
        gated_ref[pl.ds(pl.multiple_of(owner * share, share), share), :] = ref[...]
    row = (line_ref[...].astype(F32) + mm(gated_ref[...], wo[...])).astype(BF16)
    if not with_column:
        out_ref[...] = row
        return
    kept_small = (present_ref[...] * amino_ref[...]).astype(F32).astype(BF16)
    spread = mm(one_hot(iota((total, lines), 0) // pairs == iota((total, lines), 1)), kept_small)
    own = iota((total, 2 * pairs), 1) // 2 == iota((total, 2 * pairs), 0) % pairs
    sides = one_hot(iota((2 * pairs, 128), 0) % 2 == iota((2 * pairs, 128), 1) // 64)
    kept = mm(jnp.where(own, spread, 0.0).astype(BF16), sides)

    projected = mm(paired_norm(row, 64), wc[...])
    query, gate, key, value = [projected[:, 128 * n : 128 * (n + 1)] for n in range(4)]

    def grid(a):
        return a.reshape(lines, pairs, 128)

    count = jnp.maximum(jnp.sum(grid(kept), axis=0), 1.0)
    mean_query = jnp.sum(grid(kept * query), axis=0) / count * (8**-0.5)
    same_head = block_matrix(128, 8, 1.0, 1.0)
    product = (mean_query[None] * grid(key)).reshape(total, 128)
    logits = grid(mm_split(product, same_head) + 1e9 * (kept - 1.0))
    exped = jnp.exp(logits - jnp.max(logits, axis=0, keepdims=True))
    mixed = jnp.sum(exped * grid(value), axis=0) / jnp.sum(exped, axis=0)
    gated = (jax.nn.sigmoid(grid(gate)) * mixed[None]).reshape(total, 128).astype(BF16)
    result = (row.astype(F32) + mm(gated, wout[...])).astype(BF16)
    shuffled = row_shuffle(result, lines, pairs)
    for t in range(pairs):
        out_ref[:, t * 128 : (t + 1) * 128] = shuffled[t * lines : (t + 1) * lines, :]


def call(kernel, out_shape, *args, **options):
    flops = options.pop("flops", 0)
    limit = pltpu.CompilerParams(vmem_limit_bytes=VMEM_LIMIT)
    moved = sum(a.size * a.dtype.itemsize for a in args)
    cost = pl.CostEstimate(flops=flops, bytes_accessed=moved, transcendentals=0)
    return pl.pallas_call(
        kernel, out_shape=out_shape, compiler_params=limit, cost_estimate=cost, **options
    )(*args)


def shape(*dims, dtype=BF16):
    return jax.ShapeDtypeStruct(dims, dtype)


def twice(matrix):
    return jnp.kron(jnp.eye(2, dtype=matrix.dtype), matrix)


def exchange(x, flip, devices):
    return lax.ppermute(x, "res", [(d, d ^ flip) for d in range(devices)])


def layer_normalize(values_in):
    centre = values_in - jnp.mean(values_in, axis=-1, keepdims=True)
    spread = jnp.mean(centre * centre, axis=-1, keepdims=True)
    return centre * lax.rsqrt(spread + EPS)


def column_complete(line, kept, vertical_matrix, vertical_exit_matrix, heads, depth):
    lines, columns, features = line.shape
    hidden = heads * depth
    normed = layer_normalize(line.astype(F32)).astype(BF16)
    projected = mm(normed.reshape(-1, features), vertical_matrix).reshape(lines, columns, -1)
    query, gate = projected[..., :hidden], projected[..., hidden : 2 * hidden]
    key = projected[..., 2 * hidden : 2 * hidden + depth]
    value = projected[..., 2 * hidden + depth :]
    count = jnp.maximum(jnp.sum(kept, axis=0), 1.0)[:, None]
    mean_query = jnp.sum(kept[..., None] * query, axis=0) / count * depth**-0.5
    logits = jnp.einsum("ihc,sic->sih", mean_query.reshape(columns, heads, depth), key)
    logits = logits + 1e9 * (kept - 1.0)[..., None]
    exped = jnp.exp(logits - jnp.max(logits, axis=0, keepdims=True))
    mixed = jnp.einsum("sih,sic->ihc", exped, value) / jnp.sum(exped, axis=0)[..., None]
    gate = jax.nn.sigmoid(gate).reshape(lines, columns, heads, depth)
    gated = (gate * mixed[None]).reshape(-1, hidden).astype(BF16)
    update = mm(gated, vertical_exit_matrix).reshape(lines, columns, features)
    return (line.astype(F32) + update).astype(BF16)


def on_device(
    seq_size,
    res_size,
    extra_activations,
    pair,
    present,
    amino,
    offset_matrix,
    horizontal_matrix,
    horizontal_exit_matrix,
    vertical_matrix,
    vertical_exit_matrix,
):
    lines, residues = present.shape
    pairs = residues // 2
    hidden = horizontal_exit_matrix.shape[0]
    heads = offset_matrix.shape[1]
    depth = hidden // heads
    groups = 2
    size = lines // (2 * groups)
    lead = size * pairs
    keys = res_size * residues
    rows = residues * heads
    core_bit, near, far, high = 1, 2, 4, 8
    amino_row = amino.reshape(1, residues)
    me = lax.axis_index("res").astype(jnp.int32).reshape(1)
    smem = pl.BlockSpec(memory_space=pltpu.SMEM)
    vmem = pl.BlockSpec(memory_space=pltpu.VMEM)

    rest = lead + pairs
    keep, send, line = call(
        functools.partial(prep_kernel, groups),
        [shape(groups * rest, 128)] * 2 + [shape(lines * pairs, 128)],
        me,
        extra_activations,
        present,
        amino_row,
        in_specs=[smem, vmem, vmem, vmem],
        scratch_shapes=[
            pltpu.VMEM((lines * pairs, 128), BF16),
            pltpu.VMEM((2 * groups, pairs, 128), BF16),
        ],
    )

    received = exchange(send, core_bit, res_size)
    chunk = jnp.concatenate([keep, received], axis=0)
    levels = [chunk] + [exchange(chunk, high * k, res_size) for k in range(1, res_size // high)]
    column = jnp.stack(levels).reshape(len(levels), 2, groups, rest, 128)
    own = [column[:, :, g] for g in range(groups)]
    beside = [exchange(part, near, res_size) for part in own]
    across = [exchange(part, far, res_size) for part in own]
    corner = [
        exchange(beside[g], far, res_size) if g % 2 == 0 else exchange(across[g], near, res_size)
        for g in range(groups)
    ]

    per_step = 4
    bias = call(
        bias_kernel,
        shape(rows, pair.shape[1]),
        pair,
        offset_matrix,
        grid=(residues // per_step,),
        in_specs=[
            pl.BlockSpec((per_step,) + pair.shape[1:], lambda n: (n, 0, 0)),
            pl.BlockSpec(offset_matrix.shape, lambda n: (0, 0)),
        ],
        out_specs=pl.BlockSpec((rows, pair.shape[1]), lambda n: (0, 0)),
        scratch_shapes=[pltpu.VMEM((rows // 128, pair.shape[1], 128), F32)],
        flops=4 * pair.size * 128,
    )
    if seq_size > 1:
        bias = lax.all_gather(bias, "seq", axis=1, tiled=True)
    pieces = 4
    bias, lhs = call(
        functools.partial(order_kernel, groups, size, pairs, heads, pieces),
        [shape(2 * rows, keys, dtype=F32), shape(groups * size, 2 * rows, 128)],
        me,
        bias,
        exchange(bias, core_bit, res_size),
        keep,
        received,
        horizontal_matrix,
        in_specs=[smem] + [vmem] * 5,
        flops=4 * rows * keys * keys,
    )
    sums = call(
        functools.partial(start_kernel, groups, size, pairs, (0, 1, 2)),
        shape(groups * size, 2 * rows, 128, dtype=F32),
        lhs,
        bias,
        *own,
        *beside,
        *across,
        flops=groups * size * rows * keys * 2 * 256 * 2,
    )
    anywhere = pl.BlockSpec(memory_space=pl.ANY)
    mine, theirs = call(
        functools.partial(finish_kernel, heads, groups, size, pairs, 3),
        [shape(groups * lead, 128)] * 2,
        lhs,
        bias,
        sums,
        horizontal_matrix,
        keep,
        received,
        *corner,
        *own,
        *beside,
        *across,
        in_specs=[vmem] * (6 + groups) + [anywhere] * (3 * groups),
        scratch_shapes=[
            pltpu.VMEM((2, groups * lead, 128), F32),
            pltpu.VMEM((2, 8, 128), F32),
            pltpu.VMEM((3 * groups,) + own[0].shape, BF16),
        ],
        flops=groups * size * rows * keys * 2 * 256,
    )
    returned = exchange(theirs, core_bit, res_size)

    w_column = [
        vertical_matrix[:, :hidden],
        vertical_matrix[:, hidden : 2 * hidden],
        jnp.tile(vertical_matrix[:, 2 * hidden : 2 * hidden + depth], (1, heads)),
        jnp.tile(vertical_matrix[:, 2 * hidden + depth :], (1, heads)),
    ]
    with_column = seq_size == 1
    final_args = [
        me,
        line,
        present,
        amino_row,
        twice(horizontal_exit_matrix),
        jnp.concatenate([twice(w) for w in w_column], axis=1),
        twice(vertical_exit_matrix),
    ]
    final_args += [mine, returned]
    result = call(
        functools.partial(final_kernel, lines, with_column),
        shape(*extra_activations.shape) if with_column else shape(lines * pairs, 128),
        *final_args,
        in_specs=[smem] + [vmem] * (len(final_args) - 1),
        scratch_shapes=[pltpu.VMEM((lines * pairs, 128), BF16)],
    )
    if with_column:
        return result
    row = result.reshape(lines, residues, hidden)
    kept = (present * amino_row).astype(BF16)
    moved = lax.all_to_all(row, "seq", split_axis=1, concat_axis=0, tiled=True)
    moved_kept = lax.all_to_all(kept, "seq", split_axis=1, concat_axis=0, tiled=True)
    updated = column_complete(
        moved, moved_kept.astype(F32), vertical_matrix, vertical_exit_matrix, heads, depth
    )
    back = lax.all_to_all(updated, "seq", split_axis=0, concat_axis=1, tiled=True)
    return back.reshape(extra_activations.shape)


def solution(mesh):
    in_specs = (
        P("seq", "res"),
        P("res", "seq", None),
        P("seq", "res"),
        P("res"),
        P(),
        P(),
        P(),
        P(),
        P(),
    )
    sizes = mesh.shape
    return jax.shard_map(
        functools.partial(on_device, sizes["seq"], sizes["res"]),
        mesh=mesh,
        in_specs=in_specs,
        out_specs=P("seq", "res"),
        check_vma=False,
    )
```

time: 152 us -> 128 us (0.84)
  waiting for transfers between devices: 67.3 us -> 17.3 us
  Pallas kernels: 58.1 us -> 89.2 us
  between operations: 13.5 us -> 0.18 us
  starting transfers between devices: 1.38 us -> 12.4 us
  other arithmetic: 4.73 us -> 1.12 us
    all_gather x2 -> x0, waiting for transfers between devices: 66.1 us -> none  [on_device(): lax.all_gather(jnp.concatenate([keeps[g], received[g]], axis=0), 'res', a...]
    pallas_call x6, Pallas kernels: 58.1 us -> 89.2 us  [call(): pl.pallas_call(kernel, out_shape=out_shape, compiler_params=limit, cost_e...]
    ppermute x4 -> x12, waiting for transfers between devices: 1.13 us -> 17.3 us  [exchange(): return lax.ppermute(x, 'res', [(d, d ^ flip) for d in range(devices)])]
    ppermute x4 -> x12, starting transfers between devices: 1.33 us -> 12.4 us  [exchange(): return lax.ppermute(x, 'res', [(d, d ^ flip) for d in range(devices)])]
    concatenate x3 -> x0, other arithmetic: 3.55 us -> none  [the longest x2 2.85 us: on_device(): jnp.concatenate([keeps[g], received[g]], axis=0)]
    unnamed x21 -> x32, local copies, waits for them, and re-layouts: 1.58 us -> 5.09 us
    mul x8 -> x6, local copies, waits for them, and re-layouts: 3.22 us -> 1.82 us  [twice(): return jnp.kron(jnp.eye(2, dtype=matrix.dtype), matrix)]
  transfers between devices with their start and end apart: 6 -> 12, of which waited for: 3 -> 4; matrix products, arithmetic and copies ran while one was open for 5% -> 4% of each run, Pallas kernels for 25% -> 31%
where the time goes in v3:
time: 128 us
  Pallas kernels  89.2 us (70%)
  waiting for transfers between devices  17.3 us (14%)
  starting transfers between devices  12.4 us (10%)
  local copies, waits for them, and re-layouts  7.48 us (6%)
    pallas_call x6, Pallas kernels, call(): pl.pallas_call(kernel, out_shape=out_shape, compiler_params=limit, cost_e...  89.2 us
    ppermute x12, waiting for transfers between devices, exchange(): return lax.ppermute(x, 'res', [(d, d ^ flip) for d in range(devices)])  17.3 us
    ppermute x12, starting transfers between devices, exchange(): return lax.ppermute(x, 'res', [(d, d ^ flip) for d in range(devices)])  12.4 us
    unnamed x32, local copies, waits for them, and re-layouts  5.09 us
  transfers between devices with their start and end apart: 12, of which 4 were waited for; matrix products, arithmetic and copies ran while one was open for 4% of the time, Pallas kernels for 31%

profile of v3, /device:TPU:0, one launch (start us, length us, event | category | flops | bytes accessed | tf_op | source)
XLA Modules:
  0.0 127.6 jit_solution(8195094473464789357)
XLA Ops:
  0.0 2.8 %shard_map.91 = (bf16[288,128]{1,0:T(8,128)(2,1)}, bf16[288,128]{1,0:T(8,128)(2,1)}, bf16[512,128]{1,0:T(8,128)(2,1)}) custom-call(s32[1]{0:T(128)} %bitcast.me_ref, bf16[32,2048]{1,0:T(8,128)(2,1)} %m_ref.1, s32[32,32]{1,0:T(8,128)} %present_ref.3, s32[1,32]{1,0:T(1,128)} %bitcast.22), custom_call_target="tpu_custom_call" | custom-call | bytes 135300 | tf_op jit(solution)/shard_map/pallas_call | solution.py:363
  2.8 0.5 collective-permute-start.1
  3.3 1.4 %copy.15.w_ref = bf16[128,8]{1,0:T(8,128)(2,1)} copy(bf16[128,8]{0,1:T(8,128)(2,1)} %param.13) | data formatting | bytes 4096 | tf_op args[4]
  4.7 20.7 %shard_map.92.own_ref = bf16[256,1024]{1,0:T(8,128)(2,1)} custom-call(bf16[32,1024,128]{2,1,0:T(8,128)(2,1)} %x_ref.1, bf16[128,8]{1,0:T(8,128)(2,1)} %copy.15.w_ref), custom_call_target="tpu_custom_call" | custom-call | flops 2147483648 | bytes 8390656 | tf_op jit(solution)/shard_map/pallas_call | solution.py:363
  25.6 0.1 copy.12
  25.8 0.1 copy.14
  26.0 3.1 %collective-permute-start.2 = (bf16[576,128]{1,0:T(8,128)(2,1)S(1)}, bf16[576,128]{1,0:T(8,128)(2,1)S(1)}, u32[]{:S(2)}, u32[]{:S(2)}) collective-permute-start(bf16[576,128]{1,0:T(8,128)(2,1)S(1)} %constant_dynamic-update-slice_fusion), channel_id=1, source_target_pairs={{0,8},{1,9},{2,10},{3,11},{4,12},{5,13},{6,14},{7,15},{8,0},{9,1},... | collective-permute-start | bytes 442376 | tf_op jit(solution)/shard_map/ppermute | solution.py:377
  29.1 2.6 %collective-permute-start.3 = (bf16[576,128]{1,0:T(8,128)(2,1)S(1)}, bf16[576,128]{1,0:T(8,128)(2,1)S(1)}, u32[]{:S(2)}, u32[]{:S(2)}) collective-permute-start(bf16[576,128]{1,0:T(8,128)(2,1)S(1)} %constant_dynamic-update-slice_fusion), channel_id=1, source_target_pairs={{0,16},{1,17},{2,18},{3,19},{4,20},{5,21},{6,22},{7,23},{8,24},{9,... | collective-permute-start | bytes 442376 | tf_op jit(solution)/shard_map/ppermute | solution.py:377
  31.8 3.5 %collective-permute-done.2 = bf16[576,128]{1,0:T(8,128)(2,1)S(1)} collective-permute-done((bf16[576,128]{1,0:T(8,128)(2,1)S(1)}, bf16[576,128]{1,0:T(8,128)(2,1)S(1)}, u32[]{:S(2)}, u32[]{:S(2)}) %collective-permute-start.2) | collective-permute-done | bytes 147488 | tf_op jit(solution)/shard_map/ppermute | solution.py:377
  35.3 7.8 %collective-permute-done.3 = bf16[576,128]{1,0:T(8,128)(2,1)S(1)} collective-permute-done((bf16[576,128]{1,0:T(8,128)(2,1)S(1)}, bf16[576,128]{1,0:T(8,128)(2,1)S(1)}, u32[]{:S(2)}, u32[]{:S(2)}) %collective-permute-start.3) | collective-permute-done | bytes 147488 | tf_op jit(solution)/shard_map/ppermute | solution.py:377
  43.2 1.6 %collective-permute-start.5 = (bf16[4,2,144,128]{3,2,1,0:T(8,128)(2,1)S(1)}, bf16[4,2,144,128]{3,2,1,0:T(8,128)(2,1)S(1)}, u32[]{:S(2)}, u32[]{:S(2)}) collective-permute-start(bf16[4,2,144,128]{3,2,1,0:T(8,128)(2,1)S(1)} %get-tuple-element.20.refs_0_.refs_2_), channel_id=1, source_target_pairs={{0,2},{1,3},{2,0},{3,1},{4,6},{5,7},{6,4},{7,5},{8,10},{9,11},{10,... | collective-permute-start | bytes 884744 | tf_op jit(solution)/shard_map/ppermute | solution.py:377
  44.8 1.5 %collective-permute-start.8 = (bf16[4,2,144,128]{3,2,1,0:T(8,128)(2,1)S(1)}, bf16[4,2,144,128]{3,2,1,0:T(8,128)(2,1)S(1)}, u32[]{:S(2)}, u32[]{:S(2)}) collective-permute-start(bf16[4,2,144,128]{3,2,1,0:T(8,128)(2,1)S(1)} %get-tuple-element.19.refs_1_.refs_3_), channel_id=1, source_target_pairs={{0,4},{1,5},{2,6},{3,7},{4,0},{5,1},{6,2},{7,3},{8,12},{9,13},{10,... | collective-permute-start | bytes 884744 | tf_op jit(solution)/shard_map/ppermute | solution.py:377
  46.3 0.5 collective-permute-start.6
  46.8 0.5 collective-permute-start.7
  47.4 0.4 broadcast_multiply_fusion
  48.1 0.7 mul.112.wo
  48.8 0.7 mul.127.wout
  49.6 5.2 %collective-permute-done.8.refs_5_.refs_7_ = bf16[4,2,144,128]{3,2,1,0:T(8,128)(2,1)S(1)} collective-permute-done((bf16[4,2,144,128]{3,2,1,0:T(8,128)(2,1)S(1)}, bf16[4,2,144,128]{3,2,1,0:T(8,128)(2,1)S(1)}, u32[]{:S(2)}, u32[]{:S(2)}) %collective-permute-start.8) | collective-permute-done | bytes 294944 | tf_op jit(solution)/shard_map/ppermute | solution.py:377
  54.7 0.5 collective-permute-start.10
  55.3 1.5 %collective-permute-start.9 = (bf16[4,2,144,128]{3,2,1,0:T(8,128)(2,1)S(1)}, bf16[4,2,144,128]{3,2,1,0:T(8,128)(2,1)S(1)}, u32[]{:S(2)}, u32[]{:S(2)}) collective-permute-start(bf16[4,2,144,128]{3,2,1,0:T(8,128)(2,1)S(1)} %collective-permute-done.5.refs_2_.refs_4_), channel_id=1, source_target_pairs={{0,4},{1,5},{2,6},{3,7},{4,0},{5,1},{6,2},{7,3},{8,12},{9,13},{10,... | collective-permute-start | bytes 884744 | tf_op jit(solution)/shard_map/ppermute | solution.py:377
  56.8 0.8 copy-done.14
  57.6 5.3 %shard_map.93 = (f32[512,1024]{1,0:T(8,128)}, bf16[16,512,128]{2,1,0:T(8,128)(2,1)}) custom-call(s32[1]{0:T(128)} %bitcast.me_ref, bf16[256,1024]{1,0:T(8,128)(2,1)} %shard_map.92.own_ref, bf16[256,1024]{1,0:T(8,128)(2,1)} %copy-done.14, bf16[288,128]{1,0:T(8,128)(2,1)} %get-tuple-element.13.keep_ref, bf16[288,128]{1,0:T(8,128)(2,1)} %copy-done.9, ...), custom_call_target="tpu_custom_call" | custom-call | flops 1073741824 | bytes 1228804 | tf_op jit(solution)/shard_map/pallas_call | solution.py:363
  63.0 0.7 copy-done.4
  63.7 0.1 copy-done.5
  63.8 13.3 %shard_map.94.sums_ref = f32[16,512,128]{2,1,0:T(8,128)} custom-call(bf16[16,512,128]{2,1,0:T(8,128)(2,1)} %get-tuple-element.15.lhs_ref, f32[512,1024]{1,0:T(8,128)} %get-tuple-element.16.bias_ref, bf16[4,2,144,128]{3,2,1,0:T(8,128)(2,1)} %copy-done.1, bf16[4,2,144,128]{3,2,1,0:T(8,128)(2,1)} %copy-done, bf16[4,2,144,128]{3,2,1,0:T(8,128)(2,1)} %copy-done.2, ...), custom_call_target="tpu_custom_call" | custom-call | flops 4294967296 | bytes 5963776 | tf_op jit(solution)/shard_map/pallas_call | solution.py:363
  77.1 0.7 copy-done.6
  77.8 0.7 copy-done.7
  78.5 43.6 %shard_map.95 = (bf16[256,128]{1,0:T(8,128)(2,1)}, bf16[256,128]{1,0:T(8,128)(2,1)}) custom-call(bf16[16,512,128]{2,1,0:T(8,128)(2,1)} %get-tuple-element.15.lhs_ref, f32[512,1024]{1,0:T(8,128)} %get-tuple-element.16.bias_ref, f32[16,512,128]{2,1,0:T(8,128)} %shard_map.94.sums_ref, bf16[64,256]{1,0:T(8,128)(2,1)} %w_ref.4, ...), custom_call_target="tpu_custom_call" | custom-call | flops 2147483648 | bytes 10928128 | tf_op jit(solution)/shard_map/pallas_call | solution.py:363
  122.1 0.7 pad_maximum_fusion.1.wc
  122.8 0.8 collective-permute-done.11.theirs_ref
  123.6 0.6 copy-done.11
  124.2 3.4 %shard_map.96 = bf16[32,2048]{1,0:T(8,128)(2,1)} custom-call(s32[1]{0:T(128)} %bitcast.me_ref, bf16[512,128]{1,0:T(8,128)(2,1)} %get-tuple-element.12.line_ref, s32[32,32]{1,0:T(8,128)} %present_ref.3, s32[1,32]{1,0:T(1,128)} %bitcast.23, bf16[128,128]{1,0:T(8,128)(2,1)} %mul.112.wo, bf16[128,512]{1,0:T(8,128)(2,1)} %pad_maximum_fusion.1.wc, ...), custom_call_target="tpu_custom_call" | custom-call | bytes 462980 | tf_op jit(solution)/shard_map/pallas_call | solution.py:363
  (50 shorter events, 1.0 us)
Async XLA Ops:
  2.8 23.1 %collective-permute-start.1 = (bf16[288,128]{1,0:T(8,128)(2,1)}, bf16[288,128]{1,0:T(8,128)(2,1)S(1)}, u32[]{:S(2)}, u32[]{:S(2)}) collective-permute-start(bf16[288,128]{1,0:T(8,128)(2,1)} %get-tuple-element.14), channel_id=1, source_target_pairs={{0,1},{1,0},{2,3},{3,2},{4,5},{5,4},{6,7},{7,6},{8,9},{9,8},{10,11... | collective-permute-start | bytes 221192 | tf_op jit(solution)/shard_map/ppermute | solution.py:377
  4.7 20.8 %copy-start.10 = (bf16[64,144]{1,0:T(8,128)(2,1)S(1)}, bf16[64,144]{1,0:T(8,128)(2,1)}, u32[]{:S(2)}) copy-start(bf16[64,144]{1,0:T(8,128)(2,1)} %param.16) | copy-start | bytes 55300
  4.7 21.2 %copy-start.8 = (bf16[288,128]{1,0:T(8,128)(2,1)S(1)}, bf16[288,128]{1,0:T(8,128)(2,1)}, u32[]{:S(2)}) copy-start(bf16[288,128]{1,0:T(8,128)(2,1)} %get-tuple-element.13.keep_ref) | copy-start | bytes 221188
  4.7 42.6 %copy-start.12 = (bf16[64,64]{1,0:T(8,128)(2,1)S(1)}, bf16[64,64]{1,0:T(8,128)(2,1)}, u32[]{:S(2)}) copy-start(bf16[64,64]{1,0:T(8,128)(2,1)} %param.17) | copy-start | bytes 24580
  4.7 42.6 %copy-start.13 = (bf16[64,64]{1,0:T(8,128)(2,1)S(1)}, bf16[64,64]{1,0:T(8,128)(2,1)}, u32[]{:S(2)}) copy-start(bf16[64,64]{1,0:T(8,128)(2,1)} %param.15) | copy-start | bytes 24580
  25.4 31.4 %collective-permute-start = (bf16[256,1024]{1,0:T(8,128)(2,1)}, bf16[256,1024]{1,0:T(8,128)(2,1)S(1)}, u32[]{:S(2)}, u32[]{:S(2)}) collective-permute-start(bf16[256,1024]{1,0:T(8,128)(2,1)} %shard_map.92.own_ref), channel_id=1, source_target_pairs={{0,1},{1,0},{2,3},{3,2},{4,5},{5,4},{6,7},{7,6},{8,9},{9,8},{10,11... | collective-permute-start | bytes 1572872 | tf_op jit(solution)/shard_map/ppermute | solution.py:377
  26.0 30.8 %copy-start.9 = (bf16[288,128]{1,0:T(8,128)(2,1)}, bf16[288,128]{1,0:T(8,128)(2,1)S(1)}, u32[]{:S(2)}) copy-start(bf16[288,128]{1,0:T(8,128)(2,1)S(1)} %collective-permute-done.1.received_ref) | copy-start | bytes 221188
  26.0 9.3 %collective-permute-start.2 = (bf16[576,128]{1,0:T(8,128)(2,1)S(1)}, bf16[576,128]{1,0:T(8,128)(2,1)S(1)}, u32[]{:S(2)}, u32[]{:S(2)}) collective-permute-start(bf16[576,128]{1,0:T(8,128)(2,1)S(1)} %constant_dynamic-update-slice_fusion), channel_id=1, source_target_pairs={{0,8},{1,9},{2,10},{3,11},{4,12},{5,13},{6,14},{7,15},{8,0},{9,1},... | collective-permute-start | bytes 442376 | tf_op jit(solution)/shard_map/ppermute | solution.py:377
  29.1 14.0 %collective-permute-start.3 = (bf16[576,128]{1,0:T(8,128)(2,1)S(1)}, bf16[576,128]{1,0:T(8,128)(2,1)S(1)}, u32[]{:S(2)}, u32[]{:S(2)}) collective-permute-start(bf16[576,128]{1,0:T(8,128)(2,1)S(1)} %constant_dynamic-update-slice_fusion), channel_id=1, source_target_pairs={{0,16},{1,17},{2,18},{3,19},{4,20},{5,21},{6,22},{7,23},{8,24},{9,... | collective-permute-start | bytes 442376 | tf_op jit(solution)/shard_map/ppermute | solution.py:377
  31.7 11.4 %collective-permute-start.4 = (bf16[576,128]{1,0:T(8,128)(2,1)S(1)}, bf16[576,128]{1,0:T(8,128)(2,1)S(1)}, u32[]{:S(2)}, u32[]{:S(2)}) collective-permute-start(bf16[576,128]{1,0:T(8,128)(2,1)S(1)} %constant_dynamic-update-slice_fusion), channel_id=1, source_target_pairs={{0,24},{1,25},{2,26},{3,27},{4,28},{5,29},{6,30},{7,31},{8,16},{9,... | collective-permute-start | bytes 442376 | tf_op jit(solution)/shard_map/ppermute | solution.py:377
  43.2 19.8 %copy-start = (bf16[4,2,144,128]{3,2,1,0:T(8,128)(2,1)}, bf16[4,2,144,128]{3,2,1,0:T(8,128)(2,1)S(1)}, u32[]{:S(2)}) copy-start(bf16[4,2,144,128]{3,2,1,0:T(8,128)(2,1)S(1)} %get-tuple-element.19.refs_1_.refs_3_) | copy-start | bytes 884740
  43.2 19.8 %copy-start.1 = (bf16[4,2,144,128]{3,2,1,0:T(8,128)(2,1)}, bf16[4,2,144,128]{3,2,1,0:T(8,128)(2,1)S(1)}, u32[]{:S(2)}) copy-start(bf16[4,2,144,128]{3,2,1,0:T(8,128)(2,1)S(1)} %get-tuple-element.20.refs_0_.refs_2_) | copy-start | bytes 884740
  43.2 12.0 %collective-permute-start.5 = (bf16[4,2,144,128]{3,2,1,0:T(8,128)(2,1)S(1)}, bf16[4,2,144,128]{3,2,1,0:T(8,128)(2,1)S(1)}, u32[]{:S(2)}, u32[]{:S(2)}) collective-permute-start(bf16[4,2,144,128]{3,2,1,0:T(8,128)(2,1)S(1)} %get-tuple-element.20.refs_0_.refs_2_), channel_id=1, source_target_pairs={{0,2},{1,3},{2,0},{3,1},{4,6},{5,7},{6,4},{7,5},{8,10},{9,11},{10,... | collective-permute-start | bytes 884744 | tf_op jit(solution)/shard_map/ppermute | solution.py:377
  44.8 9.9 %collective-permute-start.8 = (bf16[4,2,144,128]{3,2,1,0:T(8,128)(2,1)S(1)}, bf16[4,2,144,128]{3,2,1,0:T(8,128)(2,1)S(1)}, u32[]{:S(2)}, u32[]{:S(2)}) collective-permute-start(bf16[4,2,144,128]{3,2,1,0:T(8,128)(2,1)S(1)} %get-tuple-element.19.refs_1_.refs_3_), channel_id=1, source_target_pairs={{0,4},{1,5},{2,6},{3,7},{4,0},{5,1},{6,2},{7,3},{8,12},{9,13},{10,... | collective-permute-start | bytes 884744 | tf_op jit(solution)/shard_map/ppermute | solution.py:377
  46.3 16.6 %collective-permute-start.6 = (bf16[4,2,144,128]{3,2,1,0:T(8,128)(2,1)S(1)}, bf16[4,2,144,128]{3,2,1,0:T(8,128)(2,1)S(1)}, u32[]{:S(2)}, u32[]{:S(2)}) collective-permute-start(bf16[4,2,144,128]{3,2,1,0:T(8,128)(2,1)S(1)} %get-tuple-element.19.refs_1_.refs_3_), channel_id=1, source_target_pairs={{0,2},{1,3},{2,0},{3,1},{4,6},{5,7},{6,4},{7,5},{8,10},{9,11},{10,... | collective-permute-start | bytes 884744 | tf_op jit(solution)/shard_map/ppermute | solution.py:377
  46.8 16.1 %collective-permute-start.7 = (bf16[4,2,144,128]{3,2,1,0:T(8,128)(2,1)S(1)}, bf16[4,2,144,128]{3,2,1,0:T(8,128)(2,1)S(1)}, u32[]{:S(2)}, u32[]{:S(2)}) collective-permute-start(bf16[4,2,144,128]{3,2,1,0:T(8,128)(2,1)S(1)} %get-tuple-element.20.refs_0_.refs_2_), channel_id=1, source_target_pairs={{0,4},{1,5},{2,6},{3,7},{4,0},{5,1},{6,2},{7,3},{8,12},{9,13},{10,... | collective-permute-start | bytes 884744 | tf_op jit(solution)/shard_map/ppermute | solution.py:377
  54.7 8.3 %copy-start.3 = (bf16[4,2,144,128]{3,2,1,0:T(8,128)(2,1)}, bf16[4,2,144,128]{3,2,1,0:T(8,128)(2,1)S(1)}, u32[]{:S(2)}) copy-start(bf16[4,2,144,128]{3,2,1,0:T(8,128)(2,1)S(1)} %collective-permute-done.8.refs_5_.refs_7_) | copy-start | bytes 884740
  54.7 22.3 %collective-permute-start.10 = (bf16[4,2,144,128]{3,2,1,0:T(8,128)(2,1)S(1)}, bf16[4,2,144,128]{3,2,1,0:T(8,128)(2,1)S(1)}, u32[]{:S(2)}, u32[]{:S(2)}) collective-permute-start(bf16[4,2,144,128]{3,2,1,0:T(8,128)(2,1)S(1)} %collective-permute-done.8.refs_5_.refs_7_), channel_id=1, source_target_pairs={{0,2},{1,3},{2,0},{3,1},{4,6},{5,7},{6,4},{7,5},{8,10},{9,11},{10,... | collective-permute-start | bytes 884744 | tf_op jit(solution)/shard_map/ppermute | solution.py:377
  55.3 7.7 %copy-start.2 = (bf16[4,2,144,128]{3,2,1,0:T(8,128)(2,1)}, bf16[4,2,144,128]{3,2,1,0:T(8,128)(2,1)S(1)}, u32[]{:S(2)}) copy-start(bf16[4,2,144,128]{3,2,1,0:T(8,128)(2,1)S(1)} %collective-permute-done.5.refs_2_.refs_4_) | copy-start | bytes 884740
  55.3 21.8 %collective-permute-start.9 = (bf16[4,2,144,128]{3,2,1,0:T(8,128)(2,1)S(1)}, bf16[4,2,144,128]{3,2,1,0:T(8,128)(2,1)S(1)}, u32[]{:S(2)}, u32[]{:S(2)}) collective-permute-start(bf16[4,2,144,128]{3,2,1,0:T(8,128)(2,1)S(1)} %collective-permute-done.5.refs_2_.refs_4_), channel_id=1, source_target_pairs={{0,4},{1,5},{2,6},{3,7},{4,0},{5,1},{6,2},{7,3},{8,12},{9,13},{10,... | collective-permute-start | bytes 884744 | tf_op jit(solution)/shard_map/ppermute | solution.py:377
  56.8 0.8 copy-start.14
  63.0 0.7 copy-start.4
  63.0 0.8 copy-start.5
  77.1 0.7 copy-start.6
  77.8 0.7 copy-start.7
  122.1 1.5 %collective-permute-start.11 = (bf16[256,128]{1,0:T(8,128)(2,1)}, bf16[256,128]{1,0:T(8,128)(2,1)S(1)}, u32[]{:S(2)}, u32[]{:S(2)}) collective-permute-start(bf16[256,128]{1,0:T(8,128)(2,1)} %get-tuple-element.18), channel_id=1, source_target_pairs={{0,1},{1,0},{2,3},{3,2},{4,5},{5,4},{6,7},{7,6},{8,9},{9,8},{10,11... | collective-permute-start | bytes 196616 | tf_op jit(solution)/shard_map/ppermute | solution.py:377
  123.6 0.6 copy-start.11

commit v4 on v3

--- a/solution.py
+++ b/solution.py
@@ -12,7 +12,6 @@
 BF16 = jnp.bfloat16
 LOG2E = math.log2(math.e)
 EPS = 1e-05
-VMEM_LIMIT = 56 * 1024 * 1024
 
 NT = (((1,), (1,)), ((), ()))
 
@@ -34,7 +33,7 @@
 
 
 def block_matrix(size, block, on_diagonal, elsewhere):
-    row, col = iota((size, size), 0), iota((size, size), 1)
+    row, col = iota((size, 1), 0), iota((1, size), 1)
     inside = jnp.where(row == col, on_diagonal, elsewhere)
     return jnp.where(row // block == col // block, inside, 0.0).astype(BF16)
 
@@ -58,7 +57,7 @@
 
 def row_shuffle(rows, inner, outer):
     total = rows.shape[0]
-    row, col = iota((total, total), 0), iota((total, total), 1)
+    row, col = iota((total, 1), 0), iota((1, total), 1)
     return mm(one_hot(col == (row % inner) * outer + row // inner), rows).astype(BF16)
 
 
@@ -93,7 +92,7 @@
             ref[start + rows : start + rows + pairs, :] = spread_ref[index]
 
 
-def bias_kernel(x_ref, w_ref, out_ref, acc_ref):
+def bias_kernel(x_ref, w_ref, after_ref, out_ref, acc_ref):
     step = pl.program_id(0)
     heads = w_ref.shape[1]
     per_step, keys, channels = x_ref.shape
@@ -114,13 +113,14 @@
     def _():
         acc_ref[tile] = jnp.zeros(acc_ref.shape[1:], F32)
 
-    piece = 128
+    averaging = jnp.concatenate([averaging, averaging], axis=0)
+    piece = 512
     for r in range(0, keys, piece):
         normed = []
         for n in range(0, per_step, 2):
             x = jnp.concatenate([x_ref[n, r : r + piece], x_ref[n + 1, r : r + piece]], axis=1)
             centre = mm(x, centring)
-            spread = mm_split(centre * centre, averaging)
+            spread = mm(jnp.concatenate(halves(centre * centre), axis=1), averaging)
             normed.append((centre * lax.rsqrt(spread + EPS)).astype(BF16))
         acc_ref[tile, r : r + piece, :] += mm(jnp.concatenate(normed, axis=1), placed)
 
@@ -255,11 +255,16 @@
     own_head = jnp.where(lane // depth == row, 1.0, 0.0)[None]
     masks = [masks_of(ref, size, pairs) for ref in piece_refs]
     low = iota((lhs_ref.shape[1], 128), 1) < 64
+    row, col = iota((128, 1), 0), iota((1, 128), 1)
+    averaged = jnp.where(row + 0 * col < hidden, 0.0, 1.0 / (128 - hidden)).astype(BF16)
+    wv = jnp.concatenate([wv, averaged], axis=1)
+    wv = jnp.concatenate([wv, wv], axis=0)
+    own_head = jnp.concatenate([own_head, own_head], axis=2)
 
     def settle(line, total):
-        mean = jnp.where(low, total / pltpu.roll(total, 64, 1), 0.0).astype(BF16)
-        mixed = mm(mean, wv).reshape(2 * pairs, 2 * heads, 128)
-        summed = jnp.sum(mixed * own_head, axis=1)
+        mixed = mm(jnp.concatenate(halves(total), axis=1), wv)
+        summed = jnp.sum(mixed.reshape(2 * pairs, 2 * heads, 256) * own_head, axis=1)
+        summed = summed[:, :128] / summed[:, 128:]
         start = pl.multiple_of(line * pairs, pairs)
         for n in range(2):
             attended_ref[n, pl.ds(start, pairs), :] = summed[n * pairs : (n + 1) * pairs]
@@ -316,8 +321,8 @@
 
 
 def final_kernel(
-    lines, with_column, me_ref, line_ref, present_ref, amino_ref, wo, wc, wout, mine_ref,
-    theirs_ref, out_ref, gated_ref,
+    lines, heads, with_column, me_ref, line_ref, present_ref, amino_ref, wo_ref, wc_ref, wout_ref,
+    mine_ref, theirs_ref, out_ref, gated_ref,
 ):
     total = line_ref.shape[0]
     pairs = total // lines
@@ -325,7 +330,21 @@
     share = total // 2
     for owner, ref in ((core, mine_ref), (1 - core, theirs_ref)):
         gated_ref[pl.ds(pl.multiple_of(owner * share, share), share), :] = ref[...]
-    row = (line_ref[...].astype(F32) + mm(gated_ref[...], wo[...])).astype(BF16)
+    hidden = wo_ref.shape[0]
+    depth = hidden // heads
+    rows_twice = one_hot(iota((128, 1), 0) % hidden == iota((1, hidden), 1))
+    same_residue = iota((128, 1), 0) // hidden == iota((1, 128), 1) // hidden
+
+    def twice(matrix, picked):
+        wide = mm(mm(rows_twice, matrix).astype(BF16), picked)
+        return jnp.where(same_residue, wide, 0.0).astype(BF16)
+
+    def columns(width, chosen):
+        return one_hot(iota((width, 1), 0) == chosen)
+
+    lane = iota((1, 128), 1)
+    wo = twice(wo_ref[...], columns(hidden, lane % hidden))
+    row = (line_ref[...].astype(F32) + mm(gated_ref[...], wo)).astype(BF16)
     if not with_column:
         out_ref[...] = row
         return
@@ -335,21 +354,29 @@
     sides = one_hot(iota((2 * pairs, 128), 0) % 2 == iota((2 * pairs, 128), 1) // 64)
     kept = mm(jnp.where(own, spread, 0.0).astype(BF16), sides)
 
-    projected = mm(paired_norm(row, 64), wc[...])
+    choices = [
+        lane % hidden,
+        hidden + lane % hidden,
+        2 * hidden + lane % depth,
+        2 * hidden + depth + lane % depth,
+    ]
+    wc = [twice(wc_ref[...], columns(wc_ref.shape[1], chosen)) for chosen in choices]
+    projected = mm(paired_norm(row, 64), jnp.concatenate(wc, axis=1))
     query, gate, key, value = [projected[:, 128 * n : 128 * (n + 1)] for n in range(4)]
 
     def grid(a):
         return a.reshape(lines, pairs, 128)
 
     count = jnp.maximum(jnp.sum(grid(kept), axis=0), 1.0)
-    mean_query = jnp.sum(grid(kept * query), axis=0) / count * (8**-0.5)
-    same_head = block_matrix(128, 8, 1.0, 1.0)
+    mean_query = jnp.sum(grid(kept * query), axis=0) / count * (depth**-0.5)
+    same_head = block_matrix(128, depth, 1.0, 1.0)
     product = (mean_query[None] * grid(key)).reshape(total, 128)
     logits = grid(mm_split(product, same_head) + 1e9 * (kept - 1.0))
     exped = jnp.exp(logits - jnp.max(logits, axis=0, keepdims=True))
     mixed = jnp.sum(exped * grid(value), axis=0) / jnp.sum(exped, axis=0)
     gated = (jax.nn.sigmoid(grid(gate)) * mixed[None]).reshape(total, 128).astype(BF16)
-    result = (row.astype(F32) + mm(gated, wout[...])).astype(BF16)
+    wout = twice(wout_ref[...], columns(hidden, lane % hidden))
+    result = (row.astype(F32) + mm(gated, wout)).astype(BF16)
     shuffled = row_shuffle(result, lines, pairs)
     for t in range(pairs):
         out_ref[:, t * 128 : (t + 1) * 128] = shuffled[t * lines : (t + 1) * lines, :]
@@ -357,7 +384,7 @@
 
 def call(kernel, out_shape, *args, **options):
     flops = options.pop("flops", 0)
-    limit = pltpu.CompilerParams(vmem_limit_bytes=VMEM_LIMIT)
+    limit = pltpu.CompilerParams(vmem_limit_bytes=options.pop("mib", 8) * 1024 * 1024)
     moved = sum(a.size * a.dtype.itemsize for a in args)
     cost = pl.CostEstimate(flops=flops, bytes_accessed=moved, transcendentals=0)
     return pl.pallas_call(
@@ -367,10 +394,6 @@
 
 def shape(*dims, dtype=BF16):
     return jax.ShapeDtypeStruct(dims, dtype)
-
-
-def twice(matrix):
-    return jnp.kron(jnp.eye(2, dtype=matrix.dtype), matrix)
 
 
 def exchange(x, flip, devices):
@@ -465,14 +488,17 @@
         shape(rows, pair.shape[1]),
         pair,
         offset_matrix,
+        chunk,
         grid=(residues // per_step,),
         in_specs=[
             pl.BlockSpec((per_step,) + pair.shape[1:], lambda n: (n, 0, 0)),
             pl.BlockSpec(offset_matrix.shape, lambda n: (0, 0)),
+            pl.BlockSpec(memory_space=pl.ANY),
         ],
         out_specs=pl.BlockSpec((rows, pair.shape[1]), lambda n: (0, 0)),
         scratch_shapes=[pltpu.VMEM((rows // 128, pair.shape[1], 128), F32)],
-        flops=4 * pair.size * 128,
+        flops=16 * pair.size * 128,
+        mib=16,
     )
     if seq_size > 1:
         bias = lax.all_gather(bias, "seq", axis=1, tiled=True)
@@ -488,6 +514,7 @@
         horizontal_matrix,
         in_specs=[smem] + [vmem] * 5,
         flops=4 * rows * keys * keys,
+        mib=14,
     )
     sums = call(
         functools.partial(start_kernel, groups, size, pairs, (0, 1, 2)),
@@ -498,6 +525,7 @@
         *beside,
         *across,
         flops=groups * size * rows * keys * 2 * 256 * 2,
+        mib=18,
     )
     anywhere = pl.BlockSpec(memory_space=pl.ANY)
     mine, theirs = call(
@@ -520,28 +548,23 @@
             pltpu.VMEM((3 * groups,) + own[0].shape, BF16),
         ],
         flops=groups * size * rows * keys * 2 * 256,
+        mib=22,
     )
     returned = exchange(theirs, core_bit, res_size)
 
-    w_column = [
-        vertical_matrix[:, :hidden],
-        vertical_matrix[:, hidden : 2 * hidden],
-        jnp.tile(vertical_matrix[:, 2 * hidden : 2 * hidden + depth], (1, heads)),
-        jnp.tile(vertical_matrix[:, 2 * hidden + depth :], (1, heads)),
-    ]
     with_column = seq_size == 1
     final_args = [
         me,
         line,
         present,
         amino_row,
-        twice(horizontal_exit_matrix),
-        jnp.concatenate([twice(w) for w in w_column], axis=1),
-        twice(vertical_exit_matrix),
+        horizontal_exit_matrix,
+        vertical_matrix,
+        vertical_exit_matrix,
     ]
     final_args += [mine, returned]
     result = call(
-        functools.partial(final_kernel, lines, with_column),
+        functools.partial(final_kernel, lines, heads, with_column),
         shape(*extra_activations.shape) if with_column else shape(lines * pairs, 128),
         *final_args,
         in_specs=[smem] + [vmem] * (len(final_args) - 1),

time: 128 us -> 89.1 us (0.70)
  Pallas kernels: 89.2 us -> 59.2 us
  waiting for transfers between devices: 17.3 us -> 9.33 us
    pallas_call x6, Pallas kernels: 89.2 us -> 59.2 us  [call(): pl.pallas_call(kernel, out_shape=out_shape, compiler_params=limit, cost_e...]
    ppermute x12, waiting for transfers between devices: 17.3 us -> 9.33 us  [exchange(): return lax.ppermute(x, 'res', [(d, d ^ flip) for d in range(devices)])]
    mul x6 -> x0, local copies, waits for them, and re-layouts: 1.82 us -> none  [twice(): return jnp.kron(jnp.eye(2, dtype=matrix.dtype), matrix)]
    unnamed x32 -> x22, local copies, waits for them, and re-layouts: 5.09 us -> 6.5 us
  transfers between devices with their start and end apart: 12 -> 12, of which waited for: 4 -> 5; matrix products, arithmetic and copies ran while one was open for 4% -> 1% of each run, Pallas kernels for 31% -> 27%
where the time goes in v4:
time: 89.1 us; the launch traced here: 88.9 us
  Pallas kernels  59.2 us (66%)
  starting transfers between devices  13.5 us (15%)
  waiting for transfers between devices  9.33 us (10%)
  local copies, waits for them, and re-layouts  6.55 us (7%)
    pallas_call x6, Pallas kernels, call(): pl.pallas_call(kernel, out_shape=out_shape, compiler_params=limit, cost_e...  59.2 us
    ppermute x12, starting transfers between devices, exchange(): return lax.ppermute(x, 'res', [(d, d ^ flip) for d in range(devices)])  13.5 us
    ppermute x12, waiting for transfers between devices, exchange(): return lax.ppermute(x, 'res', [(d, d ^ flip) for d in range(devices)])  9.33 us
    unnamed x22, local copies, waits for them, and re-layouts  6.5 us
  transfers between devices with their start and end apart: 12, of which 5 were waited for; matrix products, arithmetic and copies ran while one was open for 1% of the time, Pallas kernels for 27%

profile of v4, /device:TPU:0, one launch (start us, length us, event | category | flops | bytes accessed | tf_op | source)
XLA Modules:
  0.0 88.9 jit_solution(12925486645801830507)
XLA Ops:
  0.0 0.9 %copy-done = bf16[32,2048]{1,0:T(8,128)(2,1)S(1)} copy-done((bf16[32,2048]{1,0:T(8,128)(2,1)S(1)}, bf16[32,2048]{1,0:T(8,128)(2,1)}, u32[]{:S(2)}) %copy-start) | copy-done | bytes 131096
  0.9 0.7 copy-done.1
  1.6 0.7 copy-done.7
  2.3 1.2 %shard_map.91 = (bf16[288,128]{1,0:T(8,128)(2,1)S(1)}, bf16[288,128]{1,0:T(8,128)(2,1)S(1)}, bf16[512,128]{1,0:T(8,128)(2,1)S(1)}) custom-call(s32[1]{0:T(128)} %bitcast.me_ref, bf16[32,2048]{1,0:T(8,128)(2,1)S(1)} %copy-done, s32[32,32]{1,0:T(8,128)S(1)} %copy-done.1, s32[1,32]{1,0:T(1,128)S(1)} %bitcast.15), custom_call_target="tpu_custom_call" | custom-call | bytes 135300 | tf_op jit(solution)/shard_map/pallas_call | solution.py:390
  3.5 0.5 collective-permute-start
  4.0 0.8 copy.11.w_ref
  4.8 0.1 collective-permute-done.received_ref
  4.9 5.0 %collective-permute-start.4 = (bf16[576,128]{1,0:T(8,128)(2,1)S(1)}, bf16[576,128]{1,0:T(8,128)(2,1)S(1)}, u32[]{:S(2)}, u32[]{:S(2)}) collective-permute-start(bf16[576,128]{1,0:T(8,128)(2,1)S(1)} %constant_dynamic-update-slice_fusion.after_ref), channel_id=1, source_target_pairs={{0,24},{1,25},{2,26},{3,27},{4,28},{5,29},{6,30},{7,31},{8,16},{9,... | collective-permute-start | bytes 442376 | tf_op jit(solution)/shard_map/ppermute | solution.py:400
  9.9 0.6 collective-permute-start.2
  10.6 3.4 %copy-done.9 = bf16[32,1024,128]{2,1,0:T(8,128)(2,1)S(1)} copy-done((bf16[32,1024,128]{2,1,0:T(8,128)(2,1)S(1)}, bf16[32,1024,128]{2,1,0:T(8,128)(2,1)}, u32[]{:S(2)}) %copy-start.9) | copy-done | bytes 8388632
  13.9 12.5 %shard_map.92.own_ref = bf16[256,1024]{1,0:T(8,128)(2,1)S(1)} custom-call(bf16[32,1024,128]{2,1,0:T(8,128)(2,1)S(1)} %copy-done.9, bf16[128,8]{1,0:T(8,128)(2,1)S(1)} %copy.11.w_ref, bf16[576,128]{1,0:T(8,128)(2,1)S(1)} %constant_dynamic-update-slice_fusion.after_ref), custom_call_target="tpu_custom_call" | custom-call | flops 8589934592 | bytes 8538112 | tf_op jit(solution)/shard_map/pallas_call | solution.py:390
  26.5 0.1 collective-permute-start.1
  26.6 0.1 pad_maximum_fusion
  26.7 1.7 %collective-permute-start.8 = (bf16[4,2,144,128]{3,2,1,0:T(8,128)(2,1)S(1)}, bf16[4,2,144,128]{3,2,1,0:T(8,128)(2,1)S(1)}, u32[]{:S(2)}, u32[]{:S(2)}) collective-permute-start(bf16[4,2,144,128]{3,2,1,0:T(8,128)(2,1)S(1)} %get-tuple-element.19.refs_1_.refs_3_), channel_id=1, source_target_pairs={{0,4},{1,5},{2,6},{3,7},{4,0},{5,1},{6,2},{7,3},{8,12},{9,13},{10,... | collective-permute-start | bytes 884744 | tf_op jit(solution)/shard_map/ppermute | solution.py:400
  28.4 1.5 %collective-permute-start.5 = (bf16[4,2,144,128]{3,2,1,0:T(8,128)(2,1)S(1)}, bf16[4,2,144,128]{3,2,1,0:T(8,128)(2,1)S(1)}, u32[]{:S(2)}, u32[]{:S(2)}) collective-permute-start(bf16[4,2,144,128]{3,2,1,0:T(8,128)(2,1)S(1)} %get-tuple-element.20.refs_0_.refs_2_), channel_id=1, source_target_pairs={{0,2},{1,3},{2,0},{3,1},{4,6},{5,7},{6,4},{7,5},{8,10},{9,11},{10,... | collective-permute-start | bytes 884744 | tf_op jit(solution)/shard_map/ppermute | solution.py:400
  29.9 0.5 collective-permute-start.6
  30.5 0.4 collective-permute-start.7
  30.8 5.8 %collective-permute-done.8.refs_5_.refs_7_ = bf16[4,2,144,128]{3,2,1,0:T(8,128)(2,1)S(1)} collective-permute-done((bf16[4,2,144,128]{3,2,1,0:T(8,128)(2,1)S(1)}, bf16[4,2,144,128]{3,2,1,0:T(8,128)(2,1)S(1)}, u32[]{:S(2)}, u32[]{:S(2)}) %collective-permute-start.8) | collective-permute-done | bytes 294944 | tf_op jit(solution)/shard_map/ppermute | solution.py:400
  36.6 1.6 %collective-permute-start.10 = (bf16[4,2,144,128]{3,2,1,0:T(8,128)(2,1)S(1)}, bf16[4,2,144,128]{3,2,1,0:T(8,128)(2,1)S(1)}, u32[]{:S(2)}, u32[]{:S(2)}) collective-permute-start(bf16[4,2,144,128]{3,2,1,0:T(8,128)(2,1)S(1)} %collective-permute-done.8.refs_5_.refs_7_), channel_id=1, source_target_pairs={{0,2},{1,3},{2,0},{3,1},{4,6},{5,7},{6,4},{7,5},{8,10},{9,11},{10,... | collective-permute-start | bytes 884744 | tf_op jit(solution)/shard_map/ppermute | solution.py:400
  38.2 0.1 collective-permute-done.5.refs_2_.refs_4_
  38.3 1.5 %collective-permute-start.9 = (bf16[4,2,144,128]{3,2,1,0:T(8,128)(2,1)S(1)}, bf16[4,2,144,128]{3,2,1,0:T(8,128)(2,1)S(1)}, u32[]{:S(2)}, u32[]{:S(2)}) collective-permute-start(bf16[4,2,144,128]{3,2,1,0:T(8,128)(2,1)S(1)} %collective-permute-done.5.refs_2_.refs_4_), channel_id=1, source_target_pairs={{0,4},{1,5},{2,6},{3,7},{4,0},{5,1},{6,2},{7,3},{8,12},{9,13},{10,... | collective-permute-start | bytes 884744 | tf_op jit(solution)/shard_map/ppermute | solution.py:400
  39.7 2.7 %shard_map.93 = (f32[512,1024]{1,0:T(8,128)S(1)}, bf16[16,512,128]{2,1,0:T(8,128)(2,1)S(1)}) custom-call(s32[1]{0:T(128)} %bitcast.me_ref, bf16[256,1024]{1,0:T(8,128)(2,1)S(1)} %shard_map.92.own_ref, bf16[256,1024]{1,0:T(8,128)(2,1)S(1)} %collective-permute-done.1.peer_ref, bf16[288,128]{1,0:T(8,128)(2,1)S(1)} %get-tuple-element.13.keep_ref, ...), custom_call_target="tpu_custom_call" | custom-call | flops 1073741824 | bytes 1228804 | tf_op jit(solution)/shard_map/pallas_call | solution.py:390
  42.5 2.1 %collective-permute-done.6.refs_3_.refs_5_ = bf16[4,2,144,128]{3,2,1,0:T(8,128)(2,1)S(1)} collective-permute-done((bf16[4,2,144,128]{3,2,1,0:T(8,128)(2,1)S(1)}, bf16[4,2,144,128]{3,2,1,0:T(8,128)(2,1)S(1)}, u32[]{:S(2)}, u32[]{:S(2)}) %collective-permute-start.6) | collective-permute-done | bytes 294944 | tf_op jit(solution)/shard_map/ppermute | solution.py:400
  44.6 8.6 %shard_map.94.sums_ref = f32[16,512,128]{2,1,0:T(8,128)S(1)} custom-call(bf16[16,512,128]{2,1,0:T(8,128)(2,1)S(1)} %get-tuple-element.15.lhs_ref, f32[512,1024]{1,0:T(8,128)S(1)} %get-tuple-element.16.bias_ref, bf16[4,2,144,128]{3,2,1,0:T(8,128)(2,1)S(1)} %get-tuple-element.20.refs_0_.refs_2_, ...), custom_call_target="tpu_custom_call" | custom-call | flops 4294967296 | bytes 5963776 | tf_op jit(solution)/shard_map/pallas_call | solution.py:390
  53.3 0.0 copy-start.2
  53.3 0.0 copy-start.4
  53.3 0.0 copy-start.5
  53.3 0.0 copy-start.8
  53.3 31.6 %shard_map.95 = (bf16[256,128]{1,0:T(8,128)(2,1)S(1)}, bf16[256,128]{1,0:T(8,128)(2,1)S(1)}) custom-call(bf16[16,512,128]{2,1,0:T(8,128)(2,1)S(1)} %get-tuple-element.15.lhs_ref, f32[512,1024]{1,0:T(8,128)S(1)} %get-tuple-element.16.bias_ref, f32[16,512,128]{2,1,0:T(8,128)S(1)} %shard_map.94.sums_ref, bf16[64,256]{1,0:T(8,128)(2,1)S(1)} %copy-done.3, ...), custom_call_target="tpu_custom_call" | custom-call | flops 2147483648 | bytes 10928128 | tf_op jit(solution)/shard_map/pallas_call | solution.py:390
  85.0 0.1 collective-permute-start.11
  85.0 1.2 %collective-permute-done.11.theirs_ref = bf16[256,128]{1,0:T(8,128)(2,1)S(1)} collective-permute-done((bf16[256,128]{1,0:T(8,128)(2,1)S(1)}, bf16[256,128]{1,0:T(8,128)(2,1)S(1)}, u32[]{:S(2)}, u32[]{:S(2)}) %collective-permute-start.11) | collective-permute-done | bytes 65568 | tf_op jit(solution)/shard_map/ppermute | solution.py:400
  86.3 2.6 %shard_map.96 = bf16[32,2048]{1,0:T(8,128)(2,1)} custom-call(s32[1]{0:T(128)} %bitcast.me_ref, bf16[512,128]{1,0:T(8,128)(2,1)S(1)} %get-tuple-element.12.line_ref, s32[32,32]{1,0:T(8,128)S(1)} %copy-done.2, s32[1,32]{1,0:T(1,128)S(1)} %bitcast.16, bf16[64,64]{1,0:T(8,128)(2,1)S(1)} %copy-done.5, bf16[64,144]{1,0:T(8,128)(2,1)S(1)} %copy-done.4, ...), custom_call_target="tpu_custom_call" | custom-call | bytes 301188 | tf_op jit(solution)/shard_map/pallas_call | solution.py:390
  (23 shorter events, 0.1 us)
Async XLA Ops:
  0.0 0.9 %copy-start = (bf16[32,2048]{1,0:T(8,128)(2,1)S(1)}, bf16[32,2048]{1,0:T(8,128)(2,1)}, u32[]{:S(2)}) copy-start(bf16[32,2048]{1,0:T(8,128)(2,1)} %m_ref.1) | copy-start | bytes 393220
  0.9 0.7 copy-start.1
  1.6 0.7 copy-start.7
  3.5 1.4 %collective-permute-start = (bf16[288,128]{1,0:T(8,128)(2,1)S(1)}, bf16[288,128]{1,0:T(8,128)(2,1)S(1)}, u32[]{:S(2)}, u32[]{:S(2)}) collective-permute-start(bf16[288,128]{1,0:T(8,128)(2,1)S(1)} %get-tuple-element.14), channel_id=1, source_target_pairs={{0,1},{1,0},{2,3},{3,2},{4,5},{5,4},{6,7},{7,6},{8,9},{9,8},{10,11... | collective-permute-start | bytes 221192 | tf_op jit(solution)/shard_map/ppermute | solution.py:400
  4.9 34.9 %copy-start.3 = (bf16[64,256]{1,0:T(8,128)(2,1)S(1)}, bf16[64,256]{1,0:T(8,128)(2,1)}, u32[]{:S(2)}) copy-start(bf16[64,256]{1,0:T(8,128)(2,1)} %w_ref.4) | copy-start | bytes 98308
  4.9 21.6 %collective-permute-start.4 = (bf16[576,128]{1,0:T(8,128)(2,1)S(1)}, bf16[576,128]{1,0:T(8,128)(2,1)S(1)}, u32[]{:S(2)}, u32[]{:S(2)}) collective-permute-start(bf16[576,128]{1,0:T(8,128)(2,1)S(1)} %constant_dynamic-update-slice_fusion.after_ref), channel_id=1, source_target_pairs={{0,24},{1,25},{2,26},{3,27},{4,28},{5,29},{6,30},{7,31},{8,16},{9,... | collective-permute-start | bytes 442376 | tf_op jit(solution)/shard_map/ppermute | solution.py:400
  9.9 16.6 %collective-permute-start.3 = (bf16[576,128]{1,0:T(8,128)(2,1)S(1)}, bf16[576,128]{1,0:T(8,128)(2,1)S(1)}, u32[]{:S(2)}, u32[]{:S(2)}) collective-permute-start(bf16[576,128]{1,0:T(8,128)(2,1)S(1)} %constant_dynamic-update-slice_fusion.after_ref), channel_id=1, source_target_pairs={{0,16},{1,17},{2,18},{3,19},{4,20},{5,21},{6,22},{7,23},{8,24},{9,... | collective-permute-start | bytes 442376 | tf_op jit(solution)/shard_map/ppermute | solution.py:400
  9.9 16.6 %collective-permute-start.2 = (bf16[576,128]{1,0:T(8,128)(2,1)S(1)}, bf16[576,128]{1,0:T(8,128)(2,1)S(1)}, u32[]{:S(2)}, u32[]{:S(2)}) collective-permute-start(bf16[576,128]{1,0:T(8,128)(2,1)S(1)} %constant_dynamic-update-slice_fusion.after_ref), channel_id=1, source_target_pairs={{0,8},{1,9},{2,10},{3,11},{4,12},{5,13},{6,14},{7,15},{8,0},{9,1},... | collective-permute-start | bytes 442376 | tf_op jit(solution)/shard_map/ppermute | solution.py:400
  10.6 3.4 %copy-start.9 = (bf16[32,1024,128]{2,1,0:T(8,128)(2,1)S(1)}, bf16[32,1024,128]{2,1,0:T(8,128)(2,1)}, u32[]{:S(2)}) copy-start(bf16[32,1024,128]{2,1,0:T(8,128)(2,1)} %x_ref.1) | copy-start | bytes 25165828
  26.5 13.3 %collective-permute-start.1 = (bf16[256,1024]{1,0:T(8,128)(2,1)S(1)}, bf16[256,1024]{1,0:T(8,128)(2,1)S(1)}, u32[]{:S(2)}, u32[]{:S(2)}) collective-permute-start(bf16[256,1024]{1,0:T(8,128)(2,1)S(1)} %shard_map.92.own_ref), channel_id=1, source_target_pairs={{0,1},{1,0},{2,3},{3,2},{4,5},{5,4},{6,7},{7,6},{8,9},{9,8},{10,11... | collective-permute-start | bytes 1572872 | tf_op jit(solution)/shard_map/ppermute | solution.py:400
  26.7 9.9 %collective-permute-start.8 = (bf16[4,2,144,128]{3,2,1,0:T(8,128)(2,1)S(1)}, bf16[4,2,144,128]{3,2,1,0:T(8,128)(2,1)S(1)}, u32[]{:S(2)}, u32[]{:S(2)}) collective-permute-start(bf16[4,2,144,128]{3,2,1,0:T(8,128)(2,1)S(1)} %get-tuple-element.19.refs_1_.refs_3_), channel_id=1, source_target_pairs={{0,4},{1,5},{2,6},{3,7},{4,0},{5,1},{6,2},{7,3},{8,12},{9,13},{10,... | collective-permute-start | bytes 884744 | tf_op jit(solution)/shard_map/ppermute | solution.py:400
  28.4 9.8 %collective-permute-start.5 = (bf16[4,2,144,128]{3,2,1,0:T(8,128)(2,1)S(1)}, bf16[4,2,144,128]{3,2,1,0:T(8,128)(2,1)S(1)}, u32[]{:S(2)}, u32[]{:S(2)}) collective-permute-start(bf16[4,2,144,128]{3,2,1,0:T(8,128)(2,1)S(1)} %get-tuple-element.20.refs_0_.refs_2_), channel_id=1, source_target_pairs={{0,2},{1,3},{2,0},{3,1},{4,6},{5,7},{6,4},{7,5},{8,10},{9,11},{10,... | collective-permute-start | bytes 884744 | tf_op jit(solution)/shard_map/ppermute | solution.py:400
  29.9 14.7 %collective-permute-start.6 = (bf16[4,2,144,128]{3,2,1,0:T(8,128)(2,1)S(1)}, bf16[4,2,144,128]{3,2,1,0:T(8,128)(2,1)S(1)}, u32[]{:S(2)}, u32[]{:S(2)}) collective-permute-start(bf16[4,2,144,128]{3,2,1,0:T(8,128)(2,1)S(1)} %get-tuple-element.19.refs_1_.refs_3_), channel_id=1, source_target_pairs={{0,2},{1,3},{2,0},{3,1},{4,6},{5,7},{6,4},{7,5},{8,10},{9,11},{10,... | collective-permute-start | bytes 884744 | tf_op jit(solution)/shard_map/ppermute | solution.py:400
  30.5 14.1 %collective-permute-start.7 = (bf16[4,2,144,128]{3,2,1,0:T(8,128)(2,1)S(1)}, bf16[4,2,144,128]{3,2,1,0:T(8,128)(2,1)S(1)}, u32[]{:S(2)}, u32[]{:S(2)}) collective-permute-start(bf16[4,2,144,128]{3,2,1,0:T(8,128)(2,1)S(1)} %get-tuple-element.20.refs_0_.refs_2_), channel_id=1, source_target_pairs={{0,4},{1,5},{2,6},{3,7},{4,0},{5,1},{6,2},{7,3},{8,12},{9,13},{10,... | collective-permute-start | bytes 884744 | tf_op jit(solution)/shard_map/ppermute | solution.py:400
  36.6 16.7 %collective-permute-start.10 = (bf16[4,2,144,128]{3,2,1,0:T(8,128)(2,1)S(1)}, bf16[4,2,144,128]{3,2,1,0:T(8,128)(2,1)S(1)}, u32[]{:S(2)}, u32[]{:S(2)}) collective-permute-start(bf16[4,2,144,128]{3,2,1,0:T(8,128)(2,1)S(1)} %collective-permute-done.8.refs_5_.refs_7_), channel_id=1, source_target_pairs={{0,2},{1,3},{2,0},{3,1},{4,6},{5,7},{6,4},{7,5},{8,10},{9,11},{10,... | collective-permute-start | bytes 884744 | tf_op jit(solution)/shard_map/ppermute | solution.py:400
  38.3 15.0 %collective-permute-start.9 = (bf16[4,2,144,128]{3,2,1,0:T(8,128)(2,1)S(1)}, bf16[4,2,144,128]{3,2,1,0:T(8,128)(2,1)S(1)}, u32[]{:S(2)}, u32[]{:S(2)}) collective-permute-start(bf16[4,2,144,128]{3,2,1,0:T(8,128)(2,1)S(1)} %collective-permute-done.5.refs_2_.refs_4_), channel_id=1, source_target_pairs={{0,4},{1,5},{2,6},{3,7},{4,0},{5,1},{6,2},{7,3},{8,12},{9,13},{10,... | collective-permute-start | bytes 884744 | tf_op jit(solution)/shard_map/ppermute | solution.py:400
  53.3 33.0 %copy-start.2 = (s32[32,32]{1,0:T(8,128)S(1)}, s32[32,32]{1,0:T(8,128)}, u32[]{:S(2)}) copy-start(s32[32,32]{1,0:T(8,128)} %present_ref.3) | copy-start | bytes 12292
  53.3 33.0 %copy-start.4 = (bf16[64,144]{1,0:T(8,128)(2,1)S(1)}, bf16[64,144]{1,0:T(8,128)(2,1)}, u32[]{:S(2)}) copy-start(bf16[64,144]{1,0:T(8,128)(2,1)} %wc_ref.1) | copy-start | bytes 55300
  53.3 33.0 %copy-start.5 = (bf16[64,64]{1,0:T(8,128)(2,1)S(1)}, bf16[64,64]{1,0:T(8,128)(2,1)}, u32[]{:S(2)}) copy-start(bf16[64,64]{1,0:T(8,128)(2,1)} %wo_ref.1) | copy-start | bytes 24580
  53.3 33.0 %copy-start.6 = (bf16[64,64]{1,0:T(8,128)(2,1)S(1)}, bf16[64,64]{1,0:T(8,128)(2,1)}, u32[]{:S(2)}) copy-start(bf16[64,64]{1,0:T(8,128)(2,1)} %wout_ref.1) | copy-start | bytes 24580
  53.3 33.0 %copy-start.8 = (s32[32]{0:T(128)S(1)}, s32[32]{0:T(128)}, u32[]{:S(2)}) copy-start(s32[32]{0:T(128)} %param.12) | copy-start | bytes 388
  85.0 1.3 %collective-permute-start.11 = (bf16[256,128]{1,0:T(8,128)(2,1)S(1)}, bf16[256,128]{1,0:T(8,128)(2,1)S(1)}, u32[]{:S(2)}, u32[]{:S(2)}) collective-permute-start(bf16[256,128]{1,0:T(8,128)(2,1)S(1)} %get-tuple-element.18), channel_id=1, source_target_pairs={{0,1},{1,0},{2,3},{3,2},{4,5},{5,4},{6,7},{7,6},{8,9},{9,8},{10,11... | collective-permute-start | bytes 196616 | tf_op jit(solution)/shard_map/ppermute | solution.py:400

commit v5 on v4

--- a/solution.py
+++ b/solution.py
@@ -61,7 +61,7 @@
     return mm(one_hot(col == (row % inner) * outer + row // inner), rows).astype(BF16)
 
 
-def prep_kernel(groups, me_ref, m_ref, present_ref, amino_ref, *refs):
+def prep_kernel(groups, me_ref, m_ref, kept_ref, *refs):
     keep_ref, send_ref, line_ref, normed_ref, spread_ref = refs
     lines, width = m_ref.shape
     pairs = width // 128
@@ -70,7 +70,7 @@
     both = row_shuffle(jnp.concatenate([normed, stacked], axis=1), pairs, lines)
     normed_ref[...] = both[:, :128]
     line_ref[...] = both[:, 128:]
-    kept = (present_ref[...] * amino_ref[...]).astype(F32).astype(BF16)
+    kept = kept_ref[...]
     size = lines // (2 * groups)
     residues = 2 * pairs
     row, col = iota((pairs, residues), 0), iota((pairs, residues), 1)
@@ -94,14 +94,16 @@
 
 def bias_kernel(x_ref, w_ref, after_ref, out_ref, acc_ref):
     step = pl.program_id(0)
-    heads = w_ref.shape[1]
+    heads = w_ref.shape[0]
     per_step, keys, channels = x_ref.shape
     per_tile = 128 // heads
     steps = per_tile // per_step
     centring = block_matrix(2 * channels, channels, 1.0 - 1.0 / channels, -1.0 / channels)
-    averaging = block_matrix(2 * channels, channels, 1.0 / channels, 1.0 / channels)
     lane = iota((channels, 128), 1)
-    wide = mm(w_ref[...], one_hot(iota((heads, 128), 1) % heads == iota((heads, 128), 0)))
+    spread = one_hot(iota((heads, 128), 1) % heads == iota((heads, 128), 0))
+    wide = lax.dot_general(
+        w_ref[...], spread, (((0,), (0,)), ((), ())), preferred_element_type=F32
+    )
     placed = []
     for n in range(per_step):
         mine = lane // heads == (step % steps) * per_step + n
@@ -113,15 +115,15 @@
     def _():
         acc_ref[tile] = jnp.zeros(acc_ref.shape[1:], F32)
 
-    averaging = jnp.concatenate([averaging, averaging], axis=0)
     piece = 512
     for r in range(0, keys, piece):
         normed = []
         for n in range(0, per_step, 2):
             x = jnp.concatenate([x_ref[n, r : r + piece], x_ref[n + 1, r : r + piece]], axis=1)
             centre = mm(x, centring)
-            spread = mm(jnp.concatenate(halves(centre * centre), axis=1), averaging)
-            normed.append((centre * lax.rsqrt(spread + EPS)).astype(BF16))
+            for part in (centre[:, :channels], centre[:, channels:]):
+                spread = jnp.mean(part * part, axis=-1, keepdims=True)
+                normed.append((part * lax.rsqrt(spread + EPS)).astype(BF16))
         acc_ref[tile, r : r + piece, :] += mm(jnp.concatenate(normed, axis=1), placed)
 
     @pl.when(step == pl.num_programs(0) - 1)
@@ -132,8 +134,9 @@
 
 def order_kernel(
     groups, size, pairs, heads, pieces, me_ref, own_ref, peer_ref, keep_ref, received_ref, w_ref,
-    bias_ref, lhs_ref,
+    *refs,
 ):
+    column_refs, (bias_ref, lhs_ref, sums_ref) = refs[:groups], refs[groups:]
     rows, keys = own_ref.shape
     residues = 2 * pairs
     lane = iota((1, keys), 1)
@@ -181,6 +184,7 @@
                 lhs_ref[g * size + s, n * rows : (n + 1) * rows, :] = jnp.where(
                     picked, 1.0, folded
                 ).astype(BF16)
+    add_pieces(groups, size, pairs, (0,), lhs_ref, bias_ref, None, column_refs, sums_ref)
 
 
 def masks_of(ref, size, pairs):
@@ -215,23 +219,28 @@
     return mm(jnp.exp2(logits).astype(BF16), valued)
 
 
-def start_kernel(groups, size, pairs, places, lhs_ref, bias_ref, *refs):
-    out_ref = refs[-1]
-    piece_refs = [refs[n * groups : (n + 1) * groups] for n in range(len(places))]
-    masks = [[masks_of(ref, size, pairs) for ref in piece] for piece in piece_refs]
+def add_pieces(groups, size, pairs, places, lhs_ref, bias_ref, before_ref, piece_refs, out_ref):
+    masks = [masks_of(ref, size, pairs) for ref in piece_refs]
 
     def one_line(s, carry):
         for g in range(groups):
             line = g * size + s
-            total = None
+            total = None if before_ref is None else before_ref[line]
             for n, place in enumerate(places):
-                keyed, valued = keys_of(piece_refs[n][g], masks[n][g], s, pairs)
+                at = n * groups + g
+                keyed, valued = keys_of(piece_refs[at], masks[at], s, pairs)
                 part = partial_sums(lhs_ref[line], bias_ref, place, keyed, valued)
                 total = part if total is None else total + part
             out_ref[line] = total
         return carry
 
     lax.fori_loop(0, size, one_line, 0, unroll=2)
+
+
+def start_kernel(groups, size, pairs, places, lhs_ref, bias_ref, before_ref, *refs):
+    add_pieces(
+        groups, size, pairs, places, lhs_ref, bias_ref, before_ref, refs[:-1], refs[-1]
+    )
 
 
 def finish_kernel(
@@ -321,7 +330,7 @@
 
 
 def final_kernel(
-    lines, heads, with_column, me_ref, line_ref, present_ref, amino_ref, wo_ref, wc_ref, wout_ref,
+    lines, heads, with_column, me_ref, line_ref, kept_ref, wo_ref, wc_ref, wout_ref,
     mine_ref, theirs_ref, out_ref, gated_ref,
 ):
     total = line_ref.shape[0]
@@ -348,8 +357,7 @@
     if not with_column:
         out_ref[...] = row
         return
-    kept_small = (present_ref[...] * amino_ref[...]).astype(F32).astype(BF16)
-    spread = mm(one_hot(iota((total, lines), 0) // pairs == iota((total, lines), 1)), kept_small)
+    spread = mm(one_hot(iota((total, lines), 0) // pairs == iota((total, lines), 1)), kept_ref[...])
     own = iota((total, 2 * pairs), 1) // 2 == iota((total, 2 * pairs), 0) % pairs
     sides = one_hot(iota((2 * pairs, 128), 0) % 2 == iota((2 * pairs, 128), 1) // 64)
     kept = mm(jnp.where(own, spread, 0.0).astype(BF16), sides)
@@ -450,7 +458,7 @@
     keys = res_size * residues
     rows = residues * heads
     core_bit, near, far, high = 1, 2, 4, 8
-    amino_row = amino.reshape(1, residues)
+    kept = (present * amino[None, :]).astype(BF16)
     me = lax.axis_index("res").astype(jnp.int32).reshape(1)
     smem = pl.BlockSpec(memory_space=pltpu.SMEM)
     vmem = pl.BlockSpec(memory_space=pltpu.VMEM)
@@ -461,9 +469,8 @@
         [shape(groups * rest, 128)] * 2 + [shape(lines * pairs, 128)],
         me,
         extra_activations,
-        present,
-        amino_row,
-        in_specs=[smem, vmem, vmem, vmem],
+        kept,
+        in_specs=[smem, vmem, vmem],
         scratch_shapes=[
             pltpu.VMEM((lines * pairs, 128), BF16),
             pltpu.VMEM((2 * groups, pairs, 128), BF16),
@@ -477,55 +484,60 @@
     own = [column[:, :, g] for g in range(groups)]
     beside = [exchange(part, near, res_size) for part in own]
     across = [exchange(part, far, res_size) for part in own]
-    corner = [
-        exchange(beside[g], far, res_size) if g % 2 == 0 else exchange(across[g], near, res_size)
-        for g in range(groups)
-    ]
-
     per_step = 4
     bias = call(
         bias_kernel,
         shape(rows, pair.shape[1]),
         pair,
-        offset_matrix,
+        offset_matrix.T,
         chunk,
         grid=(residues // per_step,),
         in_specs=[
             pl.BlockSpec((per_step,) + pair.shape[1:], lambda n: (n, 0, 0)),
-            pl.BlockSpec(offset_matrix.shape, lambda n: (0, 0)),
+            pl.BlockSpec(offset_matrix.shape[::-1], lambda n: (0, 0)),
             pl.BlockSpec(memory_space=pl.ANY),
         ],
         out_specs=pl.BlockSpec((rows, pair.shape[1]), lambda n: (0, 0)),
         scratch_shapes=[pltpu.VMEM((rows // 128, pair.shape[1], 128), F32)],
         flops=16 * pair.size * 128,
-        mib=16,
+        mib=57,
     )
     if seq_size > 1:
         bias = lax.all_gather(bias, "seq", axis=1, tiled=True)
     pieces = 4
-    bias, lhs = call(
+    bias, lhs, sums = call(
         functools.partial(order_kernel, groups, size, pairs, heads, pieces),
-        [shape(2 * rows, keys, dtype=F32), shape(groups * size, 2 * rows, 128)],
+        [
+            shape(2 * rows, keys, dtype=F32),
+            shape(groups * size, 2 * rows, 128),
+            shape(groups * size, 2 * rows, 128, dtype=F32),
+        ],
         me,
         bias,
         exchange(bias, core_bit, res_size),
         keep,
         received,
         horizontal_matrix,
-        in_specs=[smem] + [vmem] * 5,
-        flops=4 * rows * keys * keys,
-        mib=14,
-    )
+        *own,
+        in_specs=[smem] + [vmem] * (5 + groups),
+        flops=8 * rows * keys * keys,
+        mib=18,
+    )
+    beside[0], across[1], bias = lax.optimization_barrier((beside[0], across[1], bias))
+    corner = [
+        exchange(beside[g], far, res_size) if g % 2 == 0 else exchange(across[g], near, res_size)
+        for g in range(groups)
+    ]
     sums = call(
-        functools.partial(start_kernel, groups, size, pairs, (0, 1, 2)),
+        functools.partial(start_kernel, groups, size, pairs, (1, 2)),
         shape(groups * size, 2 * rows, 128, dtype=F32),
         lhs,
         bias,
-        *own,
+        sums,
         *beside,
         *across,
-        flops=groups * size * rows * keys * 2 * 256 * 2,
-        mib=18,
+        flops=groups * size * rows * keys * 2 * 256 * 4,
+        mib=22,
     )
     anywhere = pl.BlockSpec(memory_space=pl.ANY)
     mine, theirs = call(
@@ -556,8 +568,7 @@
     final_args = [
         me,
         line,
-        present,
-        amino_row,
+        kept,
         horizontal_exit_matrix,
         vertical_matrix,
         vertical_exit_matrix,
@@ -573,7 +584,6 @@
     if with_column:
         return result
     row = result.reshape(lines, residues, hidden)
-    kept = (present * amino_row).astype(BF16)
     moved = lax.all_to_all(row, "seq", split_axis=1, concat_axis=0, tiled=True)
     moved_kept = lax.all_to_all(kept, "seq", split_axis=1, concat_axis=0, tiled=True)
     updated = column_complete(

time: 89.1 us -> 84.6 us (0.949)
  local copies, waits for them, and re-layouts: 6.55 us -> 2.03 us
  waiting for transfers between devices: 9.33 us -> 5.46 us
  Pallas kernels: 59.2 us -> 61.5 us
  other arithmetic: 0.08 us -> 1.71 us
    unnamed x22 -> x15, local copies, waits for them, and re-layouts: 6.5 us -> 1.98 us
    ppermute x12, waiting for transfers between devices: 9.33 us -> 5.46 us  [exchange(): return lax.ppermute(x, 'res', [(d, d ^ flip) for d in range(devices)])]
    pallas_call x6, Pallas kernels: 59.2 us -> 61.5 us  [call(): pl.pallas_call(kernel, out_shape=out_shape, compiler_params=limit, cost_e...]
    another operation x1, other arithmetic: 0.08 us -> 0.99 us  [on_device(): column = jnp.stack(levels).reshape(len(levels), 2, groups, rest, 128)]
  transfers between devices with their start and end apart: 12 -> 12, of which waited for: 5 -> 4; matrix products, arithmetic and copies ran while one was open for 1% -> 1% of each run, Pallas kernels for 27% -> 30%
where the time goes in v5:
time: 84.6 us; the launch traced here: 84.3 us
  Pallas kernels  61.5 us (73%)
  starting transfers between devices  13.5 us (16%)
  waiting for transfers between devices  5.46 us (6%)
  local copies, waits for them, and re-layouts  2.03 us (2%)
  other arithmetic  1.71 us (2%)
    pallas_call x6, Pallas kernels, call(): pl.pallas_call(kernel, out_shape=out_shape, compiler_params=limit, cost_e...  61.5 us
    ppermute x12, starting transfers between devices, exchange(): return lax.ppermute(x, 'res', [(d, d ^ flip) for d in range(devices)])  13.5 us
    ppermute x12, waiting for transfers between devices, exchange(): return lax.ppermute(x, 'res', [(d, d ^ flip) for d in range(devices)])  5.46 us
    unnamed x15, local copies, waits for them, and re-layouts  1.98 us
  transfers between devices with their start and end apart: 12, of which 4 were waited for; matrix products, arithmetic and copies ran while one was open for 1% of the time, Pallas kernels for 30%

profile of v5, /device:TPU:0, one launch (start us, length us, event | category | flops | bytes accessed | tf_op | source)
XLA Modules:
  0.0 84.3 jit_solution(14262336367341472772)
XLA Ops:
  0.0 0.7 multiply_convert_fusion.kept_ref
  0.7 0.9 %copy-done = bf16[32,2048]{1,0:T(8,128)(2,1)S(1)} copy-done((bf16[32,2048]{1,0:T(8,128)(2,1)S(1)}, bf16[32,2048]{1,0:T(8,128)(2,1)}, u32[]{:S(2)}) %copy-start) | copy-done | bytes 131096
  1.6 1.2 %shard_map.91 = (bf16[288,128]{1,0:T(8,128)(2,1)S(1)}, bf16[288,128]{1,0:T(8,128)(2,1)S(1)}, bf16[512,128]{1,0:T(8,128)(2,1)S(1)}) custom-call(s32[1]{0:T(128)} %bitcast.me_ref, bf16[32,2048]{1,0:T(8,128)(2,1)S(1)} %copy-done, bf16[32,32]{1,0:T(8,128)(2,1)S(1)} %multiply_convert_fusion.kept_ref), custom_call_target="tpu_custom_call" | custom-call | bytes 133124 | tf_op jit(solution)/shard_map/pallas_call | solution.py:398
  2.8 0.5 collective-permute-start
  3.3 0.9 %collective-permute-done.received_ref = bf16[288,128]{1,0:T(8,128)(2,1)S(1)} collective-permute-done((bf16[288,128]{1,0:T(8,128)(2,1)S(1)}, bf16[288,128]{1,0:T(8,128)(2,1)S(1)}, u32[]{:S(2)}, u32[]{:S(2)}) %collective-permute-start) | collective-permute-done | bytes 73760 | tf_op jit(solution)/shard_map/ppermute | solution.py:408
  4.3 5.0 %collective-permute-start.4 = (bf16[576,128]{1,0:T(8,128)(2,1)S(1)}, bf16[576,128]{1,0:T(8,128)(2,1)S(1)}, u32[]{:S(2)}, u32[]{:S(2)}) collective-permute-start(bf16[576,128]{1,0:T(8,128)(2,1)S(1)} %constant_dynamic-update-slice_fusion.after_ref), channel_id=1, source_target_pairs={{0,24},{1,25},{2,26},{3,27},{4,28},{5,29},{6,30},{7,31},{8,16},{9,... | collective-permute-start | bytes 442376 | tf_op jit(solution)/shard_map/ppermute | solution.py:408
  9.3 0.0 collective-permute-start.3
  9.3 0.6 collective-permute-start.2
  9.9 12.9 %shard_map.92.own_ref = bf16[256,1024]{1,0:T(8,128)(2,1)} custom-call(bf16[32,1024,128]{2,1,0:T(8,128)(2,1)} %x_ref.1, bf16[8,128]{1,0:T(8,128)(2,1)} %bitcast.18, bf16[576,128]{1,0:T(8,128)(2,1)} %copy-done.6), custom_call_target="tpu_custom_call" | custom-call | flops 8589934592 | bytes 8538112 | tf_op jit(solution)/shard_map/pallas_call | solution.py:398
  22.9 0.0 collective-permute-done.4
  22.9 0.0 collective-permute-done.3
  22.9 1.0 %pad_maximum_fusion = bf16[4,2,2,144,128]{4,3,2,1,0:T(8,128)(2,1)S(1)} fusion(bf16[1,2,2,144,128]{4,3,2,1,0:T(8,128)(2,1)S(1)} %bitcast.15, bf16[1,2,2,144,128]{4,3,2,1,0:T(8,128)(2,1)S(1)} %bitcast.16, bf16[1,2,2,144,128]{4,3,2,1,0:T(8,128)(2,1)S(1)} %bitcast.17, bf16[1,2,2,144,128]{4,3,2,1,0:T(8,128)(2,1)} %bitcast.14), kind=kLoop, calls=%fused_computation | loop fusion | flops 884736 | bytes 1179648 | tf_op jit(solution)/shard_map/stack | solution.py:483
  23.9 1.8 %collective-permute-start.6 = (bf16[4,2,144,128]{3,2,1,0:T(8,128)(2,1)S(1)}, bf16[4,2,144,128]{3,2,1,0:T(8,128)(2,1)S(1)}, u32[]{:S(2)}, u32[]{:S(2)}) collective-permute-start(bf16[4,2,144,128]{3,2,1,0:T(8,128)(2,1)S(1)} %get-tuple-element.27.refs_1_.refs_3_), channel_id=1, source_target_pairs={{0,4},{1,5},{2,6},{3,7},{4,0},{5,1},{6,2},{7,3},{8,12},{9,13},{10,... | collective-permute-start | bytes 884744 | tf_op jit(solution)/shard_map/ppermute | solution.py:408
  25.7 1.5 %collective-permute-start.5 = (bf16[4,2,144,128]{3,2,1,0:T(8,128)(2,1)S(1)}, bf16[4,2,144,128]{3,2,1,0:T(8,128)(2,1)S(1)}, u32[]{:S(2)}, u32[]{:S(2)}) collective-permute-start(bf16[4,2,144,128]{3,2,1,0:T(8,128)(2,1)S(1)} %get-tuple-element.28.refs_0_.refs_2_), channel_id=1, source_target_pairs={{0,2},{1,3},{2,0},{3,1},{4,6},{5,7},{6,4},{7,5},{8,10},{9,11},{10,... | collective-permute-start | bytes 884744 | tf_op jit(solution)/shard_map/ppermute | solution.py:408
  27.2 0.5 collective-permute-start.7
  27.7 0.3 collective-permute-start.8
  28.1 1.0 %copy-done.5 = bf16[256,1024]{1,0:T(8,128)(2,1)S(1)} copy-done((bf16[256,1024]{1,0:T(8,128)(2,1)S(1)}, bf16[256,1024]{1,0:T(8,128)(2,1)}, u32[]{:S(2)}) %copy-start.5) | copy-done | bytes 524312
  29.1 6.3 %shard_map.93 = (f32[512,1024]{1,0:T(8,128)S(1)}, bf16[16,512,128]{2,1,0:T(8,128)(2,1)S(1)}, f32[16,512,128]{2,1,0:T(8,128)S(1)}) custom-call(s32[1]{0:T(128)} %bitcast.me_ref, bf16[256,1024]{1,0:T(8,128)(2,1)S(1)} %copy-done.5, bf16[256,1024]{1,0:T(8,128)(2,1)S(1)} %collective-permute-done.1.peer_ref, bf16[288,128]{1,0:T(8,128)(2,1)S(1)} %get-tuple-element.17.keep_ref, ...), custom_call_target="tpu_custom_call" | custom-call | flops 2147483648 | bytes 1818628 | tf_op jit(solution)/shard_map/pallas_call | solution.py:398
  35.4 0.0 collective-permute-done.6.refs_3_.refs_7_
  35.4 0.1 collective-permute-done.5.refs_0_.refs_4_
  35.5 1.7 %collective-permute-start.9 = (bf16[4,2,144,128]{3,2,1,0:T(8,128)(2,1)S(1)}, bf16[4,2,144,128]{3,2,1,0:T(8,128)(2,1)S(1)}, u32[]{:S(2)}, u32[]{:S(2)}) collective-permute-start(bf16[4,2,144,128]{3,2,1,0:T(8,128)(2,1)S(1)} %collective-permute-done.5.refs_0_.refs_4_), channel_id=1, source_target_pairs={{0,4},{1,5},{2,6},{3,7},{4,0},{5,1},{6,2},{7,3},{8,12},{9,13},{10,... | collective-permute-start | bytes 884744 | tf_op jit(solution)/shard_map/ppermute | solution.py:408
  37.2 1.5 %collective-permute-start.10 = (bf16[4,2,144,128]{3,2,1,0:T(8,128)(2,1)S(1)}, bf16[4,2,144,128]{3,2,1,0:T(8,128)(2,1)S(1)}, u32[]{:S(2)}, u32[]{:S(2)}) collective-permute-start(bf16[4,2,144,128]{3,2,1,0:T(8,128)(2,1)S(1)} %collective-permute-done.6.refs_3_.refs_7_), channel_id=1, source_target_pairs={{0,2},{1,3},{2,0},{3,1},{4,6},{5,7},{6,4},{7,5},{8,10},{9,11},{10,... | collective-permute-start | bytes 884744 | tf_op jit(solution)/shard_map/ppermute | solution.py:408
  38.7 3.2 %collective-permute-done.7.refs_1_.refs_5_ = bf16[4,2,144,128]{3,2,1,0:T(8,128)(2,1)S(1)} collective-permute-done((bf16[4,2,144,128]{3,2,1,0:T(8,128)(2,1)S(1)}, bf16[4,2,144,128]{3,2,1,0:T(8,128)(2,1)S(1)}, u32[]{:S(2)}, u32[]{:S(2)}) %collective-permute-start.7) | collective-permute-done | bytes 294944 | tf_op jit(solution)/shard_map/ppermute | solution.py:408
  41.8 0.0 collective-permute-done.8.refs_2_.refs_6_
  41.8 5.8 %shard_map.94.sums_ref = f32[16,512,128]{2,1,0:T(8,128)S(1)} custom-call(bf16[16,512,128]{2,1,0:T(8,128)(2,1)S(1)} %get-tuple-element.19.lhs_ref, f32[512,1024]{1,0:T(8,128)S(1)} %get-tuple-element.21.bias_ref, f32[16,512,128]{2,1,0:T(8,128)S(1)} %get-tuple-element.22.before_ref, bf16[4,2,144,128]{3,2,1,0:T(8,128)(2,1)S(1)} %collective-permute-done.5.refs_0_.refs_4_, ...), custom_call_target="tpu_custom_call" | custom-call | flops 8589934592 | bytes 9568256 | tf_op jit(solution)/shard_map/pallas_call | solution.py:398
  47.7 0.0 copy-start.2
  47.7 0.0 copy-start.3
  47.7 0.0 copy-start.4
  47.8 32.7 %shard_map.95 = (bf16[256,128]{1,0:T(8,128)(2,1)S(1)}, bf16[256,128]{1,0:T(8,128)(2,1)S(1)}) custom-call(bf16[16,512,128]{2,1,0:T(8,128)(2,1)S(1)} %get-tuple-element.19.lhs_ref, f32[512,1024]{1,0:T(8,128)S(1)} %get-tuple-element.21.bias_ref, f32[16,512,128]{2,1,0:T(8,128)S(1)} %shard_map.94.sums_ref, bf16[64,256]{1,0:T(8,128)(2,1)S(1)} %copy-done.1, ...), custom_call_target="tpu_custom_call" | custom-call | flops 2147483648 | bytes 10928128 | tf_op jit(solution)/shard_map/pallas_call | solution.py:398
  80.5 0.1 collective-permute-start.11
  80.5 1.2 %collective-permute-done.11.theirs_ref = bf16[256,128]{1,0:T(8,128)(2,1)S(1)} collective-permute-done((bf16[256,128]{1,0:T(8,128)(2,1)S(1)}, bf16[256,128]{1,0:T(8,128)(2,1)S(1)}, u32[]{:S(2)}, u32[]{:S(2)}) %collective-permute-start.11) | collective-permute-done | bytes 65568 | tf_op jit(solution)/shard_map/ppermute | solution.py:408
  81.8 2.6 %shard_map.96 = bf16[32,2048]{1,0:T(8,128)(2,1)} custom-call(s32[1]{0:T(128)} %bitcast.me_ref, bf16[512,128]{1,0:T(8,128)(2,1)S(1)} %get-tuple-element.16.line_ref, bf16[32,32]{1,0:T(8,128)(2,1)S(1)} %multiply_convert_fusion.kept_ref, bf16[64,64]{1,0:T(8,128)(2,1)S(1)} %copy-done.3, bf16[64,144]{1,0:T(8,128)(2,1)S(1)} %copy-done.2, ...), custom_call_target="tpu_custom_call" | custom-call | bytes 299012 | tf_op jit(solution)/shard_map/pallas_call | solution.py:398
  (17 shorter events, 0.1 us)
Async XLA Ops:
  0.7 0.9 %copy-start = (bf16[32,2048]{1,0:T(8,128)(2,1)S(1)}, bf16[32,2048]{1,0:T(8,128)(2,1)}, u32[]{:S(2)}) copy-start(bf16[32,2048]{1,0:T(8,128)(2,1)} %m_ref.1) | copy-start | bytes 393220
  2.8 1.4 %collective-permute-start = (bf16[288,128]{1,0:T(8,128)(2,1)S(1)}, bf16[288,128]{1,0:T(8,128)(2,1)S(1)}, u32[]{:S(2)}, u32[]{:S(2)}) collective-permute-start(bf16[288,128]{1,0:T(8,128)(2,1)S(1)} %get-tuple-element.18), channel_id=1, source_target_pairs={{0,1},{1,0},{2,3},{3,2},{4,5},{5,4},{6,7},{7,6},{8,9},{9,8},{10,11... | collective-permute-start | bytes 221192 | tf_op jit(solution)/shard_map/ppermute | solution.py:408
  4.2 5.7 %copy-start.6 = (bf16[576,128]{1,0:T(8,128)(2,1)}, bf16[576,128]{1,0:T(8,128)(2,1)S(1)}, u32[]{:S(2)}) copy-start(bf16[576,128]{1,0:T(8,128)(2,1)S(1)} %constant_dynamic-update-slice_fusion.after_ref) | copy-start | bytes 442372
  4.3 18.6 %collective-permute-start.4 = (bf16[576,128]{1,0:T(8,128)(2,1)S(1)}, bf16[576,128]{1,0:T(8,128)(2,1)S(1)}, u32[]{:S(2)}, u32[]{:S(2)}) collective-permute-start(bf16[576,128]{1,0:T(8,128)(2,1)S(1)} %constant_dynamic-update-slice_fusion.after_ref), channel_id=1, source_target_pairs={{0,24},{1,25},{2,26},{3,27},{4,28},{5,29},{6,30},{7,31},{8,16},{9,... | collective-permute-start | bytes 442376 | tf_op jit(solution)/shard_map/ppermute | solution.py:408
  9.3 13.6 %collective-permute-start.3 = (bf16[576,128]{1,0:T(8,128)(2,1)S(1)}, bf16[576,128]{1,0:T(8,128)(2,1)S(1)}, u32[]{:S(2)}, u32[]{:S(2)}) collective-permute-start(bf16[576,128]{1,0:T(8,128)(2,1)S(1)} %constant_dynamic-update-slice_fusion.after_ref), channel_id=1, source_target_pairs={{0,16},{1,17},{2,18},{3,19},{4,20},{5,21},{6,22},{7,23},{8,24},{9,... | collective-permute-start | bytes 442376 | tf_op jit(solution)/shard_map/ppermute | solution.py:408
  9.3 13.6 %collective-permute-start.2 = (bf16[576,128]{1,0:T(8,128)(2,1)S(1)}, bf16[576,128]{1,0:T(8,128)(2,1)S(1)}, u32[]{:S(2)}, u32[]{:S(2)}) collective-permute-start(bf16[576,128]{1,0:T(8,128)(2,1)S(1)} %constant_dynamic-update-slice_fusion.after_ref), channel_id=1, source_target_pairs={{0,8},{1,9},{2,10},{3,11},{4,12},{5,13},{6,14},{7,15},{8,0},{9,1},... | collective-permute-start | bytes 442376 | tf_op jit(solution)/shard_map/ppermute | solution.py:408
  9.9 18.1 %copy-start.1 = (bf16[64,256]{1,0:T(8,128)(2,1)S(1)}, bf16[64,256]{1,0:T(8,128)(2,1)}, u32[]{:S(2)}) copy-start(bf16[64,256]{1,0:T(8,128)(2,1)} %w_ref.3) | copy-start | bytes 98308
  22.9 5.2 %collective-permute-start.1 = (bf16[256,1024]{1,0:T(8,128)(2,1)}, bf16[256,1024]{1,0:T(8,128)(2,1)S(1)}, u32[]{:S(2)}, u32[]{:S(2)}) collective-permute-start(bf16[256,1024]{1,0:T(8,128)(2,1)} %shard_map.92.own_ref), channel_id=1, source_target_pairs={{0,1},{1,0},{2,3},{3,2},{4,5},{5,4},{6,7},{7,6},{8,9},{9,8},{10,11... | collective-permute-start | bytes 1572872 | tf_op jit(solution)/shard_map/ppermute | solution.py:408
  23.9 11.5 %collective-permute-start.6 = (bf16[4,2,144,128]{3,2,1,0:T(8,128)(2,1)S(1)}, bf16[4,2,144,128]{3,2,1,0:T(8,128)(2,1)S(1)}, u32[]{:S(2)}, u32[]{:S(2)}) collective-permute-start(bf16[4,2,144,128]{3,2,1,0:T(8,128)(2,1)S(1)} %get-tuple-element.27.refs_1_.refs_3_), channel_id=1, source_target_pairs={{0,4},{1,5},{2,6},{3,7},{4,0},{5,1},{6,2},{7,3},{8,12},{9,13},{10,... | collective-permute-start | bytes 884744 | tf_op jit(solution)/shard_map/ppermute | solution.py:408
  25.7 9.8 %collective-permute-start.5 = (bf16[4,2,144,128]{3,2,1,0:T(8,128)(2,1)S(1)}, bf16[4,2,144,128]{3,2,1,0:T(8,128)(2,1)S(1)}, u32[]{:S(2)}, u32[]{:S(2)}) collective-permute-start(bf16[4,2,144,128]{3,2,1,0:T(8,128)(2,1)S(1)} %get-tuple-element.28.refs_0_.refs_2_), channel_id=1, source_target_pairs={{0,2},{1,3},{2,0},{3,1},{4,6},{5,7},{6,4},{7,5},{8,10},{9,11},{10,... | collective-permute-start | bytes 884744 | tf_op jit(solution)/shard_map/ppermute | solution.py:408
  27.2 14.7 %collective-permute-start.7 = (bf16[4,2,144,128]{3,2,1,0:T(8,128)(2,1)S(1)}, bf16[4,2,144,128]{3,2,1,0:T(8,128)(2,1)S(1)}, u32[]{:S(2)}, u32[]{:S(2)}) collective-permute-start(bf16[4,2,144,128]{3,2,1,0:T(8,128)(2,1)S(1)} %get-tuple-element.27.refs_1_.refs_3_), channel_id=1, source_target_pairs={{0,2},{1,3},{2,0},{3,1},{4,6},{5,7},{6,4},{7,5},{8,10},{9,11},{10,... | collective-permute-start | bytes 884744 | tf_op jit(solution)/shard_map/ppermute | solution.py:408
  27.7 14.1 %collective-permute-start.8 = (bf16[4,2,144,128]{3,2,1,0:T(8,128)(2,1)S(1)}, bf16[4,2,144,128]{3,2,1,0:T(8,128)(2,1)S(1)}, u32[]{:S(2)}, u32[]{:S(2)}) collective-permute-start(bf16[4,2,144,128]{3,2,1,0:T(8,128)(2,1)S(1)} %get-tuple-element.28.refs_0_.refs_2_), channel_id=1, source_target_pairs={{0,4},{1,5},{2,6},{3,7},{4,0},{5,1},{6,2},{7,3},{8,12},{9,13},{10,... | collective-permute-start | bytes 884744 | tf_op jit(solution)/shard_map/ppermute | solution.py:408
  28.0 1.0 %copy-start.5 = (bf16[256,1024]{1,0:T(8,128)(2,1)S(1)}, bf16[256,1024]{1,0:T(8,128)(2,1)}, u32[]{:S(2)}) copy-start(bf16[256,1024]{1,0:T(8,128)(2,1)} %shard_map.92.own_ref) | copy-start | bytes 1572868
  35.5 12.2 %collective-permute-start.9 = (bf16[4,2,144,128]{3,2,1,0:T(8,128)(2,1)S(1)}, bf16[4,2,144,128]{3,2,1,0:T(8,128)(2,1)S(1)}, u32[]{:S(2)}, u32[]{:S(2)}) collective-permute-start(bf16[4,2,144,128]{3,2,1,0:T(8,128)(2,1)S(1)} %collective-permute-done.5.refs_0_.refs_4_), channel_id=1, source_target_pairs={{0,4},{1,5},{2,6},{3,7},{4,0},{5,1},{6,2},{7,3},{8,12},{9,13},{10,... | collective-permute-start | bytes 884744 | tf_op jit(solution)/shard_map/ppermute | solution.py:408
  37.2 10.6 %collective-permute-start.10 = (bf16[4,2,144,128]{3,2,1,0:T(8,128)(2,1)S(1)}, bf16[4,2,144,128]{3,2,1,0:T(8,128)(2,1)S(1)}, u32[]{:S(2)}, u32[]{:S(2)}) collective-permute-start(bf16[4,2,144,128]{3,2,1,0:T(8,128)(2,1)S(1)} %collective-permute-done.6.refs_3_.refs_7_), channel_id=1, source_target_pairs={{0,2},{1,3},{2,0},{3,1},{4,6},{5,7},{6,4},{7,5},{8,10},{9,11},{10,... | collective-permute-start | bytes 884744 | tf_op jit(solution)/shard_map/ppermute | solution.py:408
  47.7 34.1 %copy-start.2 = (bf16[64,144]{1,0:T(8,128)(2,1)S(1)}, bf16[64,144]{1,0:T(8,128)(2,1)}, u32[]{:S(2)}) copy-start(bf16[64,144]{1,0:T(8,128)(2,1)} %wc_ref.1) | copy-start | bytes 55300
  47.7 34.1 %copy-start.3 = (bf16[64,64]{1,0:T(8,128)(2,1)S(1)}, bf16[64,64]{1,0:T(8,128)(2,1)}, u32[]{:S(2)}) copy-start(bf16[64,64]{1,0:T(8,128)(2,1)} %wo_ref.1) | copy-start | bytes 24580
  47.7 34.0 %copy-start.4 = (bf16[64,64]{1,0:T(8,128)(2,1)S(1)}, bf16[64,64]{1,0:T(8,128)(2,1)}, u32[]{:S(2)}) copy-start(bf16[64,64]{1,0:T(8,128)(2,1)} %wout_ref.1) | copy-start | bytes 24580
  80.5 1.3 %collective-permute-start.11 = (bf16[256,128]{1,0:T(8,128)(2,1)S(1)}, bf16[256,128]{1,0:T(8,128)(2,1)S(1)}, u32[]{:S(2)}, u32[]{:S(2)}) collective-permute-start(bf16[256,128]{1,0:T(8,128)(2,1)S(1)} %get-tuple-element.26), channel_id=1, source_target_pairs={{0,1},{1,0},{2,3},{3,2},{4,5},{5,4},{6,7},{7,6},{8,9},{9,8},{10,11... | collective-permute-start | bytes 196616 | tf_op jit(solution)/shard_map/ppermute | solution.py:408

commit v6 on v5

--- a/solution.py
+++ b/solution.py
@@ -76,46 +76,51 @@
     row, col = iota((pairs, residues), 0), iota((pairs, residues), 1)
     evens, odds = one_hot(col == 2 * row), one_hot(col == 2 * row + 1)
     row, col = iota((128, lines), 0) - 64, iota((128, lines), 1)
+    core = me_ref[0] % 2
     for n in range(2 * groups):
-        chosen = (row >= 0) & (row < 2 * size) & (row % size == col - n * size)
+        start = jnp.where(n // groups == core, 0, 2 * size)
+        chosen = (row >= start) & (row < start + 2 * size) & (row % size == col - n * size)
         spread = mm(one_hot(chosen), kept).astype(BF16)
-        first = iota((pairs, 128), 1) < 64 + size
+        first = iota((pairs, 128), 1) < 64 + size + start
         spread_ref[n] = jnp.where(first, mm_nt(evens, spread), mm_nt(odds, spread)).astype(BF16)
-    core = me_ref[0] % 2
     rows = size * pairs
     for ref, half in ((keep_ref, core), (send_ref, 1 - core)):
         for g in range(groups):
-            index, start = half * groups + g, g * (rows + pairs)
-            ref[start : start + rows, :] = normed_ref[
-                pl.ds(pl.multiple_of(index * rows, rows), rows), :
-            ]
-            ref[start + rows : start + rows + pairs, :] = spread_ref[index]
-
-
-def bias_kernel(x_ref, w_ref, after_ref, out_ref, acc_ref):
+            index = half * groups + g
+            ref[g, :rows] = normed_ref[pl.ds(pl.multiple_of(index * rows, rows), rows), :]
+            ref[g, rows:] = spread_ref[index]
+
+
+def bias_kernel(whole, pieces, x_ref, w_ref, after_ref, me_ref, *refs):
+    outs, (acc_ref, centring_ref, wide_ref) = refs[:-3], refs[-3:]
     step = pl.program_id(0)
     heads = w_ref.shape[0]
     per_step, keys, channels = x_ref.shape
-    per_tile = 128 // heads
-    steps = per_tile // per_step
-    centring = block_matrix(2 * channels, channels, 1.0 - 1.0 / channels, -1.0 / channels)
-    lane = iota((channels, 128), 1)
-    spread = one_hot(iota((heads, 128), 1) % heads == iota((heads, 128), 0))
-    wide = lax.dot_general(
-        w_ref[...], spread, (((0,), (0,)), ((), ())), preferred_element_type=F32
-    )
+    residues = per_step * pl.num_programs(0)
+    pairs = residues // 2
+    tiles = acc_ref.shape[0]
+    width = tiles * 128
+
+    @pl.when(step == 0)
+    def _():
+        centring_ref[...] = block_matrix(
+            2 * channels, channels, 1.0 - 1.0 / channels, -1.0 / channels
+        )
+        spread = one_hot(iota((heads, 1), 0) == iota((1, width), 1) // residues)
+        wide_ref[...] = lax.dot_general(
+            w_ref[...], spread, (((0,), (0,)), ((), ())), preferred_element_type=F32
+        )
+        acc_ref[...] = jnp.zeros(acc_ref.shape, F32)
+
+    lane = iota((1, width), 1) % residues
     placed = []
     for n in range(per_step):
-        mine = lane // heads == (step % steps) * per_step + n
-        placed.append(jnp.where(mine, wide, 0.0).astype(BF16))
+        residue = step * per_step + n
+        mine = lane == (residue % 2) * pairs + residue // 2
+        placed.append(jnp.where(mine, wide_ref[...], 0.0).astype(BF16))
     placed = jnp.concatenate(placed, axis=0)
-    tile = step // steps
-
-    @pl.when(step % steps == 0)
-    def _():
-        acc_ref[tile] = jnp.zeros(acc_ref.shape[1:], F32)
-
-    piece = 512
+    centring = centring_ref[...]
+    piece = min(512, keys)
     for r in range(0, keys, piece):
         normed = []
         for n in range(0, per_step, 2):
@@ -124,86 +129,122 @@
             for part in (centre[:, :channels], centre[:, channels:]):
                 spread = jnp.mean(part * part, axis=-1, keepdims=True)
                 normed.append((part * lax.rsqrt(spread + EPS)).astype(BF16))
-        acc_ref[tile, r : r + piece, :] += mm(jnp.concatenate(normed, axis=1), placed)
+        added = mm(jnp.concatenate(normed, axis=1), placed)
+        for n in range(tiles):
+            acc_ref[n, r : r + piece, :] += added[:, n * 128 : (n + 1) * 128]
 
     @pl.when(step == pl.num_programs(0) - 1)
     def _():
-        for n in range(acc_ref.shape[0]):
-            out_ref[n * 128 : (n + 1) * 128, :] = acc_ref[n].T.astype(BF16)
-
-
-def order_kernel(
-    groups, size, pairs, heads, pieces, me_ref, own_ref, peer_ref, keep_ref, received_ref, w_ref,
-    *refs,
-):
-    column_refs, (bias_ref, lhs_ref, sums_ref) = refs[:groups], refs[groups:]
-    rows, keys = own_ref.shape
-    residues = 2 * pairs
+        if not whole:
+            for n in range(tiles):
+                outs[0][n * 128 : (n + 1) * 128, :] = acc_ref[n].T.astype(BF16)
+            return
+        levels = keys // (2 * pieces * residues)
+        for flip in range(2):
+            user = me_ref[0] ^ flip
+            starts = [
+                (user ^ (c + 2 * q + 2 * pieces * k)) * residues + p
+                for q in range(pieces)
+                for p in range(2)
+                for k in range(levels)
+                for c in range(2)
+            ]
+            for n in range(tiles):
+                for at in range(0, keys, 128):
+                    rows = [
+                        acc_ref[n, pl.ds(start, pairs, stride=2), :]
+                        for start in starts[at // pairs : (at + 128) // pairs]
+                    ]
+                    turned = jnp.concatenate(rows, axis=0).T.astype(BF16)
+                    if flip == 0:
+                        turned = turned.astype(F32) * LOG2E
+                    outs[flip][n * 128 : (n + 1) * 128, at : at + 128] = turned
+
+
+def order_kernel(residues, pieces, me_ref, bias_ref, own_ref, send_ref):
+    rows, keys = bias_ref.shape
+    pairs = residues // 2
     lane = iota((1, keys), 1)
     each = keys // pieces
     which, rest = lane // each, lane % each
     parity, rest = rest // (each // 2), rest % (each // 2)
     place, pair = rest // pairs, rest % pairs
-    device = me_ref[0] ^ ((place % 2) + 2 * which + 2 * pieces * (place // 2))
-    target = device * residues + 2 * pair + parity
-    total = jnp.zeros((2 * rows, keys), F32)
-    for start in range(0, keys, 256):
-        chosen = one_hot(iota((256, keys), 0) + start == target)
-        both = jnp.concatenate(
-            [own_ref[:, start : start + 256], peer_ref[:, start : start + 256]], axis=0
-        )
-        total = total + mm(both, chosen)
-    bias_ref[...] = total * LOG2E
+    for flip, out_ref in enumerate((own_ref, send_ref)):
+        device = me_ref[0] ^ flip ^ ((place % 2) + 2 * which + 2 * pieces * (place // 2))
+        target = device * residues + 2 * pair + parity
+        total = jnp.zeros((rows, keys), F32)
+        for start in range(0, keys, 256):
+            chosen = one_hot(iota((256, keys), 0) + start == target)
+            total = total + mm(bias_ref[:, start : start + 256], chosen)
+        out_ref[...] = total * LOG2E if flip == 0 else total.astype(BF16)
+
+
+def query_kernel(
+    groups, size, pairs, heads, own_ref, peer_ref, keep_ref, received_ref, w_ref, *refs
+):
+    column_refs, (bias_ref, lhs_ref, sums_ref) = refs[:groups], refs[groups:]
+    rows = own_ref.shape[0]
+    bias_ref[:rows, :] = own_ref[...]
+    bias_ref[rows:, :] = peer_ref[...].astype(F32) * LOG2E
 
     hidden = w_ref.shape[0]
     depth = hidden // heads
-    row, col = iota((128, hidden), 0), iota((128, hidden), 1)
-    twice_rows = one_hot(row % hidden == col)
-    row, col = iota((4 * hidden, 128), 0), iota((4 * hidden, 128), 1)
-    wq = mm(mm(twice_rows, w_ref[...]).astype(BF16), one_hot(row == col % hidden))
-    row, col = iota((128, 128), 0), iota((128, 128), 1)
-    wq = jnp.where(row // hidden == col // hidden, wq, 0.0).astype(BF16)
-    row, col = iota((128, 4 * hidden), 0), iota((128, 4 * hidden), 1)
-    wk = mm_nt(one_hot(col == hidden + row % hidden), w_ref[...]).astype(BF16)
-    row, col = iota((hidden, 128), 0), iota((hidden, 128), 1)
-    wk = mm(wk, one_hot(row == col)).astype(BF16)
-    lane, row = iota((2 * heads, 128), 1), iota((2 * heads, 128), 0)
-    own_head = jnp.where(lane // depth == row, 1.0, 0.0)[None]
+    twice_rows = one_hot(iota((128, 1), 0) % hidden == iota((1, hidden), 1))
+    wq = mm(
+        mm(twice_rows, w_ref[...]).astype(BF16),
+        one_hot(iota((4 * hidden, 1), 0) == iota((1, 128), 1) % hidden),
+    )
+    same_residue = iota((128, 1), 0) // hidden == iota((1, 128), 1) // hidden
+    wq = jnp.where(same_residue, wq, 0.0).astype(BF16)
+    picked = one_hot(iota((1, 4 * hidden), 1) == hidden + iota((128, 1), 0) % hidden)
+    wk = mm_nt(picked, w_ref[...]).astype(BF16)
+    wk = mm(wk, one_hot(iota((hidden, 1), 0) == iota((1, 128), 1))).astype(BF16)
     lead = size * pairs
-    lane = iota((rows, 128), 1) - hidden
+    lane = iota((1, 128), 1)
+    spare = lane - hidden
     for g in range(groups):
         for n, ref in enumerate((keep_ref, received_ref)):
-            start = g * (lead + pairs)
-            query = mm(ref[start : start + lead, :], wq) * (depth**-0.5)
-            query = query.astype(BF16).astype(F32)
+            query = (mm(ref[g, :lead], wq) * (depth**-0.5)).astype(BF16).astype(F32)
             for s in range(size):
                 q = query[s * pairs : (s + 1) * pairs]
-                spread = (q[:, None, :] * own_head).reshape(rows, 128).astype(BF16)
-                folded = mm(spread, wk) * LOG2E
-                picked = (lane == s) | (lane == size + s)
+                spread = [
+                    jnp.where(lane // depth == p * heads + h, q, 0.0).astype(BF16)
+                    for h in range(heads)
+                    for p in range(2)
+                ]
+                folded = mm(jnp.concatenate(spread, axis=0), wk) * LOG2E
+                picks = (spare >= 0) & (spare < 4 * size) & (spare % size == s)
                 lhs_ref[g * size + s, n * rows : (n + 1) * rows, :] = jnp.where(
-                    picked, 1.0, folded
+                    picks, 1.0, folded
                 ).astype(BF16)
-    add_pieces(groups, size, pairs, (0,), lhs_ref, bias_ref, None, column_refs, sums_ref)
+    add_pieces(groups, size, pairs, (0,) * groups, lhs_ref, bias_ref, None, column_refs, sums_ref)
 
 
 def masks_of(ref, size, pairs):
-    lead = size * pairs
-    present = jnp.concatenate(
-        [ref[k, c, lead : lead + pairs, :] for k in range(ref.shape[0]) for c in range(2)], axis=0
-    ).astype(F32)
-    lane = iota(present.shape, 1) - 64
-    hidden = (1e9 * LOG2E) * (present - 1.0)
-    return [
-        jnp.where((lane >= p * size) & (lane < (p + 1) * size), hidden, 0.0).astype(BF16)
-        for p in range(2)
-    ]
-
-
-def keys_of(ref, masks, s, pairs):
+    start = 2 * size * pairs
+    lane = iota((1, 128), 1) - 64
+    masks = []
+    for p in range(2):
+        blocks = []
+        for k in range(ref.shape[0]):
+            hidden = (1e9 * LOG2E) * (ref[k, start : start + pairs, :].astype(F32) - 1.0)
+            for c in range(2):
+                first = (2 * c + p) * size
+                mine = (lane >= first) & (lane < first + size)
+                blocks.append(jnp.where(mine, hidden, 0.0).astype(BF16))
+        masks.append(jnp.concatenate(blocks, axis=0))
+    return masks
+
+
+def keys_of(ref, masks, s, size, pairs):
     start = pl.multiple_of(s * pairs, pairs)
     even = jnp.concatenate(
-        [ref[k, c, pl.ds(start, pairs), :] for k in range(ref.shape[0]) for c in range(2)], axis=0
+        [
+            ref[k, pl.ds(c * size * pairs + start, pairs), :]
+            for k in range(ref.shape[0])
+            for c in range(2)
+        ],
+        axis=0,
     )
     odd = pltpu.roll(even.astype(F32), 64, 1).astype(BF16)
     low = iota(even.shape, 1) < 64
@@ -225,19 +266,15 @@
     def one_line(s, carry):
         for g in range(groups):
             line = g * size + s
-            total = None if before_ref is None else before_ref[line]
-            for n, place in enumerate(places):
-                at = n * groups + g
-                keyed, valued = keys_of(piece_refs[at], masks[at], s, pairs)
-                part = partial_sums(lhs_ref[line], bias_ref, place, keyed, valued)
-                total = part if total is None else total + part
-            out_ref[line] = total
+            keyed, valued = keys_of(piece_refs[g], masks[g], s, size, pairs)
+            total = partial_sums(lhs_ref[line], bias_ref, places[g], keyed, valued)
+            out_ref[line] = total if before_ref is None else before_ref[line] + total
         return carry
 
     lax.fori_loop(0, size, one_line, 0, unroll=2)
 
 
-def start_kernel(groups, size, pairs, places, lhs_ref, bias_ref, before_ref, *refs):
+def add_kernel(groups, size, pairs, places, lhs_ref, bias_ref, before_ref, *refs):
     add_pieces(
         groups, size, pairs, places, lhs_ref, bias_ref, before_ref, refs[:-1], refs[-1]
     )
@@ -248,42 +285,49 @@
     *refs,
 ):
     piece_refs, far_refs = refs[:groups], refs[groups : 4 * groups]
-    mine_ref, theirs_ref, attended_ref, range_ref, copy_ref = refs[4 * groups :]
+    mine_ref, theirs_ref, high_ref, low_ref, range_ref, copy_ref = refs[4 * groups :]
     hidden = w_ref.shape[0]
     depth = hidden // heads
     lead = size * pairs
-    row, col = iota((4 * hidden, 128), 0), iota((4 * hidden, 128), 1)
-    pick_value = one_hot(row == 2 * hidden + col % hidden)
-    pick_gate = one_hot(row == 3 * hidden + col % hidden)
-    row, col = iota((128, hidden), 0), iota((128, hidden), 1)
-    wv = mm(mm(one_hot(row == col), w_ref[...]).astype(BF16), pick_value).astype(BF16)
-    wg = mm(mm(one_hot(row % hidden == col), w_ref[...]).astype(BF16), pick_gate)
-    row, col = iota((128, 128), 0), iota((128, 128), 1)
-    wg = jnp.where(row // hidden == col // hidden, wg, 0.0).astype(BF16)
-    lane, row = iota((2 * heads, 128), 1), iota((2 * heads, 128), 0)
-    own_head = jnp.where(lane // depth == row, 1.0, 0.0)[None]
+    blocks = 2 * heads
+    row, col = iota((128, 1), 0), iota((1, 256), 1)
+    picked = one_hot(iota((4 * hidden, 1), 0) == 2 * hidden + col % hidden)
+    picked = jnp.where(col < 128, picked, jnp.zeros_like(picked))
+    wv = mm(mm(one_hot(row == iota((1, hidden), 1)), w_ref[...]).astype(BF16), picked)
+    counted = (row >= hidden) & (col >= 128)
+    wv = jnp.where(counted, 1.0 / (128 - hidden), wv)
+    owner = col % 128 // depth
+    wv = jnp.concatenate(
+        [
+            jnp.where(owner == p * heads + h, wv, 0.0).astype(BF16)
+            for h in range(heads)
+            for p in range(2)
+        ],
+        axis=0,
+    )
+    lane = iota((1, 128), 1)
+    wg = mm(
+        mm(one_hot(row % hidden == iota((1, hidden), 1)), w_ref[...]).astype(BF16),
+        one_hot(iota((4 * hidden, 1), 0) == 3 * hidden + lane % hidden),
+    )
+    wg = jnp.where(row // hidden == lane // hidden, wg, 0.0).astype(BF16)
     masks = [masks_of(ref, size, pairs) for ref in piece_refs]
     low = iota((lhs_ref.shape[1], 128), 1) < 64
-    row, col = iota((128, 1), 0), iota((1, 128), 1)
-    averaged = jnp.where(row + 0 * col < hidden, 0.0, 1.0 / (128 - hidden)).astype(BF16)
-    wv = jnp.concatenate([wv, averaged], axis=1)
-    wv = jnp.concatenate([wv, wv], axis=0)
-    own_head = jnp.concatenate([own_head, own_head], axis=2)
 
     def settle(line, total):
-        mixed = mm(jnp.concatenate(halves(total), axis=1), wv)
-        summed = jnp.sum(mixed.reshape(2 * pairs, 2 * heads, 256) * own_head, axis=1)
-        summed = summed[:, :128] / summed[:, 128:]
         start = pl.multiple_of(line * pairs, pairs)
-        for n in range(2):
-            attended_ref[n, pl.ds(start, pairs), :] = summed[n * pairs : (n + 1) * pairs]
+        for ref, part in zip((high_ref, low_ref), halves(total)):
+            for n in range(2):
+                for b in range(blocks):
+                    at = (n * blocks + b) * pairs
+                    ref[n, pl.ds(start, pairs), b * 128 : (b + 1) * 128] = part[at : at + pairs]
 
     range_ref[...] = jnp.ones(range_ref.shape, F32)
 
     def one_line(s, carry):
         for g in range(groups):
             line = g * size + s
-            keyed, valued = keys_of(piece_refs[g], masks[g], s, pairs)
+            keyed, valued = keys_of(piece_refs[g], masks[g], s, size, pairs)
             total = sums_ref[line] + partial_sums(lhs_ref[line], bias_ref, place, keyed, valued)
             settle(line, total)
             weight = jnp.where(low, 1.0, total).reshape(-1, 8, 128)
@@ -304,7 +348,7 @@
 
             def exact_line(s, carry):
                 line = g * size + s
-                both = [keys_of(r, m, s, pairs) for r, m in zip(ordered, all_masks)]
+                both = [keys_of(r, m, s, size, pairs) for r, m in zip(ordered, all_masks)]
                 logits = []
                 for n, (keyed, _) in enumerate(both):
                     width = keyed.shape[0]
@@ -322,11 +366,12 @@
             lax.fori_loop(0, size, exact_line, 0)
 
     for n, (ref, out_ref) in enumerate(((keep_ref, mine_ref), (received_ref, theirs_ref))):
+        mixed = mm(high_ref[n], wv) + mm(low_ref[n], wv)
+        mixed = mixed[:, :128] / mixed[:, 128:]
         for g in range(groups):
-            start = g * (lead + pairs)
-            gate = jax.nn.sigmoid(mm(ref[start : start + lead, :], wg))
+            gate = jax.nn.sigmoid(mm(ref[g, :lead], wg))
             at = slice(g * lead, (g + 1) * lead)
-            out_ref[at, :] = (gate * attended_ref[n, at, :]).astype(BF16)
+            out_ref[at, :] = (gate * mixed[at]).astype(BF16)
 
 
 def final_kernel(
@@ -466,7 +511,7 @@
     rest = lead + pairs
     keep, send, line = call(
         functools.partial(prep_kernel, groups),
-        [shape(groups * rest, 128)] * 2 + [shape(lines * pairs, 128)],
+        [shape(groups, rest, 128)] * 2 + [shape(lines * pairs, 128)],
         me,
         extra_activations,
         kept,
@@ -478,67 +523,89 @@
     )
 
     received = exchange(send, core_bit, res_size)
-    chunk = jnp.concatenate([keep, received], axis=0)
+    chunk = jnp.concatenate(
+        [keep[:, :lead], received[:, :lead], keep[:, lead:] + received[:, lead:]], axis=1
+    )
     levels = [chunk] + [exchange(chunk, high * k, res_size) for k in range(1, res_size // high)]
-    column = jnp.stack(levels).reshape(len(levels), 2, groups, rest, 128)
-    own = [column[:, :, g] for g in range(groups)]
+    own = [jnp.stack([level[g] for level in levels]) for g in range(groups)]
     beside = [exchange(part, near, res_size) for part in own]
     across = [exchange(part, far, res_size) for part in own]
-    per_step = 4
+
+    per_step = 8
+    pieces = 4
+    whole = seq_size == 1
+    bias_rows = [shape(rows, keys, dtype=F32), shape(rows, keys)]
     bias = call(
-        bias_kernel,
-        shape(rows, pair.shape[1]),
+        functools.partial(bias_kernel, whole, pieces),
+        bias_rows if whole else [shape(rows, pair.shape[1])],
         pair,
         offset_matrix.T,
         chunk,
+        me,
         grid=(residues // per_step,),
         in_specs=[
             pl.BlockSpec((per_step,) + pair.shape[1:], lambda n: (n, 0, 0)),
             pl.BlockSpec(offset_matrix.shape[::-1], lambda n: (0, 0)),
             pl.BlockSpec(memory_space=pl.ANY),
+            smem,
         ],
-        out_specs=pl.BlockSpec((rows, pair.shape[1]), lambda n: (0, 0)),
-        scratch_shapes=[pltpu.VMEM((rows // 128, pair.shape[1], 128), F32)],
+        out_specs=[pl.BlockSpec((rows, pair.shape[1]), lambda n: (0, 0))] * (1 + whole),
+        scratch_shapes=[
+            pltpu.VMEM((rows // 128, pair.shape[1], 128), F32),
+            pltpu.VMEM((2 * pair.shape[2], 2 * pair.shape[2]), BF16),
+            pltpu.VMEM((pair.shape[2], rows), F32),
+        ],
         flops=16 * pair.size * 128,
         mib=57,
     )
-    if seq_size > 1:
-        bias = lax.all_gather(bias, "seq", axis=1, tiled=True)
-    pieces = 4
+    if not whole:
+        bias = call(
+            functools.partial(order_kernel, residues, pieces),
+            bias_rows,
+            me,
+            lax.all_gather(bias[0], "seq", axis=1, tiled=True),
+            in_specs=[smem, vmem],
+            mib=14,
+        )
     bias, lhs, sums = call(
-        functools.partial(order_kernel, groups, size, pairs, heads, pieces),
+        functools.partial(query_kernel, groups, size, pairs, heads),
         [
             shape(2 * rows, keys, dtype=F32),
             shape(groups * size, 2 * rows, 128),
             shape(groups * size, 2 * rows, 128, dtype=F32),
         ],
-        me,
-        bias,
-        exchange(bias, core_bit, res_size),
+        bias[0],
+        exchange(bias[1], core_bit, res_size),
         keep,
         received,
         horizontal_matrix,
         *own,
-        in_specs=[smem] + [vmem] * (5 + groups),
+        in_specs=[vmem] * (5 + groups),
         flops=8 * rows * keys * keys,
         mib=18,
     )
-    beside[0], across[1], bias = lax.optimization_barrier((beside[0], across[1], bias))
+
+    def add(sums, places, parts):
+        return call(
+            functools.partial(add_kernel, groups, size, pairs, places),
+            shape(*sums.shape, dtype=F32),
+            lhs,
+            bias,
+            sums,
+            *parts,
+            flops=groups * size * rows * keys * 2 * 256 * 2,
+            mib=20,
+        )
+
+    beside[0], across[1], sums = lax.optimization_barrier((beside[0], across[1], sums))
     corner = [
         exchange(beside[g], far, res_size) if g % 2 == 0 else exchange(across[g], near, res_size)
         for g in range(groups)
     ]
-    sums = call(
-        functools.partial(start_kernel, groups, size, pairs, (1, 2)),
-        shape(groups * size, 2 * rows, 128, dtype=F32),
-        lhs,
-        bias,
-        sums,
-        *beside,
-        *across,
-        flops=groups * size * rows * keys * 2 * 256 * 4,
-        mib=22,
-    )
+    sums = add(sums, (1, 2), (beside[0], across[1]))
+    beside[1], across[0], sums = lax.optimization_barrier((beside[1], across[0], sums))
+    sums = add(sums, (2, 1), (across[0], beside[1]))
+    corner[0], corner[1], sums = lax.optimization_barrier((corner[0], corner[1], sums))
     anywhere = pl.BlockSpec(memory_space=pl.ANY)
     mine, theirs = call(
         functools.partial(finish_kernel, heads, groups, size, pairs, 3),
@@ -555,12 +622,13 @@
         *across,
         in_specs=[vmem] * (6 + groups) + [anywhere] * (3 * groups),
         scratch_shapes=[
-            pltpu.VMEM((2, groups * lead, 128), F32),
+            pltpu.VMEM((2, groups * lead, 128 * 2 * heads), BF16),
+            pltpu.VMEM((2, groups * lead, 128 * 2 * heads), BF16),
             pltpu.VMEM((2, 8, 128), F32),
             pltpu.VMEM((3 * groups,) + own[0].shape, BF16),
         ],
         flops=groups * size * rows * keys * 2 * 256,
-        mib=22,
+        mib=24,
     )
     returned = exchange(theirs, core_bit, res_size)
 

time: 84.6 us -> 76.4 us (0.903)
  Pallas kernels: 61.5 us -> 54.8 us
  waiting for transfers between devices: 5.46 us -> 4.32 us
  local copies, waits for them, and re-layouts: 2.03 us -> 3.12 us
  other arithmetic: 1.71 us -> 0.81 us
    pallas_call x6 -> x7, Pallas kernels: 61.5 us -> 54.8 us  [call(): pl.pallas_call(kernel, out_shape=out_shape, compiler_params=limit, cost_e...]
    ppermute x12, waiting for transfers between devices: 5.46 us -> 4.32 us  [exchange(): return lax.ppermute(x, 'res', [(d, d ^ flip) for d in range(devices)])]
    slice x0 -> x6, local copies, waits for them, and re-layouts: none -> 0.97 us  [the longest x4 0.96 us: on_device(): own = [jnp.stack([level[g] for level in levels]) for g in range(groups)]]
    another operation x1 -> x2, other arithmetic: 0.99 us -> 0.08 us  [on_device(): own = [jnp.stack([level[g] for level in levels]) for g in range(groups)]]
    unnamed x15 -> x14, local copies, waits for them, and re-layouts: 1.98 us -> 2.15 us
  transfers between devices with their start and end apart: 12 -> 12, of which waited for: 4 -> 5; matrix products, arithmetic and copies ran while one was open for 1% -> 1% of each run, Pallas kernels for 30% -> 29%
where the time goes in v6:
time: 76.4 us; the launch traced here: 76 us
  Pallas kernels  54.8 us (72%)
  starting transfers between devices  12.9 us (17%)
  waiting for transfers between devices  4.32 us (6%)
  local copies, waits for them, and re-layouts  3.12 us (4%)
  other arithmetic  0.81 us (1%)
    pallas_call x7, Pallas kernels, call(): pl.pallas_call(kernel, out_shape=out_shape, compiler_params=limit, cost_e...  54.8 us
    ppermute x12, starting transfers between devices, exchange(): return lax.ppermute(x, 'res', [(d, d ^ flip) for d in range(devices)])  12.9 us
    ppermute x12, waiting for transfers between devices, exchange(): return lax.ppermute(x, 'res', [(d, d ^ flip) for d in range(devices)])  4.32 us
    unnamed x14, local copies, waits for them, and re-layouts  2.15 us
  transfers between devices with their start and end apart: 12, of which 5 were waited for; matrix products, arithmetic and copies ran while one was open for 1% of the time, Pallas kernels for 29%

profile of v6, /device:TPU:0, one launch (start us, length us, event | category | flops | bytes accessed | tf_op | source)
XLA Modules:
  0.0 76.0 jit_solution(2738193287967899108)
XLA Ops:
  0.0 0.7 multiply_convert_fusion.kept_ref
  0.7 0.9 %copy-done = bf16[32,2048]{1,0:T(8,128)(2,1)S(1)} copy-done((bf16[32,2048]{1,0:T(8,128)(2,1)S(1)}, bf16[32,2048]{1,0:T(8,128)(2,1)}, u32[]{:S(2)}) %copy-start) | copy-done | bytes 131096
  1.6 1.2 %shard_map.91 = (bf16[2,144,128]{2,1,0:T(8,128)(2,1)S(1)}, bf16[2,144,128]{2,1,0:T(8,128)(2,1)S(1)}, bf16[512,128]{1,0:T(8,128)(2,1)S(1)}) custom-call(s32[1]{0:T(128)} %bitcast.me_ref, bf16[32,2048]{1,0:T(8,128)(2,1)S(1)} %copy-done, bf16[32,32]{1,0:T(8,128)(2,1)S(1)} %multiply_convert_fusion.kept_ref), custom_call_target="tpu_custom_call" | custom-call | bytes 133124 | tf_op jit(solution)/shard_map/pallas_call | solution.py:443
  2.8 0.5 collective-permute-start
  3.3 0.9 %collective-permute-done.received_ref = bf16[2,144,128]{2,1,0:T(8,128)(2,1)S(1)} collective-permute-done((bf16[2,144,128]{2,1,0:T(8,128)(2,1)S(1)}, bf16[2,144,128]{2,1,0:T(8,128)(2,1)S(1)}, u32[]{:S(2)}, u32[]{:S(2)}) %collective-permute-start) | collective-permute-done | bytes 73760 | tf_op jit(solution)/shard_map/ppermute | solution.py:453
  4.3 5.0 %collective-permute-start.4 = (bf16[2,272,128]{2,1,0:T(8,128)(2,1)S(1)}, bf16[2,272,128]{2,1,0:T(8,128)(2,1)S(1)}, u32[]{:S(2)}, u32[]{:S(2)}) collective-permute-start(bf16[2,272,128]{2,1,0:T(8,128)(2,1)S(1)} %pad_maximum_fusion.2.after_ref), channel_id=1, source_target_pairs={{0,24},{1,25},{2,26},{3,27},{4,28},{5,29},{6,30},{7,31},{8,16},{9,... | collective-permute-start | bytes 417800 | tf_op jit(solution)/shard_map/ppermute | solution.py:453
  9.3 0.6 collective-permute-start.2
  9.9 9.4 %shard_map.92 = (f32[256,1024]{1,0:T(8,128)}, bf16[256,1024]{1,0:T(8,128)(2,1)}) custom-call(bf16[32,1024,128]{2,1,0:T(8,128)(2,1)} %x_ref.1, bf16[8,128]{1,0:T(8,128)(2,1)} %bitcast.2, bf16[2,272,128]{2,1,0:T(8,128)(2,1)} %copy-done.6, s32[1]{0:T(128)} %bitcast.me_ref), custom_call_target="tpu_custom_call" | custom-call | flops 8589934592 | bytes 8529924 | tf_op jit(solution)/shard_map/pallas_call | solution.py:443
  19.3 0.0 collective-permute-start.1
  19.3 0.9 %fusion = (bf16[1,272,128]{2,1,0:T(8,128)(2,1)S(1)}, bf16[1,272,128]{2,1,0:T(8,128)(2,1)S(1)}) fusion(bf16[2,272,128]{2,1,0:T(8,128)(2,1)} %copy-done.6), kind=kLoop, calls=%fused_computation.5 | loop fusion | bytes 278528 | tf_op jit(solution)/shard_map/slice | solution.py:530
  20.3 1.1 %collective-permute-done.3 = bf16[2,272,128]{2,1,0:T(8,128)(2,1)S(1)} collective-permute-done((bf16[2,272,128]{2,1,0:T(8,128)(2,1)S(1)}, bf16[2,272,128]{2,1,0:T(8,128)(2,1)S(1)}, u32[]{:S(2)}, u32[]{:S(2)}) %collective-permute-start.3) | collective-permute-done | bytes 139296 | tf_op jit(solution)/shard_map/ppermute | solution.py:453
  21.5 1.6 %collective-permute-start.5 = (bf16[4,272,128]{2,1,0:T(8,128)(2,1)S(1)}, bf16[4,272,128]{2,1,0:T(8,128)(2,1)S(1)}, u32[]{:S(2)}, u32[]{:S(2)}) collective-permute-start(bf16[4,272,128]{2,1,0:T(8,128)(2,1)S(1)} %pad_maximum_fusion.refs_0_.refs_2_), channel_id=1, source_target_pairs={{0,2},{1,3},{2,0},{3,1},{4,6},{5,7},{6,4},{7,5},{8,10},{9,11},{10,... | collective-permute-start | bytes 835592 | tf_op jit(solution)/shard_map/ppermute | solution.py:453
  23.1 1.6 %collective-permute-start.6 = (bf16[4,272,128]{2,1,0:T(8,128)(2,1)S(1)}, bf16[4,272,128]{2,1,0:T(8,128)(2,1)S(1)}, u32[]{:S(2)}, u32[]{:S(2)}) collective-permute-start(bf16[4,272,128]{2,1,0:T(8,128)(2,1)S(1)} %pad_maximum_fusion.1.refs_1_.refs_3_), channel_id=1, source_target_pairs={{0,4},{1,5},{2,6},{3,7},{4,0},{5,1},{6,2},{7,3},{8,12},{9,13},{10,... | collective-permute-start | bytes 835592 | tf_op jit(solution)/shard_map/ppermute | solution.py:453
  24.7 0.5 collective-permute-start.10
  25.2 0.5 collective-permute-start.9
  25.7 1.2 %copy-done.5 = f32[256,1024]{1,0:T(8,128)S(1)} copy-done((f32[256,1024]{1,0:T(8,128)S(1)}, f32[256,1024]{1,0:T(8,128)}, u32[]{:S(2)}) %copy-start.5) | copy-done | bytes 1048600
  26.9 5.2 %shard_map.93 = (f32[512,1024]{1,0:T(8,128)S(1)}, bf16[16,512,128]{2,1,0:T(8,128)(2,1)S(1)}, f32[16,512,128]{2,1,0:T(8,128)S(1)}) custom-call(f32[256,1024]{1,0:T(8,128)S(1)} %copy-done.5, bf16[256,1024]{1,0:T(8,128)(2,1)S(1)} %collective-permute-done.1.peer_ref, bf16[2,144,128]{2,1,0:T(8,128)(2,1)S(1)} %get-tuple-element.25.keep_ref, ...), custom_call_target="tpu_custom_call" | custom-call | flops 2147483648 | bytes 2310144 | tf_op jit(solution)/shard_map/pallas_call | solution.py:443
  32.1 0.0 collective-permute-done.5.refs_0_.refs_4_
  32.1 0.6 collective-permute-done.6.refs_1_.refs_7_
  32.7 1.5 %collective-permute-start.7 = (bf16[4,272,128]{2,1,0:T(8,128)(2,1)S(1)}, bf16[4,272,128]{2,1,0:T(8,128)(2,1)S(1)}, u32[]{:S(2)}, u32[]{:S(2)}) collective-permute-start(bf16[4,272,128]{2,1,0:T(8,128)(2,1)S(1)} %collective-permute-done.5.refs_0_.refs_4_), channel_id=1, source_target_pairs={{0,4},{1,5},{2,6},{3,7},{4,0},{5,1},{6,2},{7,3},{8,12},{9,13},{10,... | collective-permute-start | bytes 835592 | tf_op jit(solution)/shard_map/ppermute | solution.py:453
  34.3 0.9 %collective-permute-start.8 = (bf16[4,272,128]{2,1,0:T(8,128)(2,1)S(1)}, bf16[4,272,128]{2,1,0:T(8,128)(2,1)S(1)}, u32[]{:S(2)}, u32[]{:S(2)}) collective-permute-start(bf16[4,272,128]{2,1,0:T(8,128)(2,1)S(1)} %collective-permute-done.6.refs_1_.refs_7_), channel_id=1, source_target_pairs={{0,2},{1,3},{2,0},{3,1},{4,6},{5,7},{6,4},{7,5},{8,10},{9,11},{10,... | collective-permute-start | bytes 835592 | tf_op jit(solution)/shard_map/ppermute | solution.py:453
  35.2 3.6 %shard_map.94.before_ref = f32[16,512,128]{2,1,0:T(8,128)S(1)} custom-call(bf16[16,512,128]{2,1,0:T(8,128)(2,1)S(1)} %get-tuple-element.29.lhs_ref, f32[512,1024]{1,0:T(8,128)S(1)} %get-tuple-element.30.bias_ref, f32[16,512,128]{2,1,0:T(8,128)S(1)} %get-tuple-element.34.before_ref, bf16[4,272,128]{2,1,0:T(8,128)(2,1)S(1)} %collective-permute-done.5.refs_0_.refs_4_, ...), custom_call_target="tpu_custom_call" | custom-call | flops 4294967296 | bytes 8945664 | tf_op jit(solution)/shard_map/pallas_call | solution.py:443
  38.9 3.6 %shard_map.95.sums_ref = f32[16,512,128]{2,1,0:T(8,128)S(1)} custom-call(bf16[16,512,128]{2,1,0:T(8,128)(2,1)S(1)} %get-tuple-element.29.lhs_ref, f32[512,1024]{1,0:T(8,128)S(1)} %get-tuple-element.30.bias_ref, f32[16,512,128]{2,1,0:T(8,128)S(1)} %shard_map.94.before_ref, bf16[4,272,128]{2,1,0:T(8,128)(2,1)S(1)} %collective-permute-done.10.refs_0_.refs_6_, ...), custom_call_target="tpu_custom_call" | custom-call | flops 4294967296 | bytes 8945664 | tf_op jit(solution)/shard_map/pallas_call | solution.py:443
  42.5 0.0 copy-start.2
  42.5 0.0 copy-start.3
  42.5 0.0 copy-start.4
  42.5 0.4 collective-permute-done.7.refs_0_
  42.9 0.0 collective-permute-done.8.refs_1_
  42.9 29.2 %shard_map.96 = (bf16[256,128]{1,0:T(8,128)(2,1)S(1)}, bf16[256,128]{1,0:T(8,128)(2,1)S(1)}) custom-call(bf16[16,512,128]{2,1,0:T(8,128)(2,1)S(1)} %get-tuple-element.29.lhs_ref, f32[512,1024]{1,0:T(8,128)S(1)} %get-tuple-element.30.bias_ref, f32[16,512,128]{2,1,0:T(8,128)S(1)} %shard_map.95.sums_ref, bf16[64,256]{1,0:T(8,128)(2,1)S(1)} %copy-done.1, ...), custom_call_target="tpu_custom_call" | custom-call | flops 2147483648 | bytes 10797056 | tf_op jit(solution)/shard_map/pallas_call | solution.py:443
  72.2 0.1 collective-permute-start.11
  72.2 1.2 %collective-permute-done.11.theirs_ref = bf16[256,128]{1,0:T(8,128)(2,1)S(1)} collective-permute-done((bf16[256,128]{1,0:T(8,128)(2,1)S(1)}, bf16[256,128]{1,0:T(8,128)(2,1)S(1)}, u32[]{:S(2)}, u32[]{:S(2)}) %collective-permute-start.11) | collective-permute-done | bytes 65568 | tf_op jit(solution)/shard_map/ppermute | solution.py:453
  73.5 2.6 %shard_map.97 = bf16[32,2048]{1,0:T(8,128)(2,1)} custom-call(s32[1]{0:T(128)} %bitcast.me_ref, bf16[512,128]{1,0:T(8,128)(2,1)S(1)} %get-tuple-element.24.line_ref, bf16[32,32]{1,0:T(8,128)(2,1)S(1)} %multiply_convert_fusion.kept_ref, bf16[64,64]{1,0:T(8,128)(2,1)S(1)} %copy-done.3, bf16[64,144]{1,0:T(8,128)(2,1)S(1)} %copy-done.2, ...), custom_call_target="tpu_custom_call" | custom-call | bytes 299012 | tf_op jit(solution)/shard_map/pallas_call | solution.py:443
  (24 shorter events, 0.2 us)
Async XLA Ops:
  0.7 0.9 %copy-start = (bf16[32,2048]{1,0:T(8,128)(2,1)S(1)}, bf16[32,2048]{1,0:T(8,128)(2,1)}, u32[]{:S(2)}) copy-start(bf16[32,2048]{1,0:T(8,128)(2,1)} %m_ref.1) | copy-start | bytes 393220
  2.8 1.4 %collective-permute-start = (bf16[2,144,128]{2,1,0:T(8,128)(2,1)S(1)}, bf16[2,144,128]{2,1,0:T(8,128)(2,1)S(1)}, u32[]{:S(2)}, u32[]{:S(2)}) collective-permute-start(bf16[2,144,128]{2,1,0:T(8,128)(2,1)S(1)} %get-tuple-element.26), channel_id=1, source_target_pairs={{0,1},{1,0},{2,3},{3,2},{4,5},{5,4},{6,7},{7,6},{8,9},{9,8},{10,11... | collective-permute-start | bytes 221192 | tf_op jit(solution)/shard_map/ppermute | solution.py:453
  4.3 5.7 %copy-start.6 = (bf16[2,272,128]{2,1,0:T(8,128)(2,1)}, bf16[2,272,128]{2,1,0:T(8,128)(2,1)S(1)}, u32[]{:S(2)}) copy-start(bf16[2,272,128]{2,1,0:T(8,128)(2,1)S(1)} %pad_maximum_fusion.2.after_ref) | copy-start | bytes 417796
  4.3 16.0 %collective-permute-start.4 = (bf16[2,272,128]{2,1,0:T(8,128)(2,1)S(1)}, bf16[2,272,128]{2,1,0:T(8,128)(2,1)S(1)}, u32[]{:S(2)}, u32[]{:S(2)}) collective-permute-start(bf16[2,272,128]{2,1,0:T(8,128)(2,1)S(1)} %pad_maximum_fusion.2.after_ref), channel_id=1, source_target_pairs={{0,24},{1,25},{2,26},{3,27},{4,28},{5,29},{6,30},{7,31},{8,16},{9,... | collective-permute-start | bytes 417800 | tf_op jit(solution)/shard_map/ppermute | solution.py:453
  9.3 12.1 %collective-permute-start.3 = (bf16[2,272,128]{2,1,0:T(8,128)(2,1)S(1)}, bf16[2,272,128]{2,1,0:T(8,128)(2,1)S(1)}, u32[]{:S(2)}, u32[]{:S(2)}) collective-permute-start(bf16[2,272,128]{2,1,0:T(8,128)(2,1)S(1)} %pad_maximum_fusion.2.after_ref), channel_id=1, source_target_pairs={{0,16},{1,17},{2,18},{3,19},{4,20},{5,21},{6,22},{7,23},{8,24},{9,... | collective-permute-start | bytes 417800 | tf_op jit(solution)/shard_map/ppermute | solution.py:453
  9.3 12.1 %collective-permute-start.2 = (bf16[2,272,128]{2,1,0:T(8,128)(2,1)S(1)}, bf16[2,272,128]{2,1,0:T(8,128)(2,1)S(1)}, u32[]{:S(2)}, u32[]{:S(2)}) collective-permute-start(bf16[2,272,128]{2,1,0:T(8,128)(2,1)S(1)} %pad_maximum_fusion.2.after_ref), channel_id=1, source_target_pairs={{0,8},{1,9},{2,10},{3,11},{4,12},{5,13},{6,14},{7,15},{8,0},{9,1},... | collective-permute-start | bytes 417800 | tf_op jit(solution)/shard_map/ppermute | solution.py:453
  9.9 15.8 %copy-start.1 = (bf16[64,256]{1,0:T(8,128)(2,1)S(1)}, bf16[64,256]{1,0:T(8,128)(2,1)}, u32[]{:S(2)}) copy-start(bf16[64,256]{1,0:T(8,128)(2,1)} %w_ref.3) | copy-start | bytes 98308
  19.3 6.4 %collective-permute-start.1 = (bf16[256,1024]{1,0:T(8,128)(2,1)}, bf16[256,1024]{1,0:T(8,128)(2,1)S(1)}, u32[]{:S(2)}, u32[]{:S(2)}) collective-permute-start(bf16[256,1024]{1,0:T(8,128)(2,1)} %get-tuple-element.28), channel_id=1, source_target_pairs={{0,1},{1,0},{2,3},{3,2},{4,5},{5,4},{6,7},{7,6},{8,9},{9,8},{10,11... | collective-permute-start | bytes 1572872 | tf_op jit(solution)/shard_map/ppermute | solution.py:453
  21.5 10.6 %collective-permute-start.5 = (bf16[4,272,128]{2,1,0:T(8,128)(2,1)S(1)}, bf16[4,272,128]{2,1,0:T(8,128)(2,1)S(1)}, u32[]{:S(2)}, u32[]{:S(2)}) collective-permute-start(bf16[4,272,128]{2,1,0:T(8,128)(2,1)S(1)} %pad_maximum_fusion.refs_0_.refs_2_), channel_id=1, source_target_pairs={{0,2},{1,3},{2,0},{3,1},{4,6},{5,7},{6,4},{7,5},{8,10},{9,11},{10,... | collective-permute-start | bytes 835592 | tf_op jit(solution)/shard_map/ppermute | solution.py:453
  23.1 9.7 %collective-permute-start.6 = (bf16[4,272,128]{2,1,0:T(8,128)(2,1)S(1)}, bf16[4,272,128]{2,1,0:T(8,128)(2,1)S(1)}, u32[]{:S(2)}, u32[]{:S(2)}) collective-permute-start(bf16[4,272,128]{2,1,0:T(8,128)(2,1)S(1)} %pad_maximum_fusion.1.refs_1_.refs_3_), channel_id=1, source_target_pairs={{0,4},{1,5},{2,6},{3,7},{4,0},{5,1},{6,2},{7,3},{8,12},{9,13},{10,... | collective-permute-start | bytes 835592 | tf_op jit(solution)/shard_map/ppermute | solution.py:453
  24.7 14.2 %collective-permute-start.10 = (bf16[4,272,128]{2,1,0:T(8,128)(2,1)S(1)}, bf16[4,272,128]{2,1,0:T(8,128)(2,1)S(1)}, u32[]{:S(2)}, u32[]{:S(2)}) collective-permute-start(bf16[4,272,128]{2,1,0:T(8,128)(2,1)S(1)} %pad_maximum_fusion.refs_0_.refs_2_), channel_id=1, source_target_pairs={{0,4},{1,5},{2,6},{3,7},{4,0},{5,1},{6,2},{7,3},{8,12},{9,13},{10,... | collective-permute-start | bytes 835592 | tf_op jit(solution)/shard_map/ppermute | solution.py:453
  25.2 13.7 %collective-permute-start.9 = (bf16[4,272,128]{2,1,0:T(8,128)(2,1)S(1)}, bf16[4,272,128]{2,1,0:T(8,128)(2,1)S(1)}, u32[]{:S(2)}, u32[]{:S(2)}) collective-permute-start(bf16[4,272,128]{2,1,0:T(8,128)(2,1)S(1)} %pad_maximum_fusion.1.refs_1_.refs_3_), channel_id=1, source_target_pairs={{0,2},{1,3},{2,0},{3,1},{4,6},{5,7},{6,4},{7,5},{8,10},{9,11},{10,... | collective-permute-start | bytes 835592 | tf_op jit(solution)/shard_map/ppermute | solution.py:453
  25.7 1.2 %copy-start.5 = (f32[256,1024]{1,0:T(8,128)S(1)}, f32[256,1024]{1,0:T(8,128)}, u32[]{:S(2)}) copy-start(f32[256,1024]{1,0:T(8,128)} %get-tuple-element.27.own_ref) | copy-start | bytes 3145732
  32.7 10.2 %collective-permute-start.7 = (bf16[4,272,128]{2,1,0:T(8,128)(2,1)S(1)}, bf16[4,272,128]{2,1,0:T(8,128)(2,1)S(1)}, u32[]{:S(2)}, u32[]{:S(2)}) collective-permute-start(bf16[4,272,128]{2,1,0:T(8,128)(2,1)S(1)} %collective-permute-done.5.refs_0_.refs_4_), channel_id=1, source_target_pairs={{0,4},{1,5},{2,6},{3,7},{4,0},{5,1},{6,2},{7,3},{8,12},{9,13},{10,... | collective-permute-start | bytes 835592 | tf_op jit(solution)/shard_map/ppermute | solution.py:453
  34.3 8.7 %collective-permute-start.8 = (bf16[4,272,128]{2,1,0:T(8,128)(2,1)S(1)}, bf16[4,272,128]{2,1,0:T(8,128)(2,1)S(1)}, u32[]{:S(2)}, u32[]{:S(2)}) collective-permute-start(bf16[4,272,128]{2,1,0:T(8,128)(2,1)S(1)} %collective-permute-done.6.refs_1_.refs_7_), channel_id=1, source_target_pairs={{0,2},{1,3},{2,0},{3,1},{4,6},{5,7},{6,4},{7,5},{8,10},{9,11},{10,... | collective-permute-start | bytes 835592 | tf_op jit(solution)/shard_map/ppermute | solution.py:453
  42.5 31.0 %copy-start.2 = (bf16[64,144]{1,0:T(8,128)(2,1)S(1)}, bf16[64,144]{1,0:T(8,128)(2,1)}, u32[]{:S(2)}) copy-start(bf16[64,144]{1,0:T(8,128)(2,1)} %wc_ref.1) | copy-start | bytes 55300
  42.5 31.0 %copy-start.3 = (bf16[64,64]{1,0:T(8,128)(2,1)S(1)}, bf16[64,64]{1,0:T(8,128)(2,1)}, u32[]{:S(2)}) copy-start(bf16[64,64]{1,0:T(8,128)(2,1)} %wo_ref.1) | copy-start | bytes 24580
  42.5 31.0 %copy-start.4 = (bf16[64,64]{1,0:T(8,128)(2,1)S(1)}, bf16[64,64]{1,0:T(8,128)(2,1)}, u32[]{:S(2)}) copy-start(bf16[64,64]{1,0:T(8,128)(2,1)} %wout_ref.1) | copy-start | bytes 24580
  72.2 1.3 %collective-permute-start.11 = (bf16[256,128]{1,0:T(8,128)(2,1)S(1)}, bf16[256,128]{1,0:T(8,128)(2,1)S(1)}, u32[]{:S(2)}, u32[]{:S(2)}) collective-permute-start(bf16[256,128]{1,0:T(8,128)(2,1)S(1)} %get-tuple-element.42), channel_id=1, source_target_pairs={{0,1},{1,0},{2,3},{3,2},{4,5},{5,4},{6,7},{7,6},{8,9},{9,8},{10,11... | collective-permute-start | bytes 196616 | tf_op jit(solution)/shard_map/ppermute | solution.py:453

commit v7 on v6

--- a/solution.py
+++ b/solution.py
@@ -92,7 +92,7 @@
 
 
 def bias_kernel(whole, pieces, x_ref, w_ref, after_ref, me_ref, *refs):
-    outs, (acc_ref, centring_ref, wide_ref) = refs[:-3], refs[-3:]
+    outs, (acc_ref, centring_ref, averaging_ref, wide_ref) = refs[:-4], refs[-4:]
     step = pl.program_id(0)
     heads = w_ref.shape[0]
     per_step, keys, channels = x_ref.shape
@@ -106,6 +106,9 @@
         centring_ref[...] = block_matrix(
             2 * channels, channels, 1.0 - 1.0 / channels, -1.0 / channels
         )
+        averaging_ref[...] = block_matrix(
+            2 * channels, channels, 1.0 / channels, 1.0 / channels
+        )
         spread = one_hot(iota((heads, 1), 0) == iota((1, width), 1) // residues)
         wide_ref[...] = lax.dot_general(
             w_ref[...], spread, (((0,), (0,)), ((), ())), preferred_element_type=F32
@@ -119,16 +122,15 @@
         mine = lane == (residue % 2) * pairs + residue // 2
         placed.append(jnp.where(mine, wide_ref[...], 0.0).astype(BF16))
     placed = jnp.concatenate(placed, axis=0)
-    centring = centring_ref[...]
+    centring, averaging = centring_ref[...], averaging_ref[...]
     piece = min(512, keys)
     for r in range(0, keys, piece):
         normed = []
         for n in range(0, per_step, 2):
             x = jnp.concatenate([x_ref[n, r : r + piece], x_ref[n + 1, r : r + piece]], axis=1)
             centre = mm(x, centring)
-            for part in (centre[:, :channels], centre[:, channels:]):
-                spread = jnp.mean(part * part, axis=-1, keepdims=True)
-                normed.append((part * lax.rsqrt(spread + EPS)).astype(BF16))
+            spread = mm((centre * centre).astype(BF16), averaging)
+            normed.append((centre * lax.rsqrt(spread + EPS)).astype(BF16))
         added = mm(jnp.concatenate(normed, axis=1), placed)
         for n in range(tiles):
             acc_ref[n, r : r + piece, :] += added[:, n * 128 : (n + 1) * 128]
@@ -143,7 +145,7 @@
         for flip in range(2):
             user = me_ref[0] ^ flip
             starts = [
-                (user ^ (c + 2 * q + 2 * pieces * k)) * residues + p
+                ((user % (2 * pieces) ^ (c + 2 * q)) + 2 * pieces * k) * residues + p
                 for q in range(pieces)
                 for p in range(2)
                 for k in range(levels)
@@ -156,8 +158,6 @@
                         for start in starts[at // pairs : (at + 128) // pairs]
                     ]
                     turned = jnp.concatenate(rows, axis=0).T.astype(BF16)
-                    if flip == 0:
-                        turned = turned.astype(F32) * LOG2E
                     outs[flip][n * 128 : (n + 1) * 128, at : at + 128] = turned
 
 
@@ -170,13 +170,14 @@
     parity, rest = rest // (each // 2), rest % (each // 2)
     place, pair = rest // pairs, rest % pairs
     for flip, out_ref in enumerate((own_ref, send_ref)):
-        device = me_ref[0] ^ flip ^ ((place % 2) + 2 * which + 2 * pieces * (place // 2))
+        device = (me_ref[0] % (2 * pieces)) ^ flip ^ ((place % 2) + 2 * which)
+        device = device + 2 * pieces * (place // 2)
         target = device * residues + 2 * pair + parity
         total = jnp.zeros((rows, keys), F32)
         for start in range(0, keys, 256):
             chosen = one_hot(iota((256, keys), 0) + start == target)
             total = total + mm(bias_ref[:, start : start + 256], chosen)
-        out_ref[...] = total * LOG2E if flip == 0 else total.astype(BF16)
+        out_ref[...] = total.astype(BF16)
 
 
 def query_kernel(
@@ -184,7 +185,7 @@
 ):
     column_refs, (bias_ref, lhs_ref, sums_ref) = refs[:groups], refs[groups:]
     rows = own_ref.shape[0]
-    bias_ref[:rows, :] = own_ref[...]
+    bias_ref[:rows, :] = own_ref[...].astype(F32) * LOG2E
     bias_ref[rows:, :] = peer_ref[...].astype(F32) * LOG2E
 
     hidden = w_ref.shape[0]
@@ -285,7 +286,7 @@
     *refs,
 ):
     piece_refs, far_refs = refs[:groups], refs[groups : 4 * groups]
-    mine_ref, theirs_ref, high_ref, low_ref, range_ref, copy_ref = refs[4 * groups :]
+    mine_ref, theirs_ref, turned_ref, range_ref, copy_ref = refs[4 * groups :]
     hidden = w_ref.shape[0]
     depth = hidden // heads
     lead = size * pairs
@@ -316,11 +317,11 @@
 
     def settle(line, total):
         start = pl.multiple_of(line * pairs, pairs)
-        for ref, part in zip((high_ref, low_ref), halves(total)):
-            for n in range(2):
-                for b in range(blocks):
-                    at = (n * blocks + b) * pairs
-                    ref[n, pl.ds(start, pairs), b * 128 : (b + 1) * 128] = part[at : at + pairs]
+        total = total.astype(BF16)
+        for n in range(2):
+            for b in range(blocks):
+                part = total[(n * blocks + b) * pairs : (n * blocks + b + 1) * pairs]
+                turned_ref[n, pl.ds(start, pairs), b * 128 : (b + 1) * 128] = part
 
     range_ref[...] = jnp.ones(range_ref.shape, F32)
 
@@ -365,13 +366,13 @@
 
             lax.fori_loop(0, size, exact_line, 0)
 
+    mixed = mm(turned_ref[...].reshape(2 * groups * lead, blocks * 128), wv)
+    mixed = (mixed[:, :128] / mixed[:, 128:]).reshape(2, groups * lead, 128)
     for n, (ref, out_ref) in enumerate(((keep_ref, mine_ref), (received_ref, theirs_ref))):
-        mixed = mm(high_ref[n], wv) + mm(low_ref[n], wv)
-        mixed = mixed[:, :128] / mixed[:, 128:]
         for g in range(groups):
             gate = jax.nn.sigmoid(mm(ref[g, :lead], wg))
             at = slice(g * lead, (g + 1) * lead)
-            out_ref[at, :] = (gate * mixed[at]).astype(BF16)
+            out_ref[at, :] = (gate * mixed[n, at]).astype(BF16)
 
 
 def final_kernel(
@@ -526,15 +527,16 @@
     chunk = jnp.concatenate(
         [keep[:, :lead], received[:, :lead], keep[:, lead:] + received[:, lead:]], axis=1
     )
-    levels = [chunk] + [exchange(chunk, high * k, res_size) for k in range(1, res_size // high)]
-    own = [jnp.stack([level[g] for level in levels]) for g in range(groups)]
+    heights = [[d + high * k for k in range(res_size // high)] for d in range(high)]
+    levels = lax.all_gather(chunk, "res", axis_index_groups=heights)
+    own = [levels[:, g] for g in range(groups)]
     beside = [exchange(part, near, res_size) for part in own]
     across = [exchange(part, far, res_size) for part in own]
 
     per_step = 8
     pieces = 4
     whole = seq_size == 1
-    bias_rows = [shape(rows, keys, dtype=F32), shape(rows, keys)]
+    bias_rows = [shape(rows, keys)] * 2
     bias = call(
         functools.partial(bias_kernel, whole, pieces),
         bias_rows if whole else [shape(rows, pair.shape[1])],
@@ -552,6 +554,7 @@
         out_specs=[pl.BlockSpec((rows, pair.shape[1]), lambda n: (0, 0))] * (1 + whole),
         scratch_shapes=[
             pltpu.VMEM((rows // 128, pair.shape[1], 128), F32),
+            pltpu.VMEM((2 * pair.shape[2], 2 * pair.shape[2]), BF16),
             pltpu.VMEM((2 * pair.shape[2], 2 * pair.shape[2]), BF16),
             pltpu.VMEM((pair.shape[2], rows), F32),
         ],
@@ -623,7 +626,6 @@
         in_specs=[vmem] * (6 + groups) + [anywhere] * (3 * groups),
         scratch_shapes=[
             pltpu.VMEM((2, groups * lead, 128 * 2 * heads), BF16),
-            pltpu.VMEM((2, groups * lead, 128 * 2 * heads), BF16),
             pltpu.VMEM((2, 8, 128), F32),
             pltpu.VMEM((3 * groups,) + own[0].shape, BF16),
         ],

time: 76.4 us -> 87.8 us (1.15)
  blocking collectives: 0 us -> 18 us
  starting transfers between devices: 12.9 us -> 7.36 us
  waiting for transfers between devices: 4.32 us -> 2.91 us
  local copies, waits for them, and re-layouts: 3.12 us -> 2.02 us
  Pallas kernels: 54.8 us -> 55.7 us
    all_gather x0 -> x1, blocking collectives: none -> 18 us  [on_device(): levels = lax.all_gather(chunk, 'res', axis_index_groups=heights)]
    ppermute x12 -> x9, starting transfers between devices: 12.9 us -> 7.36 us  [exchange(): return lax.ppermute(x, 'res', [(d, d ^ flip) for d in range(devices)])]
    ppermute x12 -> x9, waiting for transfers between devices: 4.32 us -> 2.91 us  [exchange(): return lax.ppermute(x, 'res', [(d, d ^ flip) for d in range(devices)])]
    slice x4 -> x0, local copies, waits for them, and re-layouts: 0.96 us -> none  [on_device(): own = [jnp.stack([level[g] for level in levels]) for g in range(groups)]]
    pallas_call x7, Pallas kernels: 54.8 us -> 55.7 us  [call(): pl.pallas_call(kernel, out_shape=out_shape, compiler_params=limit, cost_e...]
  transfers between devices with their start and end apart: 12 -> 9, of which waited for: 5 -> 3; matrix products, arithmetic and copies ran while one was open for 1% -> 0% of each run, Pallas kernels for 29% -> 14%
where the time goes in v7:
time: 87.8 us; the launch traced here: 87.5 us
  Pallas kernels  55.7 us (63%)
  blocking collectives  18 us (21%)
  starting transfers between devices  7.36 us (8%)
  waiting for transfers between devices  2.91 us (3%)
  local copies, waits for them, and re-layouts  2.02 us (2%)
  other arithmetic  1.4 us (2%)
    pallas_call x7, Pallas kernels, call(): pl.pallas_call(kernel, out_shape=out_shape, compiler_params=limit, cost_e...  55.7 us
    all_gather x1, blocking collectives, on_device(): levels = lax.all_gather(chunk, 'res', axis_index_groups=heights)  18 us
    ppermute x9, starting transfers between devices, exchange(): return lax.ppermute(x, 'res', [(d, d ^ flip) for d in range(devices)])  7.36 us
    ppermute x9, waiting for transfers between devices, exchange(): return lax.ppermute(x, 'res', [(d, d ^ flip) for d in range(devices)])  2.91 us
    unnamed x14, local copies, waits for them, and re-layouts  1.97 us
  transfers between devices with their start and end apart: 9, of which 3 were waited for; matrix products, arithmetic and copies ran while one was open for 0% of the time, Pallas kernels for 14%

profile of v7, /device:TPU:0, one launch (start us, length us, event | category | flops | bytes accessed | tf_op | source)
XLA Modules:
  0.0 87.5 jit_solution(12521035607029318037)
XLA Ops:
  0.0 0.7 multiply_convert_fusion.kept_ref
  0.7 0.9 %copy-done = bf16[32,2048]{1,0:T(8,128)(2,1)S(1)} copy-done((bf16[32,2048]{1,0:T(8,128)(2,1)S(1)}, bf16[32,2048]{1,0:T(8,128)(2,1)}, u32[]{:S(2)}) %copy-start) | copy-done | bytes 131096
  1.6 1.2 %shard_map.91 = (bf16[2,144,128]{2,1,0:T(8,128)(2,1)S(1)}, bf16[2,144,128]{2,1,0:T(8,128)(2,1)S(1)}, bf16[512,128]{1,0:T(8,128)(2,1)S(1)}) custom-call(s32[1]{0:T(128)} %bitcast.me_ref, bf16[32,2048]{1,0:T(8,128)(2,1)S(1)} %copy-done, bf16[32,32]{1,0:T(8,128)(2,1)S(1)} %multiply_convert_fusion.kept_ref), custom_call_target="tpu_custom_call" | custom-call | bytes 133124 | tf_op jit(solution)/shard_map/pallas_call | solution.py:444
  2.9 0.5 collective-permute-start
  3.3 0.9 %collective-permute-done.received_ref = bf16[2,144,128]{2,1,0:T(8,128)(2,1)S(1)} collective-permute-done((bf16[2,144,128]{2,1,0:T(8,128)(2,1)S(1)}, bf16[2,144,128]{2,1,0:T(8,128)(2,1)S(1)}, u32[]{:S(2)}, u32[]{:S(2)}) %collective-permute-start) | collective-permute-done | bytes 73760 | tf_op jit(solution)/shard_map/ppermute | solution.py:454
  4.3 0.7 pad_maximum_fusion.after_ref
  4.9 11.0 %shard_map.92 = (bf16[256,1024]{1,0:T(8,128)(2,1)}, bf16[256,1024]{1,0:T(8,128)(2,1)}) custom-call(bf16[32,1024,128]{2,1,0:T(8,128)(2,1)} %x_ref.1, bf16[8,128]{1,0:T(8,128)(2,1)} %bitcast.12, bf16[2,272,128]{2,1,0:T(8,128)(2,1)} %pad_maximum_fusion.after_ref, s32[1]{0:T(128)} %bitcast.me_ref), custom_call_target="tpu_custom_call" | custom-call | flops 8589934592 | bytes 8529924 | tf_op jit(solution)/shard_map/pallas_call | solution.py:444
  16.0 0.4 collective-permute-start.1
  16.3 18.0 %all-gather = bf16[8,272,128]{2,1,0:T(8,128)(2,1)S(1)} all-gather(bf16[2,272,128]{2,1,0:T(8,128)(2,1)S(1)} %copy-done.6), channel_id=2, replica_groups={{0,8,16,24},{1,9,17,25},{2,10,18,26},{3,11,19,27},{4,12,20,28},{5,13,21..., dimensions={0}, use_global_device_ids=true | all-gather | bytes 696320 | tf_op jit(solution)/shard_map/all_gather | solution.py:531
  34.4 1.6 %collective-permute-start.3 = (bf16[4,272,128]{2,1,0:T(8,128)(2,1)S(1)}, bf16[4,272,128]{2,1,0:T(8,128)(2,1)S(1)}, u32[]{:S(2)}, u32[]{:S(2)}) collective-permute-start(bf16[4,272,128]{2,1,0:T(8,128)(2,1)S(1)} %get-tuple-element.43.refs_1_.refs_3_), channel_id=1, source_target_pairs={{0,4},{1,5},{2,6},{3,7},{4,0},{5,1},{6,2},{7,3},{8,12},{9,13},{10,... | collective-permute-start | bytes 835592 | tf_op jit(solution)/shard_map/ppermute | solution.py:454
  36.0 1.5 %collective-permute-start.2 = (bf16[4,272,128]{2,1,0:T(8,128)(2,1)S(1)}, bf16[4,272,128]{2,1,0:T(8,128)(2,1)S(1)}, u32[]{:S(2)}, u32[]{:S(2)}) collective-permute-start(bf16[4,272,128]{2,1,0:T(8,128)(2,1)S(1)} %get-tuple-element.44.refs_0_.refs_2_), channel_id=1, source_target_pairs={{0,2},{1,3},{2,0},{3,1},{4,6},{5,7},{6,4},{7,5},{8,10},{9,11},{10,... | collective-permute-start | bytes 835592 | tf_op jit(solution)/shard_map/ppermute | solution.py:454
  37.4 0.5 collective-permute-start.6
  38.0 0.5 collective-permute-start.7
  38.5 0.0 collective-permute-done.1.peer_ref
  38.5 1.0 %copy-done.5 = bf16[256,1024]{1,0:T(8,128)(2,1)S(1)} copy-done((bf16[256,1024]{1,0:T(8,128)(2,1)S(1)}, bf16[256,1024]{1,0:T(8,128)(2,1)}, u32[]{:S(2)}) %copy-start.5) | copy-done | bytes 524312
  39.5 5.2 %shard_map.93 = (f32[512,1024]{1,0:T(8,128)S(1)}, bf16[16,512,128]{2,1,0:T(8,128)(2,1)S(1)}, f32[16,512,128]{2,1,0:T(8,128)S(1)}) custom-call(bf16[256,1024]{1,0:T(8,128)(2,1)S(1)} %copy-done.5, bf16[256,1024]{1,0:T(8,128)(2,1)S(1)} %collective-permute-done.1.peer_ref, bf16[2,144,128]{2,1,0:T(8,128)(2,1)S(1)} %get-tuple-element.25.keep_ref, ...), custom_call_target="tpu_custom_call" | custom-call | flops 2147483648 | bytes 1785856 | tf_op jit(solution)/shard_map/pallas_call | solution.py:444
  44.8 0.0 collective-permute-done.3.refs_1_.refs_7_
  44.8 0.7 collective-permute-done.2.refs_0_.refs_4_
  45.5 0.8 collective-permute-start.4
  46.4 1.5 %collective-permute-start.5 = (bf16[4,272,128]{2,1,0:T(8,128)(2,1)S(1)}, bf16[4,272,128]{2,1,0:T(8,128)(2,1)S(1)}, u32[]{:S(2)}, u32[]{:S(2)}) collective-permute-start(bf16[4,272,128]{2,1,0:T(8,128)(2,1)S(1)} %collective-permute-done.3.refs_1_.refs_7_), channel_id=1, source_target_pairs={{0,2},{1,3},{2,0},{3,1},{4,6},{5,7},{6,4},{7,5},{8,10},{9,11},{10,... | collective-permute-start | bytes 835592 | tf_op jit(solution)/shard_map/ppermute | solution.py:454
  47.9 3.6 %shard_map.94.before_ref = f32[16,512,128]{2,1,0:T(8,128)S(1)} custom-call(bf16[16,512,128]{2,1,0:T(8,128)(2,1)S(1)} %get-tuple-element.29.lhs_ref, f32[512,1024]{1,0:T(8,128)S(1)} %get-tuple-element.30.bias_ref, f32[16,512,128]{2,1,0:T(8,128)S(1)} %get-tuple-element.34.before_ref, bf16[4,272,128]{2,1,0:T(8,128)(2,1)S(1)} %collective-permute-done.2.refs_0_.refs_4_, ...), custom_call_target="tpu_custom_call" | custom-call | flops 4294967296 | bytes 8945664 | tf_op jit(solution)/shard_map/pallas_call | solution.py:444
  51.5 0.0 collective-permute-done.7.refs_0_.refs_6_
  51.5 3.6 %shard_map.95.sums_ref = f32[16,512,128]{2,1,0:T(8,128)S(1)} custom-call(bf16[16,512,128]{2,1,0:T(8,128)(2,1)S(1)} %get-tuple-element.29.lhs_ref, f32[512,1024]{1,0:T(8,128)S(1)} %get-tuple-element.30.bias_ref, f32[16,512,128]{2,1,0:T(8,128)S(1)} %shard_map.94.before_ref, bf16[4,272,128]{2,1,0:T(8,128)(2,1)S(1)} %collective-permute-done.7.refs_0_.refs_6_, ...), custom_call_target="tpu_custom_call" | custom-call | flops 4294967296 | bytes 8945664 | tf_op jit(solution)/shard_map/pallas_call | solution.py:444
  55.1 0.0 copy-start.2
  55.2 0.0 copy-start.3
  55.2 0.0 copy-start.4
  55.2 0.0 collective-permute-done.4.refs_0_
  55.2 0.0 collective-permute-done.5.refs_1_
  55.2 28.4 %shard_map.96 = (bf16[256,128]{1,0:T(8,128)(2,1)S(1)}, bf16[256,128]{1,0:T(8,128)(2,1)S(1)}) custom-call(bf16[16,512,128]{2,1,0:T(8,128)(2,1)S(1)} %get-tuple-element.29.lhs_ref, f32[512,1024]{1,0:T(8,128)S(1)} %get-tuple-element.30.bias_ref, f32[16,512,128]{2,1,0:T(8,128)S(1)} %shard_map.95.sums_ref, bf16[64,256]{1,0:T(8,128)(2,1)S(1)} %copy-done.1, ...), custom_call_target="tpu_custom_call" | custom-call | flops 2147483648 | bytes 10797056 | tf_op jit(solution)/shard_map/pallas_call | solution.py:444
  83.6 0.1 collective-permute-start.8
  83.7 1.2 %collective-permute-done.8.theirs_ref = bf16[256,128]{1,0:T(8,128)(2,1)S(1)} collective-permute-done((bf16[256,128]{1,0:T(8,128)(2,1)S(1)}, bf16[256,128]{1,0:T(8,128)(2,1)S(1)}, u32[]{:S(2)}, u32[]{:S(2)}) %collective-permute-start.8) | collective-permute-done | bytes 65568 | tf_op jit(solution)/shard_map/ppermute | solution.py:454
  85.0 2.6 %shard_map.97 = bf16[32,2048]{1,0:T(8,128)(2,1)} custom-call(s32[1]{0:T(128)} %bitcast.me_ref, bf16[512,128]{1,0:T(8,128)(2,1)S(1)} %get-tuple-element.24.line_ref, bf16[32,32]{1,0:T(8,128)(2,1)S(1)} %multiply_convert_fusion.kept_ref, bf16[64,64]{1,0:T(8,128)(2,1)S(1)} %copy-done.3, bf16[64,144]{1,0:T(8,128)(2,1)S(1)} %copy-done.2, ...), custom_call_target="tpu_custom_call" | custom-call | bytes 299012 | tf_op jit(solution)/shard_map/pallas_call | solution.py:444
  (14 shorter events, 0.1 us)
Async XLA Ops:
  0.7 0.9 %copy-start = (bf16[32,2048]{1,0:T(8,128)(2,1)S(1)}, bf16[32,2048]{1,0:T(8,128)(2,1)}, u32[]{:S(2)}) copy-start(bf16[32,2048]{1,0:T(8,128)(2,1)} %m_ref.1) | copy-start | bytes 393220
  2.9 1.4 %collective-permute-start = (bf16[2,144,128]{2,1,0:T(8,128)(2,1)S(1)}, bf16[2,144,128]{2,1,0:T(8,128)(2,1)S(1)}, u32[]{:S(2)}, u32[]{:S(2)}) collective-permute-start(bf16[2,144,128]{2,1,0:T(8,128)(2,1)S(1)} %get-tuple-element.26), channel_id=1, source_target_pairs={{0,1},{1,0},{2,3},{3,2},{4,5},{5,4},{6,7},{7,6},{8,9},{9,8},{10,11... | collective-permute-start | bytes 221192 | tf_op jit(solution)/shard_map/ppermute | solution.py:454
  4.9 11.4 %copy-start.6 = (bf16[2,272,128]{2,1,0:T(8,128)(2,1)S(1)}, bf16[2,272,128]{2,1,0:T(8,128)(2,1)}, u32[]{:S(2)}) copy-start(bf16[2,272,128]{2,1,0:T(8,128)(2,1)} %pad_maximum_fusion.after_ref) | copy-start | bytes 417796
  4.9 33.6 %copy-start.1 = (bf16[64,256]{1,0:T(8,128)(2,1)S(1)}, bf16[64,256]{1,0:T(8,128)(2,1)}, u32[]{:S(2)}) copy-start(bf16[64,256]{1,0:T(8,128)(2,1)} %w_ref.3) | copy-start | bytes 98308
  16.0 22.5 %collective-permute-start.1 = (bf16[256,1024]{1,0:T(8,128)(2,1)}, bf16[256,1024]{1,0:T(8,128)(2,1)S(1)}, u32[]{:S(2)}, u32[]{:S(2)}) collective-permute-start(bf16[256,1024]{1,0:T(8,128)(2,1)} %get-tuple-element.28), channel_id=1, source_target_pairs={{0,1},{1,0},{2,3},{3,2},{4,5},{5,4},{6,7},{7,6},{8,9},{9,8},{10,11... | collective-permute-start | bytes 1572872 | tf_op jit(solution)/shard_map/ppermute | solution.py:454
  34.4 10.4 %collective-permute-start.3 = (bf16[4,272,128]{2,1,0:T(8,128)(2,1)S(1)}, bf16[4,272,128]{2,1,0:T(8,128)(2,1)S(1)}, u32[]{:S(2)}, u32[]{:S(2)}) collective-permute-start(bf16[4,272,128]{2,1,0:T(8,128)(2,1)S(1)} %get-tuple-element.43.refs_1_.refs_3_), channel_id=1, source_target_pairs={{0,4},{1,5},{2,6},{3,7},{4,0},{5,1},{6,2},{7,3},{8,12},{9,13},{10,... | collective-permute-start | bytes 835592 | tf_op jit(solution)/shard_map/ppermute | solution.py:454
  36.0 9.6 %collective-permute-start.2 = (bf16[4,272,128]{2,1,0:T(8,128)(2,1)S(1)}, bf16[4,272,128]{2,1,0:T(8,128)(2,1)S(1)}, u32[]{:S(2)}, u32[]{:S(2)}) collective-permute-start(bf16[4,272,128]{2,1,0:T(8,128)(2,1)S(1)} %get-tuple-element.44.refs_0_.refs_2_), channel_id=1, source_target_pairs={{0,2},{1,3},{2,0},{3,1},{4,6},{5,7},{6,4},{7,5},{8,10},{9,11},{10,... | collective-permute-start | bytes 835592 | tf_op jit(solution)/shard_map/ppermute | solution.py:454
  37.4 14.1 %collective-permute-start.6 = (bf16[4,272,128]{2,1,0:T(8,128)(2,1)S(1)}, bf16[4,272,128]{2,1,0:T(8,128)(2,1)S(1)}, u32[]{:S(2)}, u32[]{:S(2)}) collective-permute-start(bf16[4,272,128]{2,1,0:T(8,128)(2,1)S(1)} %get-tuple-element.43.refs_1_.refs_3_), channel_id=1, source_target_pairs={{0,2},{1,3},{2,0},{3,1},{4,6},{5,7},{6,4},{7,5},{8,10},{9,11},{10,... | collective-permute-start | bytes 835592 | tf_op jit(solution)/shard_map/ppermute | solution.py:454
  38.0 13.5 %collective-permute-start.7 = (bf16[4,272,128]{2,1,0:T(8,128)(2,1)S(1)}, bf16[4,272,128]{2,1,0:T(8,128)(2,1)S(1)}, u32[]{:S(2)}, u32[]{:S(2)}) collective-permute-start(bf16[4,272,128]{2,1,0:T(8,128)(2,1)S(1)} %get-tuple-element.44.refs_0_.refs_2_), channel_id=1, source_target_pairs={{0,4},{1,5},{2,6},{3,7},{4,0},{5,1},{6,2},{7,3},{8,12},{9,13},{10,... | collective-permute-start | bytes 835592 | tf_op jit(solution)/shard_map/ppermute | solution.py:454
  38.5 1.0 %copy-start.5 = (bf16[256,1024]{1,0:T(8,128)(2,1)S(1)}, bf16[256,1024]{1,0:T(8,128)(2,1)}, u32[]{:S(2)}) copy-start(bf16[256,1024]{1,0:T(8,128)(2,1)} %get-tuple-element.27.own_ref) | copy-start | bytes 1572868
  45.5 9.6 %collective-permute-start.4 = (bf16[4,272,128]{2,1,0:T(8,128)(2,1)S(1)}, bf16[4,272,128]{2,1,0:T(8,128)(2,1)S(1)}, u32[]{:S(2)}, u32[]{:S(2)}) collective-permute-start(bf16[4,272,128]{2,1,0:T(8,128)(2,1)S(1)} %collective-permute-done.2.refs_0_.refs_4_), channel_id=1, source_target_pairs={{0,4},{1,5},{2,6},{3,7},{4,0},{5,1},{6,2},{7,3},{8,12},{9,13},{10,... | collective-permute-start | bytes 835592 | tf_op jit(solution)/shard_map/ppermute | solution.py:454
  46.4 8.8 %collective-permute-start.5 = (bf16[4,272,128]{2,1,0:T(8,128)(2,1)S(1)}, bf16[4,272,128]{2,1,0:T(8,128)(2,1)S(1)}, u32[]{:S(2)}, u32[]{:S(2)}) collective-permute-start(bf16[4,272,128]{2,1,0:T(8,128)(2,1)S(1)} %collective-permute-done.3.refs_1_.refs_7_), channel_id=1, source_target_pairs={{0,2},{1,3},{2,0},{3,1},{4,6},{5,7},{6,4},{7,5},{8,10},{9,11},{10,... | collective-permute-start | bytes 835592 | tf_op jit(solution)/shard_map/ppermute | solution.py:454
  55.1 29.8 %copy-start.2 = (bf16[64,144]{1,0:T(8,128)(2,1)S(1)}, bf16[64,144]{1,0:T(8,128)(2,1)}, u32[]{:S(2)}) copy-start(bf16[64,144]{1,0:T(8,128)(2,1)} %wc_ref.1) | copy-start | bytes 55300
  55.2 29.8 %copy-start.3 = (bf16[64,64]{1,0:T(8,128)(2,1)S(1)}, bf16[64,64]{1,0:T(8,128)(2,1)}, u32[]{:S(2)}) copy-start(bf16[64,64]{1,0:T(8,128)(2,1)} %wo_ref.1) | copy-start | bytes 24580
  55.2 29.8 %copy-start.4 = (bf16[64,64]{1,0:T(8,128)(2,1)S(1)}, bf16[64,64]{1,0:T(8,128)(2,1)}, u32[]{:S(2)}) copy-start(bf16[64,64]{1,0:T(8,128)(2,1)} %wout_ref.1) | copy-start | bytes 24580
  83.6 1.3 %collective-permute-start.8 = (bf16[256,128]{1,0:T(8,128)(2,1)S(1)}, bf16[256,128]{1,0:T(8,128)(2,1)S(1)}, u32[]{:S(2)}, u32[]{:S(2)}) collective-permute-start(bf16[256,128]{1,0:T(8,128)(2,1)S(1)} %get-tuple-element.42), channel_id=1, source_target_pairs={{0,1},{1,0},{2,3},{3,2},{4,5},{5,4},{6,7},{7,6},{8,9},{9,8},{10,11... | collective-permute-start | bytes 196616 | tf_op jit(solution)/shard_map/ppermute | solution.py:454
